TPU v7x, 32 devices: a whole 2x2x4 slice. The times are simulated.
32 devices in a mesh: tile: 8 (over z, y), seg: 4 (over x, core).
Axes of the slice: x: 2, y: 2, z: 4, core: 2. Of those that a mesh axis runs over, the one named last changes fastest.
Arguments:
- patches: bfloat16 [8, 257, 1536], P('tile'), may hold values from -6 to 6
- vit_norm_gain: float32 [1536], replicated, may hold values from 0.5 to 1.5
- vit_query: bfloat16 [1536, 1536], P('tile', 'seg'), may hold values from -1 to 1
- vit_key: bfloat16 [1536, 1536], P('tile', 'seg'), may hold values from -1 to 1
- vit_value: bfloat16 [1536, 1536], P('tile', 'seg'), may hold values from -0.15625 to 0.15625
- vit_out: bfloat16 [1536, 1536], P('seg'), may hold values from -0.15625 to 0.15625
- layer_scale: float32 [1536], replicated, may hold values from 0.25 to 2.5
- final_gain: float32 [1536], replicated, may hold values from 0.5 to 1.5
- embed_proj: bfloat16 [1536, 768], P(None, 'seg'), may hold values from -0.15625 to 0.15625
- embed_bias: float32 [768], P('seg'), may hold values from -3 to 3
- slide_pos: int32 [8], replicated, may hold values from 0 to 2047, as said below
- cached: bfloat16 [2048, 768], P('tile'), may hold values from -6 to 6
- kept: int32 [2048], P('tile'), may hold values 0 or 1
- mask_token: float32 [768], replicated, may hold values from -4 to 4
- slide_gain: float32 [768], replicated, may hold values from 0.5 to 1.5
- slide_query: bfloat16 [768, 768], P(None, 'seg'), may hold values from -1 to 1
- slide_key: bfloat16 [768, 768], P(None, 'seg'), may hold values from -1 to 1
- slide_value: bfloat16 [768, 768], P(None, 'seg'), may hold values from -0.21875 to 0.21875
- slide_out: bfloat16 [768, 768], P('seg'), may hold values from -0.21875 to 0.21875
- offsets: int32 [5, 12], replicated, may hold values from 0 to 15, as said below
Outputs:
- slide_next: bfloat16 [2048, 768], P(('tile', 'seg'))
Inputs may be any that keep to these rules, and one draw needn't show every extreme that they name: `slide_pos`: distinct positions of the slide sequence. `offsets`: entry [b, h] is below 2 ** b.
All inputs are finite; a program needn't handle non-finite values. No bound on the sum of `kept` on one device may be relied on, other than what follows from the above.
Results may differ from a plain program's by a relative error of at most 0.0095.
Values may be sent and summed in bfloat16 or wider, within the bound.
No kernel may reach another device: no remote copies, remote signals or barrier semaphores. Data moves between devices by JAX's collectives and lax.ppermute only.
A program may use at most 64 MiB of HBM per device.

v0:
```python
import math

import jax
import jax.numpy as jnp
from jax import lax
from jax.sharding import PartitionSpec as P

DV = 1536
HV = 24
DS = 768
HS = 12


epsilon = 1e-06


def partner(block, axis, bit):
    count = lax.axis_size(axis)
    route = []
    for low in range(count):
        high = low | 1 << bit
        if high != low and high < count:
            route += [(low, high), (high, low)]
    return lax.ppermute(block, axis, route)


def layer_norm(values, scaling):
    center = values - jnp.mean(values, axis=-1, keepdims=True)
    spread = jnp.mean(center * center, axis=-1, keepdims=True)
    return center * lax.rsqrt(spread + epsilon) * scaling


def pick_rows(values, stride, residue):
    amount = values.shape[0] // stride
    shaped = values.reshape((amount, stride) + values.shape[1:])
    return lax.dynamic_index_in_dim(shaped, residue, 1, keepdims=False)


def spread_rows(values, stride, residue, filler):
    amount = values.shape[0]
    shaped = jnp.full((amount, stride) + values.shape[1:], filler, jnp.float32)
    placed = lax.dynamic_update_slice_in_dim(shaped, values[:, None], residue, 1)
    return placed.reshape((amount * stride,) + values.shape[1:])


def collect_segment(blocks, levels):
    for bit_level in range(levels):
        blocks = jnp.concatenate((blocks, partner(blocks, "tile", bit_level)), axis=1)
    return blocks


def shards(
    patches,
    vit_norm_gain,
    vit_query,
    vit_key,
    vit_value,
    vit_out,
    layer_scale,
    final_gain,
    embed_proj,
    embed_bias,
    slide_pos,
    cached,
    kept,
    mask_token,
    slide_gain,
    slide_query,
    slide_key,
    slide_value,
    slide_out,
    offsets,
):
    tiles_here, tokens, vit_width = patches.shape
    head_size = DV // HV
    local_cols = vit_query.shape[1]
    local_heads = local_cols // head_size
    scale_vit = 1.0 / math.sqrt(head_size)
    flat_tokens = patches.reshape(tiles_here * tokens, vit_width)
    normed = layer_norm(flat_tokens.astype(jnp.float32), vit_norm_gain).astype(jnp.bfloat16)
    class_normed = normed.reshape(tiles_here, tokens, vit_width)[:, 0]
    pieces = (
        lax.all_gather(vit_query, "tile", axis=0, tiled=True),
        lax.all_gather(vit_key, "tile", axis=0, tiled=True),
        lax.all_gather(vit_value, "tile", axis=0, tiled=True),
    )
    queries = (
        jnp.dot(class_normed, pieces[0], preferred_element_type=jnp.float32)
        .astype(jnp.bfloat16)
        .reshape(tiles_here, local_heads, head_size)
    )
    keys_vit = (
        jnp.dot(normed, pieces[1], preferred_element_type=jnp.float32)
        .astype(jnp.bfloat16)
        .reshape(tiles_here, tokens, local_heads, head_size)
    )
    values_vit = (
        jnp.dot(normed, pieces[2], preferred_element_type=jnp.float32)
        .astype(jnp.bfloat16)
        .reshape(tiles_here, tokens, local_heads, head_size)
    )
    scores = (
        jnp.einsum("nhd,nkhd->nhk", queries, keys_vit, preferred_element_type=jnp.float32)
        * scale_vit
    )
    highest = jnp.max(scores, axis=-1, keepdims=True)
    exponent = jnp.exp(scores - highest)
    weights_vit = (exponent / jnp.sum(exponent, axis=-1, keepdims=True)).astype(jnp.bfloat16)
    mixture = (
        jnp.einsum("nhk,nkhd->nhd", weights_vit, values_vit, preferred_element_type=jnp.float32)
        .astype(jnp.bfloat16)
        .reshape(tiles_here, local_cols)
    )
    partial_attn = jnp.dot(mixture, vit_out, preferred_element_type=jnp.float32)
    attended = lax.psum(partial_attn, "seg")
    pooled = patches[:, 0].astype(jnp.float32) + layer_scale * attended
    summary = layer_norm(pooled, final_gain).astype(jnp.bfloat16)
    embedded = (
        jnp.dot(summary, embed_proj, preferred_element_type=jnp.float32) + embed_bias
    ).astype(jnp.bfloat16)
    seq_rows = cached.shape[0]
    seg_count = lax.axis_size("seg")
    first_seq = lax.axis_index("tile") * seq_rows
    row_ids = jnp.arange(seq_rows, dtype=jnp.int32)
    pieces = lax.all_gather(embedded, ("tile", "seg"), axis=0, tiled=True)
    number = pieces.shape[0]
    global_row = jnp.arange(number, dtype=jnp.int32)
    owner_dev = global_row // tiles_here
    column_block = owner_dev % seg_count
    source = owner_dev // seg_count * tiles_here + global_row % tiles_here
    target = jnp.take(slide_pos, source) - first_seq
    matches = target[None, :] == row_ids[:, None]
    updated = []
    for block_index in range(seg_count):
        chosen = (matches & (column_block[None, :] == block_index)).astype(jnp.bfloat16)
        updated.append(jnp.dot(chosen, pieces, preferred_element_type=jnp.float32))
    first_hits = (matches & (column_block[None, :] == 0)).astype(jnp.float32)
    updated.append(jnp.sum(first_hits, axis=1))
    gathered = tuple(updated)
    placed = jnp.concatenate(gathered[:seg_count], axis=1).astype(jnp.bfloat16)
    arrived = gathered[seg_count] > 0.5
    mask_row = mask_token.astype(jnp.bfloat16)
    slide_rows = jnp.where(
        kept[:, None] == 0, mask_row[None, :], jnp.where(arrived[:, None], placed, cached)
    )
    slide_normed = layer_norm(slide_rows.astype(jnp.float32), slide_gain).astype(jnp.bfloat16)
    head_dim = DS // HS
    heads_here = slide_query.shape[1] // head_dim
    scale_slide = 1.0 / math.sqrt(head_dim)

    def heads_first(matrix):
        result = jnp.dot(slide_normed, matrix, preferred_element_type=jnp.float32).astype(
            jnp.bfloat16
        )
        return result.reshape(seq_rows, heads_here, head_dim).transpose(1, 0, 2)

    query_heads = heads_first(slide_query)
    keyval_heads = jnp.concatenate((heads_first(slide_key), heads_first(slide_value)), axis=2)
    head_offsets = lax.dynamic_slice_in_dim(
        offsets, lax.axis_index("seg") * heads_here, heads_here, 1
    )
    branches = offsets.shape[0]
    tile_bits = lax.axis_size("tile").bit_length() - 1
    level_counts = [min(2 * branch + 1, tile_bits) for branch in range(branches)]
    picker = jax.vmap(pick_rows, in_axes=(0, None, 0))
    picked_queries = []
    picked_keyvals = []
    for branch in range(branches):
        stride = 2**branch
        picked_queries.append(picker(query_heads, stride, head_offsets[branch]))
        picked_keyvals.append(picker(keyval_heads, stride, head_offsets[branch]))
    segments = [
        collect_segment(picked_keyvals[branch], level_counts[branch]) for branch in range(branches)
    ]
    widen = jax.vmap(spread_rows, in_axes=(0, None, 0, None))
    for branch in range(branches):
        stride = 2**branch
        keys_seg = segments[branch][:, :, :head_dim]
        values_seg = segments[branch][:, :, head_dim:]
        scores_seg = (
            jnp.einsum(
                "hqd,hkd->hqk", picked_queries[branch], keys_seg, preferred_element_type=jnp.float32
            )
            * scale_slide
        )
        highest_seg = jnp.max(scores_seg, axis=-1)
        exponent_seg = jnp.exp(scores_seg - highest_seg[..., None])
        denom_seg = jnp.sum(exponent_seg, axis=-1)
        numer_seg = jnp.einsum(
            "hqk,hkd->hqd",
            exponent_seg.astype(jnp.bfloat16),
            values_seg,
            preferred_element_type=jnp.float32,
        )
        if branch == 0:
            run_max, run_den, run_num = (highest_seg, denom_seg, numer_seg)
        else:
            full_max = widen(highest_seg, stride, head_offsets[branch], -1e30)
            full_den = widen(denom_seg, stride, head_offsets[branch], 0.0)
            full_num = widen(numer_seg, stride, head_offsets[branch], 0.0)
            new_max = jnp.maximum(run_max, full_max)
            keep_old = jnp.exp(run_max - new_max)
            take_new = jnp.exp(full_max - new_max)
            run_den = run_den * keep_old + full_den * take_new
            run_num = run_num * keep_old[..., None] + full_num * take_new[..., None]
            run_max = new_max
    attended_slide = (
        (run_num / run_den[..., None])
        .transpose(1, 0, 2)
        .reshape(seq_rows, heads_here * head_dim)
        .astype(jnp.bfloat16)
    )
    out_rows = seq_rows // seg_count
    summed = lax.psum_scatter(
        jnp.dot(attended_slide, slide_out, preferred_element_type=jnp.float32).astype(jnp.bfloat16),
        "seg",
        scatter_dimension=0,
        tiled=True,
    ).astype(jnp.float32)
    own_rows = lax.dynamic_slice_in_dim(slide_rows, lax.axis_index("seg") * out_rows, out_rows, 0)
    return (own_rows.astype(jnp.float32) + summed).astype(jnp.bfloat16)


def solution(mesh):
    return jax.shard_map(
        shards,
        mesh=mesh,
        in_specs=(
            P("tile", None, None),
            P(),
            P("tile", "seg"),
            P("tile", "seg"),
            P("tile", "seg"),
            P("seg", None),
            P(),
            P(),
            P(None, "seg"),
            P("seg"),
            P(),
            P("tile", None),
            P("tile"),
            P(),
            P(),
            P(None, "seg"),
            P(None, "seg"),
            P(None, "seg"),
            P("seg", None),
            P(),
        ),
        out_specs=P(("tile", "seg"), None),
        check_vma=False,
    )
```

profile of v0, /device:TPU:0, one launch (start us, length us, event | category | flops | bytes accessed | tf_op | source)
XLA Modules:
  0.0 535.2 jit_solution(1919300095591627910)
XLA Ops:
  17.5 35.9 %all-gather.7.cloned.1.call-done = bf16[1536,384]{1,0:T(8,128)(2,1)} async-done(((bf16[192,384]{1,0:T(8,128)(2,1)}), bf16[1536,384]{1,0:T(8,128)(2,1)}) %all-gather.7.cloned.1.call-update) | async-done | bytes 1179664 | tf_op jit(solution)/shard_map/all_gather | solution.py:84
  55.5 39.9 %all-gather.9.cloned.1.call-done = bf16[1536,384]{1,0:T(8,128)(2,1)} async-done(((bf16[192,384]{1,0:T(8,128)(2,1)}), bf16[1536,384]{1,0:T(8,128)(2,1)}) %all-gather.9.cloned.1.call-update) | async-done | bytes 1179664 | tf_op jit(solution)/shard_map/all_gather | solution.py:85
  97.6 39.9 %all-gather.5.cloned.1.call-done = bf16[1536,384]{1,0:T(8,128)(2,1)} async-done(((bf16[192,384]{1,0:T(8,128)(2,1)}), bf16[1536,384]{1,0:T(8,128)(2,1)}) %all-gather.5.cloned.1.call-update) | async-done | bytes 1179664 | tf_op jit(solution)/shard_map/all_gather | solution.py:83
  137.4 2.9 convolution_reduce_fusion
  141.6 5.9 %psum.7 = f32[1,1536]{1,0:T(1,128)S(1)} all-reduce(f32[1,1536]{1,0:T(1,128)S(1)} %fusion.132), channel_id=1, replica_groups=mesh['tile'=8,'seg'=4] {'seg'}, use_global_device_ids=true, to_apply=%region_5.0 | all-reduce | flops 1536 | bytes 12288 | tf_op jit(solution)/shard_map/psum | solution.py:115
  151.7 39.3 %all-reduce.4 = bf16[6144]{0:T(1024)(128)(2,1)S(1)} all-reduce(bf16[6144]{0:T(1024)(128)(2,1)S(1)} %dynamic-update-slice.24), channel_id=2, replica_groups=mesh['tile'=8,'seg'=4] {'tile','seg'}, use_global_device_ids=true, to_apply=%add.4 | all-reduce | flops 6144 | bytes 24576
  223.1 19.4 %while.18 = (s32[]{:T(128)}, f32[3,16,16]{2,1,0:T(8,128)S(1)}, s32[3,3]{1,0:T(4,128)S(1)}, f32[3,16,1]{1,0,2:T(4,128)S(1)}, s32[]{:T(128)}, /*index=5*/s32[3]{0:T(128)S(1)}, s32[]{:T(128)}) while((s32[]{:T(128)}, f32[3,16,16]{2,1,0:T(8,128)S(1)}, s32[3,3]{1,0:T(4,128)S(1)}, f32[3,16,1]{1,0,2:T(4,128)S(1)}, s32[]{:T(128)}, ...), condition=%wide.while_cond.6, body=%wide.while_body.6.sunk | while | flops 35 | bytes 755 | solution.py:42
  242.5 19.4 %while.23 = (s32[]{:T(128)}, f32[3,16,16]{2,1,0:T(8,128)S(1)}, s32[3,3]{1,0:T(4,128)S(1)}, f32[3,16,1]{1,0,2:T(4,128)S(1)}, s32[]{:T(128)}, /*index=5*/s32[3]{0:T(128)S(1)}, s32[]{:T(128)}) while((s32[]{:T(128)}, f32[3,16,16]{2,1,0:T(8,128)S(1)}, s32[3,3]{1,0:T(4,128)S(1)}, f32[3,16,1]{1,0,2:T(4,128)S(1)}, s32[]{:T(128)}, ...), condition=%wide.while_cond.11, body=%wide.while_body.11.sunk | while | flops 35 | bytes 755 | solution.py:42
  262.0 20.7 %while.19 = (s32[]{:T(128)}, f32[3,16,16,64]{3,2,1,0:T(8,128)S(1)}, s32[3,4]{1,0:T(4,128)S(1)}, f32[3,16,1,64]{3,2,1,0:T(1,128)S(1)}, s32[]{:T(128)}, /*index=5*/s32[4]{0:T(128)S(1)}, s32[]{:T(128)}) while((s32[]{:T(128)}, f32[3,16,16,64]{3,2,1,0:T(8,128)S(1)}, s32[3,4]{1,0:T(4,128)S(1)}, f32[3,16,1,64]{3,2,1,0:T(1,128)S(1)}, s32[]{:T(128)}, ...), condition=%wide.while_cond.7, body=%wide.while_body.7.sunk | while | flops 1053 | bytes 20683 | solution.py:42
  262.7 3.2 and_reduce_fusion.31
  269.6 3.2 and_reduce_fusion.31
  276.6 3.2 and_reduce_fusion.31
  288.9 19.3 %while.16 = (s32[]{:T(128)}, f32[3,32,8]{1,2,0:T(8,128)S(1)}, s32[3,3]{1,0:T(4,128)S(1)}, f32[3,32,1]{1,0,2:T(4,128)S(1)}, s32[]{:T(128)}, /*index=5*/s32[3]{0:T(128)S(1)}, s32[]{:T(128)}) while((s32[]{:T(128)}, f32[3,32,8]{1,2,0:T(8,128)S(1)}, s32[3,3]{1,0:T(4,128)S(1)}, f32[3,32,1]{1,0,2:T(4,128)S(1)}, s32[]{:T(128)}, /*index=5*/s32[3]{0:T(128)S(1)}, ...), condition=%wide.while_cond.4, body=%wide.while_body.4.sunk | while | flops 51 | bytes 819 | solution.py:42
  289.6 2.6 and_reduce_fusion.28
  296.1 2.6 and_reduce_fusion.28
  302.5 2.6 and_reduce_fusion.28
  308.3 21.3 %while.17 = (s32[]{:T(128)}, f32[3,32,8,64]{3,2,1,0:T(8,128)S(1)}, s32[3,4]{1,0:T(4,128)S(1)}, f32[3,32,1,64]{3,2,1,0:T(1,128)S(1)}, s32[]{:T(128)}, /*index=5*/s32[4]{0:T(128)S(1)}, s32[]{:T(128)}) while((s32[]{:T(128)}, f32[3,32,8,64]{3,2,1,0:T(8,128)S(1)}, s32[3,4]{1,0:T(4,128)S(1)}, f32[3,32,1,64]{3,2,1,0:T(1,128)S(1)}, s32[]{:T(128)}, ...), condition=%wide.while_cond.5, body=%wide.while_body.5.sunk | while | flops 2077 | bytes 41163 | solution.py:42
  309.0 3.2 and_reduce_fusion.29
  316.1 3.2 and_reduce_fusion.29
  323.2 3.2 and_reduce_fusion.29
  329.7 19.3 %while.22 = (s32[]{:T(128)}, f32[3,32,8]{1,2,0:T(8,128)S(1)}, s32[3,3]{1,0:T(4,128)S(1)}, f32[3,32,1]{1,0,2:T(4,128)S(1)}, s32[]{:T(128)}, /*index=5*/s32[3]{0:T(128)S(1)}, s32[]{:T(128)}) while((s32[]{:T(128)}, f32[3,32,8]{1,2,0:T(8,128)S(1)}, s32[3,3]{1,0:T(4,128)S(1)}, f32[3,32,1]{1,0,2:T(4,128)S(1)}, s32[]{:T(128)}, ...), condition=%wide.while_cond.10, body=%wide.while_body.10.sunk | while | flops 51 | bytes 819 | solution.py:42
  330.4 2.6 and_reduce_fusion.34
  336.8 2.6 and_reduce_fusion.34
  343.2 2.6 and_reduce_fusion.34
  358.4 19.2 %while.14 = (s32[]{:T(128)}, f32[3,64,4]{1,2,0:T(4,128)S(1)}, s32[3,3]{1,0:T(4,128)S(1)}, f32[3,64,1]{1,0,2:T(4,128)S(1)}, s32[]{:T(128)}, /*index=5*/s32[3]{0:T(128)S(1)}, s32[]{:T(128)}) while((s32[]{:T(128)}, f32[3,64,4]{1,2,0:T(4,128)S(1)}, s32[3,3]{1,0:T(4,128)S(1)}, f32[3,64,1]{1,0,2:T(4,128)S(1)}, s32[]{:T(128)}, /*index=5*/s32[3]{0:T(128)S(1)}, ...), condition=%wide.while_cond.2, body=%wide.while_body.2.sunk | while | flops 83 | bytes 1459 | solution.py:42
  377.6 25.9 %while.15 = (s32[]{:T(128)}, f32[3,64,4,64]{3,2,1,0:T(4,128)S(1)}, s32[3,4]{1,0:T(4,128)}, f32[3,64,1,64]{3,2,1,0:T(1,128)S(1)}, s32[]{:T(128)}, /*index=5*/s32[4]{0:T(128)}, s32[]{:T(128)}) while((s32[]{:T(128)}, f32[3,64,4,64]{3,2,1,0:T(4,128)S(1)}, s32[3,4]{1,0:T(4,128)}, f32[3,64,1,64]{3,2,1,0:T(1,128)S(1)}, s32[]{:T(128)}, ...), condition=%wide.while_cond.3, body=%wide.while_body.3.sunk | while | flops 4125 | bytes 82123 | solution.py:42
  378.9 3.9 and_reduce_fusion.27
  387.6 3.9 and_reduce_fusion.27
  396.2 3.9 and_reduce_fusion.27
  403.6 21.5 %while.21 = (s32[]{:T(128)}, f32[3,64,4]{1,2,0:T(4,128)S(1)}, s32[3,3]{1,0:T(4,128)}, f32[3,64,1]{1,0,2:T(4,128)S(1)}, s32[]{:T(128)}, /*index=5*/s32[3]{0:T(128)S(1)}, s32[]{:T(128)}) while((s32[]{:T(128)}, f32[3,64,4]{1,2,0:T(4,128)S(1)}, s32[3,3]{1,0:T(4,128)}, f32[3,64,1]{1,0,2:T(4,128)S(1)}, s32[]{:T(128)}, /*index=5*/s32[3]{0:T(128)S(1)}, ...), condition=%wide.while_cond.9, body=%wide.while_body.9.sunk | while | flops 83 | bytes 1459 | solution.py:42
  404.9 2.6 and_reduce_fusion.33
  419.2 2.6 and_reduce_fusion.33
  429.6 19.6 %while.12 = (s32[]{:T(128)}, f32[3,128,2]{1,2,0:T(2,128)S(1)}, s32[3,3]{1,0:T(4,128)S(1)}, f32[3,128,1]{1,0,2:T(4,128)S(1)}, s32[]{:T(128)}, /*index=5*/s32[3]{0:T(128)S(1)}, s32[]{:T(128)}) while((s32[]{:T(128)}, f32[3,128,2]{1,2,0:T(2,128)S(1)}, s32[3,3]{1,0:T(4,128)S(1)}, f32[3,128,1]{1,0,2:T(4,128)S(1)}, s32[]{:T(128)}, /*index=5*/s32[3]{0:T(128)S(1)}, ...), condition=%wide.while_cond, body=%wide.while_body.sunk | while | flops 147 | bytes 2739 | solution.py:42
  430.2 2.6 and_reduce_fusion.24
  436.8 2.6 and_reduce_fusion.24
  443.3 2.6 and_reduce_fusion.24
  449.1 19.6 %while.20 = (s32[]{:T(128)}, f32[3,128,2]{1,2,0:T(2,128)S(1)}, s32[3,3]{1,0:T(4,128)S(1)}, f32[3,128,1]{1,0,2:T(4,128)S(1)}, s32[]{:T(128)}, /*index=5*/s32[3]{0:T(128)S(1)}, s32[]{:T(128)}) while((s32[]{:T(128)}, f32[3,128,2]{1,2,0:T(2,128)S(1)}, s32[3,3]{1,0:T(4,128)S(1)}, f32[3,128,1]{1,0,2:T(4,128)S(1)}, s32[]{:T(128)}, ...), condition=%wide.while_cond.8, body=%wide.while_body.8.sunk | while | flops 147 | bytes 2739 | solution.py:42
  449.8 2.6 and_reduce_fusion.32
  456.4 2.6 and_reduce_fusion.32
  462.9 2.6 and_reduce_fusion.32
  468.9 30.9 %while.13 = (s32[]{:T(128)}, f32[3,128,2,64]{3,2,1,0:T(2,128)S(1)}, s32[3,4]{1,0:T(4,128)}, f32[3,128,1,64]{1,3,0,2:T(8,128)}, s32[]{:T(128)}, /*index=5*/s32[4]{0:T(128)S(1)}, s32[]{:T(128)}) while((s32[]{:T(128)}, f32[3,128,2,64]{3,2,1,0:T(2,128)S(1)}, s32[3,4]{1,0:T(4,128)}, f32[3,128,1,64]{1,3,0,2:T(8,128)}, s32[]{:T(128)}, ...), condition=%wide.while_cond.1, body=%wide.while_body.1.sunk | while | flops 8221 | bytes 295115 | solution.py:42
  470.3 3.3 and_reduce_fusion.25
  476.4 2.8 dynamic-update-slice.42
  480.6 3.3 and_reduce_fusion.25
  486.7 2.8 dynamic-update-slice.42
  490.9 3.3 and_reduce_fusion.25
  497.0 2.8 dynamic-update-slice.42
  504.2 22.8 %reduce-scatter.4.cloned.1.call-done = bf16[64,768]{1,0:T(8,128)(2,1)} async-done(((bf16[256,768]{1,0:T(8,128)(2,1)}), bf16[64,768]{1,0:T(8,128)(2,1)}) %reduce-scatter.4.cloned.1.call-update) | async-done | bytes 98320 | tf_op jit(solution)/shard_map/reduce_scatter | solution.py:214
  (432 shorter events, 246.3 us)
Async XLA Ops:
  6.5 134.8 %copy-start = (bf16[384,1536]{1,0:T(8,128)(2,1)S(1)}, bf16[384,1536]{1,0:T(8,128)(2,1)}, u32[]{:S(2)}) copy-start(bf16[384,1536]{1,0:T(8,128)(2,1)} %param.25) | copy-start | bytes 3538948
  6.5 4.2 copy-start.2
  6.5 46.8 %all-gather.7.cloned.1.call-start = ((), (), s32[]{:S(2)}) async-start(), calls=%async_computation.2 | async-start | bytes 1327104 | tf_op jit(solution)/shard_map/all_gather | solution.py:84
  7.3 88.1 %all-gather.9.cloned.1.call-start = ((), (), s32[]{:S(2)}) async-start(), calls=%async_computation.3 | async-start | bytes 1327104 | tf_op jit(solution)/shard_map/all_gather | solution.py:85
  8.0 129.4 %all-gather.5.cloned.1.call-start = ((), (), s32[]{:S(2)}) async-start(), calls=%async_computation.1 | async-start | bytes 1327104 | tf_op jit(solution)/shard_map/all_gather | solution.py:83
  8.7 518.3 %reduce-scatter.4.cloned.1.call-start = ((), (), s32[]{:S(2)}) async-start(), calls=%async_computation.4 | async-start | bytes 491520 | tf_op jit(solution)/shard_map/reduce_scatter | solution.py:214
  10.8 1.9 copy-start.22
  10.8 2.4 copy-start.23
  10.8 4.2 copy-start.27
  10.8 4.2 copy-start.28
  10.8 4.2 copy-start.29
  10.8 4.2 copy-start.30
  10.8 5.8 %copy-start.20 = (f32[1536]{0:T(1024)S(1)}, f32[1536]{0:T(1024)}, u32[]{:S(2)}) copy-start(f32[1536]{0:T(1024)} %param.27) | copy-start | bytes 18436
  10.8 5.8 %copy-start.1 = (s32[8]{0:T(128)S(1)}, s32[8]{0:T(128)}, u32[]{:S(2)}) copy-start(s32[8]{0:T(128)} %param.30) | copy-start | bytes 100
  11.2 6.2 %copy-start.35 = (s32[256]{0:T(256)S(1)}, s32[256]{0:T(256)}, u32[]{:S(2)}) copy-start(s32[256]{0:T(256)} %param.32) | copy-start | bytes 3076
  11.2 42.1 %copy-start.19 = (f32[1536]{0:T(1024)S(1)}, f32[1536]{0:T(1024)}, u32[]{:S(2)}) copy-start(f32[1536]{0:T(1024)} %param.21) | copy-start | bytes 18436
  97.5 49.9 %copy-start.21 = (f32[1536]{0:T(1024)S(1)}, f32[1536]{0:T(1024)}, u32[]{:S(2)}) copy-start(f32[1536]{0:T(1024)} %param.26) | copy-start | bytes 18436
  140.4 11.0 %copy-start.26 = (f32[192]{0:T(256)S(1)}, f32[192]{0:T(256)}, u32[]{:S(2)}) copy-start(f32[192]{0:T(256)} %param.29) | copy-start | bytes 2308
  140.4 51.8 %copy-start.6 = (bf16[256,768]{1,0:T(8,128)(2,1)S(1)}, bf16[256,768]{1,0:T(8,128)(2,1)}, u32[]{:S(2)}) copy-start(bf16[256,768]{1,0:T(8,128)(2,1)} %param.31) | copy-start | bytes 1179652
  141.6 51.5 %copy-start.31 = (bf16[768,192]{0,1:T(8,128)(2,1)S(1)}, bf16[768,192]{0,1:T(8,128)(2,1)}, u32[]{:S(2)}) copy-start(bf16[768,192]{0,1:T(8,128)(2,1)} %param.35) | copy-start | bytes 884740
  141.6 51.5 %copy-start.34 = (f32[768]{0:T(1024)S(1)}, f32[768]{0:T(1024)}, u32[]{:S(2)}) copy-start(f32[768]{0:T(1024)} %param.34) | copy-start | bytes 9220
  195.3 14.7 %collective-permute-start.10 = (bf16[3,16,128]{1,2,0:T(8,128)(2,1)S(1)}, bf16[3,16,128]{1,2,0:T(8,128)(2,1)S(1)}, u32[]{:S(2)}, u32[]{:S(2)}) collective-permute-start(bf16[3,16,128]{1,2,0:T(8,128)(2,1)S(1)} %copy.341), channel_id=1, source_target_pairs={{0,4},{4,0},{8,12},{12,8},{16,20},{20,16},{24,28},{28,24},{1,5},{5... | collective-permute-start | bytes 36872 | tf_op jit(solution)/shard_map/ppermute | solution.py:24
  198.3 153.1 %collective-permute-start = (bf16[3,256,128]{1,2,0:T(8,128)(2,1)S(1)}, bf16[3,256,128]{1,2,0:T(8,128)(2,1)S(1)}, u32[]{:S(2)}, u32[]{:S(2)}) collective-permute-start(bf16[3,256,128]{1,2,0:T(8,128)(2,1)S(1)} %gather_fusion.2), channel_id=1, source_target_pairs={{0,4},{4,0},{8,12},{12,8},{16,20},{20,16},{24,28},{28,24},{1,5},{5... | collective-permute-start | bytes 589832 | tf_op jit(solution)/shard_map/ppermute | solution.py:24
  202.6 81.8 %collective-permute-start.1 = (bf16[3,128,128]{1,2,0:T(8,128)(2,1)S(1)}, bf16[3,128,128]{1,2,0:T(8,128)(2,1)S(1)}, u32[]{:S(2)}, u32[]{:S(2)}) collective-permute-start(bf16[3,128,128]{1,2,0:T(8,128)(2,1)S(1)} %copy.299), channel_id=1, source_target_pairs={{0,4},{4,0},{8,12},{12,8},{16,20},{20,16},{24,28},{28,24},{1,5},{5... | collective-permute-start | bytes 294920 | tf_op jit(solution)/shard_map/ppermute | solution.py:24
  206.4 16.6 %copy-start.12 = (s32[3]{0:T(128)S(1)}, s32[3]{0:T(128)}, u32[]{:S(2)}) copy-start(s32[3]{0:T(128)} %constant.1102) | copy-start | bytes 40
  206.6 10.6 %collective-permute-start.4 = (bf16[3,64,128]{1,2,0:T(8,128)(2,1)S(1)}, bf16[3,64,128]{1,2,0:T(8,128)(2,1)S(1)}, u32[]{:S(2)}, u32[]{:S(2)}) collective-permute-start(bf16[3,64,128]{1,2,0:T(8,128)(2,1)S(1)} %copy.313), channel_id=1, source_target_pairs={{0,4},{4,0},{8,12},{12,8},{16,20},{20,16},{24,28},{28,24},{1,5},{5... | collective-permute-start | bytes 147464 | tf_op jit(solution)/shard_map/ppermute | solution.py:24
  208.0 4.7 collective-permute-start.7
  210.2 4.7 collective-permute-start.11
  212.8 49.3 %copy-start.18 = (s32[4]{0:T(128)S(1)}, s32[4]{0:T(128)}, u32[]{:S(2)}) copy-start(s32[4]{0:T(128)} %constant.1115) | copy-start | bytes 52
  212.8 6.6 %collective-permute-start.8 = (bf16[3,64,128]{1,2,0:T(8,128)(2,1)S(1)}, bf16[3,64,128]{1,2,0:T(8,128)(2,1)S(1)}, u32[]{:S(2)}, u32[]{:S(2)}) collective-permute-start(bf16[3,64,128]{1,2,0:T(8,128)(2,1)S(1)} %pad_maximum_fusion.8), channel_id=1, source_target_pairs={{0,8},{8,0},{4,12},{12,4},{16,24},{24,16},{20,28},{28,20},{1,9},{9... | collective-permute-start | bytes 147464 | tf_op jit(solution)/shard_map/ppermute | solution.py:24
  215.0 7.3 %collective-permute-start.12 = (bf16[3,64,128]{1,2,0:T(8,128)(2,1)S(1)}, bf16[3,64,128]{1,2,0:T(8,128)(2,1)S(1)}, u32[]{:S(2)}, u32[]{:S(2)}) collective-permute-start(bf16[3,64,128]{1,2,0:T(8,128)(2,1)S(1)} %pad_maximum_fusion.11), channel_id=1, source_target_pairs={{0,16},{16,0},{4,20},{20,4},{8,24},{24,8},{12,28},{28,12},{1,17},{... | collective-permute-start | bytes 147464 | tf_op jit(solution)/shard_map/ppermute | solution.py:24
  217.3 67.8 %collective-permute-start.5 = (bf16[3,128,128]{1,2,0:T(8,128)(2,1)S(1)}, bf16[3,128,128]{1,2,0:T(8,128)(2,1)S(1)}, u32[]{:S(2)}, u32[]{:S(2)}) collective-permute-start(bf16[3,128,128]{1,2,0:T(8,128)(2,1)S(1)} %pad_maximum_fusion.7), channel_id=1, source_target_pairs={{0,8},{8,0},{4,12},{12,4},{16,24},{24,16},{20,28},{28,20},{1,9},{9... | collective-permute-start | bytes 294920 | tf_op jit(solution)/shard_map/ppermute | solution.py:24
  219.5 68.6 %collective-permute-start.9 = (bf16[3,128,128]{1,2,0:T(8,128)(2,1)S(1)}, bf16[3,128,128]{1,2,0:T(8,128)(2,1)S(1)}, u32[]{:S(2)}, u32[]{:S(2)}) collective-permute-start(bf16[3,128,128]{1,2,0:T(8,128)(2,1)S(1)} %pad_maximum_fusion.9), channel_id=1, source_target_pairs={{0,16},{16,0},{4,20},{20,4},{8,24},{24,8},{12,28},{28,12},{1,17},{... | collective-permute-start | bytes 294920 | tf_op jit(solution)/shard_map/ppermute | solution.py:24
  262.0 26.9 %copy-start.11 = (s32[3]{0:T(128)S(1)}, s32[3]{0:T(128)}, u32[]{:S(2)}) copy-start(s32[3]{0:T(128)} %constant.1078) | copy-start | bytes 40
  282.9 25.4 %copy-start.17 = (s32[4]{0:T(128)S(1)}, s32[4]{0:T(128)}, u32[]{:S(2)}) copy-start(s32[4]{0:T(128)} %constant.1090) | copy-start | bytes 52
  285.1 68.9 %collective-permute-start.2 = (bf16[3,256,128]{1,2,0:T(8,128)(2,1)}, bf16[3,256,128]{1,2,0:T(8,128)(2,1)}, u32[]{:S(2)}, u32[]{:S(2)}) collective-permute-start(bf16[3,256,128]{1,2,0:T(8,128)(2,1)} %pad_maximum_fusion.4), channel_id=1, source_target_pairs={{0,8},{8,0},{4,12},{12,4},{16,24},{24,16},{20,28},{28,20},{1,9},{9... | collective-permute-start | bytes 589832 | tf_op jit(solution)/shard_map/ppermute | solution.py:24
  285.9 70.6 %collective-permute-start.6 = (bf16[3,256,128]{1,2,0:T(8,128)(2,1)}, bf16[3,256,128]{1,2,0:T(8,128)(2,1)}, u32[]{:S(2)}, u32[]{:S(2)}) collective-permute-start(bf16[3,256,128]{1,2,0:T(8,128)(2,1)} %pad_maximum_fusion.5), channel_id=1, source_target_pairs={{0,16},{16,0},{4,20},{20,4},{8,24},{24,8},{12,28},{28,12},{1,17},{... | collective-permute-start | bytes 589832 | tf_op jit(solution)/shard_map/ppermute | solution.py:24
  353.5 4.1 copy-start.8
  354.0 4.3 copy-start.10
  354.0 4.3 copy-start.25
  355.8 70.6 %collective-permute-start.3 = (bf16[3,512,128]{1,2,0:T(8,128)(2,1)}, bf16[3,512,128]{1,2,0:T(8,128)(2,1)}, u32[]{:S(2)}, u32[]{:S(2)}) collective-permute-start(bf16[3,512,128]{1,2,0:T(8,128)(2,1)} %pad_maximum_fusion.1), channel_id=1, source_target_pairs={{0,16},{16,0},{4,20},{20,4},{8,24},{24,8},{12,28},{28,12},{1,17},{... | collective-permute-start | bytes 1179656 | tf_op jit(solution)/shard_map/ppermute | solution.py:24
  403.6 23.9 %copy-start.5 = (bf16[3,128,64]{1,2,0:T(8,128)(2,1)S(1)}, bf16[3,128,64]{1,2,0:T(8,128)(2,1)}, u32[]{:S(2)}) copy-start(bf16[3,128,64]{1,2,0:T(8,128)(2,1)} %gather_fusion.3) | copy-start | bytes 147460
  429.1 39.7 %copy-start.16 = (s32[4]{0:T(128)S(1)}, s32[4]{0:T(128)}, u32[]{:S(2)}) copy-start(s32[4]{0:T(128)} %constant.1041) | copy-start | bytes 52
  468.8 32.4 %copy-start.13 = (f32[3,256]{1,0:T(4,128)S(1)}, f32[3,256]{1,0:T(4,128)}, u32[]{:S(2)}) copy-start(f32[3,256]{1,0:T(4,128)} %reshape.651) | copy-start | bytes 9220
  468.9 32.4 %copy-start.14 = (f32[3,256]{1,0:T(4,128)S(1)}, f32[3,256]{1,0:T(4,128)}, u32[]{:S(2)}) copy-start(f32[3,256]{1,0:T(4,128)} %reshape.650) | copy-start | bytes 9220
  468.9 32.4 %copy-start.15 = (f32[3,256]{1,0:T(4,128)S(1)}, f32[3,256]{1,0:T(4,128)}, u32[]{:S(2)}) copy-start(f32[3,256]{1,0:T(4,128)} %reshape.642) | copy-start | bytes 9220
  468.9 32.5 %copy-start.4 = (f32[3,256,64]{1,2,0:T(8,128)S(1)}, f32[3,256,64]{1,2,0:T(8,128)}, u32[]{:S(2)}) copy-start(f32[3,256,64]{1,2,0:T(8,128)} %copy.346) | copy-start | bytes 589828
  501.0 2.2 copy-start.7
  (5 other events, 7.3 us)
Sparse Core Ops, SparseCore 0:
  9.5 43.7 all-gather.6
  55.5 39.8 all-gather.8
  97.6 39.8 all-gather.4
  504.3 22.6 reduce-scatter.3
where the time goes:
time: 539 us; the launch traced here: 535 us
  other arithmetic  187 us (35%)
  waiting for transfers between devices  147 us (27%)
  local copies, waits for them, and re-layouts  107 us (20%)
  blocking collectives  45.2 us (8%)
  matrix products  18.3 us (3%)
  between operations  15.5 us (3%)
  starting transfers between devices  15.4 us (3%)
    scatter x72, other arithmetic  171 us
    scatter x126, local copies, waits for them, and re-layouts  84.2 us
    all_gather x1, waiting for transfers between devices, shards(): lax.all_gather(vit_value, 'tile', axis=0, tiled=True)  39.9 us
    all_gather x1, waiting for transfers between devices, shards(): lax.all_gather(vit_query, 'tile', axis=0, tiled=True)  39.9 us
    unnamed x1, blocking collectives  39.3 us
    all_gather x1, waiting for transfers between devices, shards(): lax.all_gather(vit_key, 'tile', axis=0, tiled=True)  35.9 us
    reduce_scatter x1, waiting for transfers between devices, shards(): lax.psum_scatter(jnp.dot(attended_slide, slide_out, preferred_element_typ...  22.8 us
    ppermute x13, starting transfers between devices, partner(): return lax.ppermute(block, axis, route)  15.3 us
  transfers between devices with their start and end apart: 17, of which 8 were waited for; matrix products, arithmetic and copies ran while one was open for 41% of the time, Pallas kernels for 0%

commit v1 on v0

v1 whole, which is shorter than its diff:
```python
import functools
import math

import jax
import jax.numpy as jnp
from jax import lax
from jax.experimental import pallas as pl
from jax.experimental.pallas import tpu as pltpu
from jax.sharding import PartitionSpec as P

DV = 1536
HV = 24
DS = 768
HS = 12
HEAD = 64

EPS = 1e-06
LOW = -1e30
F32 = jnp.float32
BF16 = jnp.bfloat16
I32 = jnp.int32
VMEM = pl.BlockSpec(memory_space=pltpu.VMEM)
SMEM = pl.BlockSpec(memory_space=pltpu.SMEM)
NT = (((1,), (1,)), ((), ()))
ROOM = 56 * 1024 * 1024


def params():
    return pltpu.CompilerParams(vmem_limit_bytes=ROOM)


def round_up(value, unit):
    return -(-value // unit) * unit


def layer_norm(values, scaling):
    center = values - jnp.mean(values, axis=-1, keepdims=True)
    spread = jnp.mean(center * center, axis=-1, keepdims=True)
    return center * lax.rsqrt(spread + EPS) * scaling


def dot(a, b):
    return jnp.dot(a, b, preferred_element_type=F32)


def dot_nt(a, b):
    return lax.dot_general(a, b, NT, preferred_element_type=F32)


def class_kernel(fresh, patch_ref, gain_ref, pos_ref, kept_ref, where_ref, pack_ref):
    parts, width = pack_ref.shape
    cut = DV // parts
    rows = kept_ref.shape[0]
    row = patch_ref[0, 0:1].astype(F32)
    normed = layer_norm(row, gain_ref[...]).astype(BF16).astype(F32)
    first = where_ref[0] * rows
    ids = lax.broadcasted_iota(I32, (rows, width), 0) + first
    hit = (ids == pos_ref[...]) & (kept_ref[...] != 0)
    flags = jnp.max(jnp.where(hit, 1.0, 0.0), axis=0, keepdims=True)
    pack_ref[...] = jnp.broadcast_to(flags, (parts, width))
    for part in range(parts):
        pack_ref[part : part + 1, 0:cut] = normed[:, part * cut : (part + 1) * cut]


def base_kernel(
    cached_ref, kept_ref, mask_ref, gain_ref, wq_ref, wk_ref, wv_ref, rows_ref, q_ref, kv_ref
):
    rows = jnp.where(
        kept_ref[...] == 0, mask_ref[...].astype(BF16).astype(F32), cached_ref[...].astype(F32)
    )
    rows_ref[...] = rows.astype(BF16)
    normed = layer_norm(rows, gain_ref[...]).astype(BF16)
    project(normed, wq_ref, wk_ref, wv_ref, q_ref, kv_ref)


def project(normed, wq_ref, wk_ref, wv_ref, q_ref, kv_ref):
    q = dot(normed, wq_ref[...]).astype(BF16) * BF16(1.0 / math.sqrt(HEAD))
    k = dot(normed, wk_ref[...]).astype(BF16)
    v = dot(normed, wv_ref[...]).astype(BF16)
    q_ref[:, 0:192] = q
    q_ref[:, 192:256] = jnp.zeros((q.shape[0], 64), BF16)
    kv_ref[:, 0:192] = k
    kv_ref[:, 192:256] = v[:, 128:192]
    kv_ref[:, 256:384] = v[:, 0:128]


def query_kernel(cut, pack_ref, wq_ref, part_ref):
    rows = pack_ref[:, 0:cut].astype(BF16)
    part = dot(rows, wq_ref[...])
    if len(part_ref.shape) == 3:
        part_ref[...] = jnp.broadcast_to(part[None], part_ref.shape)
    else:
        part_ref[...] = part


def fold_kernel(part_ref, wk_ref, fold_ref):
    if len(part_ref.shape) == 3:
        queries = part_ref[0]
        for index in range(1, part_ref.shape[0]):
            queries = queries + part_ref[index]
    else:
        queries = part_ref[...]
    tiles, width = queries.shape
    queries = queries.astype(BF16).astype(F32)
    spread = jnp.broadcast_to(queries[:, None], (tiles, 8, width))
    head = lax.broadcasted_iota(I32, spread.shape, 1)
    lane = lax.broadcasted_iota(I32, spread.shape, 2)
    spread = jnp.where(lane // HEAD == head, spread, 0.0).reshape(tiles * 8, width).astype(BF16)
    cut = wk_ref.shape[0]
    result = dot_nt(spread, wk_ref[...]).reshape(tiles, 8, cut)
    fold_ref[:, :, 0:cut] = result


def tile_kernel(
    cut, patch_ref, gain_ref, fold_ref, wv_ref, wo_ref, scale_ref, bias_ref, where_ref,
    sent_ref, fold_s,
):
    for part in range(fold_ref.shape[0]):
        fold_s[:, part * cut : (part + 1) * cut] = fold_ref[part, :, 0:cut]
    tokens = patch_ref[0].astype(F32)
    normed = layer_norm(tokens, gain_ref[...]).astype(BF16)
    scores = dot_nt(fold_s[...].astype(BF16), normed) * (1.0 / math.sqrt(HEAD))
    highest = jnp.max(scores, axis=-1, keepdims=True)
    exponent = jnp.exp(scores - highest)
    prob = (exponent / jnp.sum(exponent, axis=-1, keepdims=True)).astype(BF16)
    mixed = dot(prob, normed).astype(BF16)
    values = dot(mixed, wv_ref[...])
    head = lax.broadcasted_iota(I32, values.shape, 0)
    lane = lax.broadcasted_iota(I32, values.shape, 1)
    tmix = jnp.sum(jnp.where(lane // HEAD == head, values, 0.0), axis=0, keepdims=True)
    tmix = jnp.broadcast_to(tmix, (8, tmix.shape[1])).astype(BF16)
    share = dot(tmix, wo_ref[...])[0:1] * scale_ref[...]
    share = share + jnp.where(where_ref[1] == 0, tokens[0:1], 0.0)
    devices = sent_ref.shape[0]
    sent_ref[:, 0:DV] = jnp.broadcast_to(share, (devices, DV))
    sent_ref[:, DV:] = jnp.broadcast_to(bias_ref[...], (devices, bias_ref.shape[1]))


def branch_rows(position, axis, offset_ref, where_ref, head, span, total):
    shape = (1, 8) if axis == 1 else (8, 1)
    branch = lax.broadcasted_iota(I32, shape, axis)
    residue = jnp.full(shape, -1, I32)
    shift = jnp.zeros(shape, I32)
    for b in range(offset_ref.shape[0]):
        residue = jnp.where(branch == b, offset_ref[b, where_ref[1] * 3 + head], residue)
        length = min(2 * span * 4**b, total)
        shift = jnp.where(branch == b, length.bit_length() - 1, shift)
    below = jnp.left_shift(jnp.int32(1), branch) - 1
    mine = jnp.right_shift(jnp.zeros(shape, I32) + where_ref[0] * span, shift)
    return ((position & below) == residue) & (jnp.right_shift(position, shift) == mine)


def value_lanes(head):
    group = {0: 2, 1: 3, 2: 1}[head]
    lane = lax.broadcasted_iota(I32, (1, 256), 1)
    return lane // HEAD == group


def attend(q, q_rows, kv_ref, k_rows, head):
    lane = lax.broadcasted_iota(I32, (1, 256), 1)
    q_head = jnp.where(lane // HEAD == head, q, jnp.zeros_like(q))
    scores = dot_nt(q_head, kv_ref[:, 0:256])
    count = dot(q_rows, k_rows)
    scores = jnp.where(count > 0.5, scores, LOW)
    highest = jnp.max(scores, axis=-1, keepdims=True)
    weight = jnp.exp(scores - highest) * count
    denom = jnp.sum(weight, axis=-1, keepdims=True)
    numer = dot(weight.astype(BF16), kv_ref[:, 128:384])
    return highest, denom, numer


def as_bf16(condition):
    return jnp.where(condition, 1.0, 0.0).astype(BF16)


def merge(old, new):
    old_max, old_den, old_num = old
    new_max, new_den, new_num = new
    top = jnp.maximum(old_max, new_max)
    keep = jnp.exp(old_max - top)
    take = jnp.exp(new_max - top)
    return top, old_den * keep + new_den * take, old_num * keep + new_num * take


def store_state(state, head, ml_ref, acc_ref):
    highest, denom, numer = state
    lane = lax.broadcasted_iota(I32, (1, 128), 1)
    ml = jnp.where(lane == head, highest, ml_ref[...])
    ml_ref[...] = jnp.where(lane == head + 8, denom, ml)
    acc_ref[...] = jnp.where(value_lanes(head), numer, acc_ref[...])


def load_state(head, ml_ref, acc_ref):
    return ml_ref[:, head : head + 1], ml_ref[:, head + 8 : head + 9], acc_ref[...]


def key_rows(step, block, pos_ref, flag_ref, offset_ref, where_ref, head, span, total):
    position = lax.broadcasted_iota(I32, (1, block), 1) + step * block
    rows = branch_rows(position, 0, offset_ref, where_ref, head, span, total)
    taken = (position == pos_ref[...]) & (flag_ref[...] > 0.5)
    taken = jnp.max(jnp.where(taken, 1.0, 0.0), axis=0, keepdims=True)
    return as_bf16(rows & (taken < 0.5))


def base_attention_kernel(
    span, total, q_ref, kv_ref, pos_ref, flag_ref, offset_ref, where_ref, ml_ref, acc_ref
):
    step = pl.program_id(0)
    block = kv_ref.shape[0]
    rows = q_ref.shape[0]

    @pl.when(step == 0)
    def _():
        lane = lax.broadcasted_iota(I32, (rows, 128), 1)
        ml_ref[...] = jnp.where(lane < 8, LOW, 0.0)
        acc_ref[...] = jnp.zeros_like(acc_ref)

    place = lax.broadcasted_iota(I32, (rows, 1), 0) + where_ref[0] * span
    for head in range(3):
        q_rows = as_bf16(branch_rows(place, 1, offset_ref, where_ref, head, span, total))
        k_rows = key_rows(
            step, block, pos_ref, flag_ref, offset_ref, where_ref, head, span, total
        )
        new = attend(q_ref[...], q_rows, kv_ref, k_rows, head)
        store_state(merge(load_state(head, ml_ref, acc_ref), new), head, ml_ref, acc_ref)


def fresh_kernel(
    span, total, shares_ref, final_ref, embed_ref, gain_ref, wq_ref, wk_ref, wv_ref,
    q_ref, kv_ref, pos_ref, posrow_ref, flag_ref, flagrow_ref, ml_ref, acc_ref, rows_ref,
    offset_ref, where_ref, out0_ref, out1_ref, out2_ref, out3_ref, mine_ref,
    fresh_s, qf_s, kvf_s, mlf_s, accf_s, att_s,
):
    step = pl.program_id(0)
    block = kv_ref.shape[0]
    rows = q_ref.shape[0]
    padded = fresh_s.shape[0]
    seg = where_ref[1]

    @pl.when(step == 0)
    def _():
        shares = shares_ref[:, 0:DV]
        groups = shares_ref.shape[0] // 4
        pooled = jnp.sum(shares.reshape(groups, 4, DV), axis=1)
        summary = layer_norm(pooled, final_ref[...]).astype(BF16)
        fresh_s[...] = jnp.zeros_like(fresh_s)
        for part in range(4):
            cols = slice(part * 192, (part + 1) * 192)
            piece = dot(summary, embed_ref[part]) + shares_ref[part : part + 1, DV : DV + 192]
            fresh_s[0:groups, cols] = piece.astype(BF16).astype(F32)
        normed = layer_norm(fresh_s[...], gain_ref[...]).astype(BF16)
        project(normed, wq_ref, wk_ref, wv_ref, qf_s, kvf_s)
        lane = lax.broadcasted_iota(I32, (padded, 128), 1)
        mlf_s[...] = jnp.where(lane < 8, LOW, 0.0)
        accf_s[...] = jnp.zeros_like(accf_s)

    for head in range(3):
        q_rows = as_bf16(branch_rows(pos_ref[...], 1, offset_ref, where_ref, head, span, total))
        k_rows = key_rows(
            step, block, pos_ref, flag_ref, offset_ref, where_ref, head, span, total
        )
        new = attend(qf_s[...], q_rows, kv_ref, k_rows, head)
        store_state(merge(load_state(head, mlf_s, accf_s), new), head, mlf_s, accf_s)

    @pl.when(step == pl.num_programs(0) - 1)
    def _():
        place = lax.broadcasted_iota(I32, (rows, 1), 0) + where_ref[0] * span
        base = jnp.zeros((rows, 256), F32)
        fresh = jnp.zeros((padded, 256), F32)
        for head in range(3):
            q_rows = as_bf16(branch_rows(place, 1, offset_ref, where_ref, head, span, total))
            f_rows = as_bf16(
                branch_rows(pos_ref[...], 1, offset_ref, where_ref, head, span, total)
            )
            k_rows = as_bf16(
                branch_rows(posrow_ref[...], 0, offset_ref, where_ref, head, span, total)
                & (flagrow_ref[...] > 0.5)
            )
            lanes = value_lanes(head)
            new = attend(q_ref[...], q_rows, kvf_s, k_rows, head)
            top, den, num = merge(load_state(head, ml_ref, acc_ref), new)
            base = jnp.where(lanes, num / den, base)
            new = attend(qf_s[...], f_rows, kvf_s, k_rows, head)
            top, den, num = merge(load_state(head, mlf_s, accf_s), new)
            fresh = jnp.where(lanes, num / jnp.where(den > 0.0, den, 1.0), fresh)
        chosen = as_bf16((place == posrow_ref[...]) & (flagrow_ref[...] > 0.5))
        hit = jnp.sum(chosen.astype(F32), axis=1, keepdims=True) > 0.5
        att_s[...] = jnp.where(hit, dot(chosen, fresh.astype(BF16)), base)
        count = rows // 4
        outs = (out0_ref, out1_ref, out2_ref, out3_ref)
        for mask in range(4):
            start = pl.multiple_of((seg ^ mask) * count, count)
            outs[mask][...] = att_s[pl.ds(start, count), :].astype(BF16)
        start = pl.multiple_of(seg * count, count)
        place = lax.broadcasted_iota(I32, (count, 1), 0) + where_ref[0] * span + start
        chosen = as_bf16((place == posrow_ref[...]) & (flagrow_ref[...] > 0.5))
        hit = jnp.sum(chosen.astype(F32), axis=1, keepdims=True) > 0.5
        placed = dot(chosen, fresh_s[...].astype(BF16))
        old = rows_ref[pl.ds(start, count), :].astype(F32)
        mine_ref[...] = jnp.where(hit, placed, old)


def out_kernel(a0_ref, a1_ref, a2_ref, a3_ref, wo_ref, mine_ref, where_ref, out_ref):
    total = mine_ref[...]
    seg = where_ref[1]
    for mask, ref in enumerate((a0_ref, a1_ref, a2_ref, a3_ref)):
        weight = wo_ref[seg ^ mask]
        att = ref[...]
        total = total + dot(att[:, 128:256], weight[0:128])
        total = total + dot(att[:, 64:128], weight[128:192])
    out_ref[...] = total.astype(BF16)


def trade(block, axis, mask):
    count = lax.axis_size(axis)
    return lax.ppermute(block, axis, [(i, i ^ mask) for i in range(count)])


def gather_tile(block):
    return lax.all_gather(block, "tile", axis=0, tiled=True)


def shards(
    patches, vit_norm_gain, vit_query, vit_key, vit_value, vit_out, layer_scale, final_gain,
    embed_proj, embed_bias, slide_pos, cached, kept, mask_token, slide_gain, slide_query,
    slide_key, slide_value, slide_out, offsets,
):
    tiles = lax.axis_size("tile")
    segs = lax.axis_size("seg")
    devices = tiles * segs
    span = cached.shape[0]
    total = span * tiles
    cut, local_cols = vit_query.shape
    fresh = slide_pos.shape[0]
    padded = max(16, fresh)
    call = pl.pallas_call
    sds = jax.ShapeDtypeStruct

    here = jnp.stack([lax.axis_index("tile"), lax.axis_index("seg")]).astype(I32)
    kept_col = kept.reshape(span, 1)
    gain_vit = vit_norm_gain.reshape(1, DV)
    gain_slide = slide_gain.reshape(1, DS)

    base_rows, q_base, kv_base = call(
        base_kernel,
        out_shape=(sds((span, DS), BF16), sds((span, 256), BF16), sds((span, 384), BF16)),
        in_specs=[VMEM] * 7,
        out_specs=(VMEM,) * 3,
        compiler_params=params(),
        name="base_rows",
    )(cached, kept_col, mask_token.reshape(1, DS), gain_slide, slide_query, slide_key, slide_value)

    width = round_up(cut + fresh, 128)
    posrow = jnp.full((1, width), -1, I32).at[0, cut : cut + fresh].set(slide_pos)
    pack = call(
        functools.partial(class_kernel, fresh),
        out_shape=sds((tiles, width), F32),
        grid=(1,),
        in_specs=[
            pl.BlockSpec((1, 16, DV), lambda i: (0, 0, 0)), VMEM, VMEM, VMEM, SMEM,
        ],
        out_specs=VMEM,
        compiler_params=params(),
        name="class_row",
    )(patches, gain_vit, posrow, kept_col, here)
    pack = lax.all_to_all(pack, "tile", 0, 0, tiled=True)
    kv_all = gather_tile(kv_base)
    wv_all = gather_tile(vit_value)
    embed_all = lax.all_gather(embed_proj, "seg", axis=0)
    slide_out_all = lax.all_gather(slide_out, "seg", axis=0)

    flags = jnp.sum(pack[:, cut : cut + fresh], axis=0)
    flag_row = jnp.pad(flags, (0, padded - fresh)).reshape(1, padded)
    flag_col = flag_row.reshape(padded, 1)
    pos_pad = jnp.pad(slide_pos, (0, padded - fresh), constant_values=-1)
    pos_row, pos_col = pos_pad.reshape(1, padded), pos_pad.reshape(padded, 1)

    small = tiles <= 8
    part_shape = (tiles, fresh, local_cols) if small else (fresh, local_cols)
    part = call(
        functools.partial(query_kernel, cut),
        out_shape=sds(part_shape, F32),
        in_specs=[VMEM] * 2,
        out_specs=VMEM,
        compiler_params=params(),
        name="query_share",
    )(pack, vit_query)
    if small:
        part = lax.all_to_all(part, "tile", 0, 0, tiled=True)
    else:
        part = lax.psum(part, "tile")
    folded = call(
        fold_kernel,
        out_shape=sds((fresh, 8, round_up(cut, 128)), F32),
        in_specs=[VMEM] * 2,
        out_specs=VMEM,
        compiler_params=params(),
        name="fold_key",
    )(part, vit_key)
    folded = lax.all_to_all(folded, "tile", 0, 0, tiled=True)

    bias_row = jnp.pad(embed_bias, (0, 256 - embed_bias.shape[0])).reshape(1, 256)
    sent = call(
        functools.partial(tile_kernel, cut),
        out_shape=sds((devices, DV + 256), F32),
        in_specs=[VMEM] * 7 + [SMEM],
        out_specs=VMEM,
        scratch_shapes=[pltpu.VMEM((8, DV), F32)],
        compiler_params=params(),
        name="tile_attention",
    )(
        patches, gain_vit, folded, wv_all, vit_out, layer_scale.reshape(1, DV), bias_row, here,
    )
    shares = lax.all_to_all(sent, ("tile", "seg"), 0, 0, tiled=True)

    block = min(total, 2048)
    steps = total // block
    kv_spec = pl.BlockSpec((block, 384), lambda i: (i, 0))
    ml, acc = call(
        functools.partial(base_attention_kernel, span, total),
        out_shape=(sds((span, 128), F32), sds((span, 256), F32)),
        grid=(steps,),
        in_specs=[VMEM, kv_spec, VMEM, VMEM, SMEM, SMEM],
        out_specs=(VMEM, VMEM),
        compiler_params=params(),
        name="base_attention",
    )(q_base, kv_all, pos_col, flag_col, offsets, here)

    count = span // segs
    outs = call(
        functools.partial(fresh_kernel, span, total),
        out_shape=(sds((count, 256), BF16),) * 4 + (sds((count, DS), F32),),
        grid=(steps,),
        in_specs=[VMEM] * 8 + [kv_spec] + [VMEM] * 7 + [SMEM] * 2,
        out_specs=(VMEM,) * 5,
        scratch_shapes=[
            pltpu.VMEM((padded, DS), F32),
            pltpu.VMEM((padded, 256), BF16),
            pltpu.VMEM((padded, 384), BF16),
            pltpu.VMEM((padded, 128), F32),
            pltpu.VMEM((padded, 256), F32),
            pltpu.VMEM((span, 256), F32),
        ],
        compiler_params=params(),
        name="fresh_attention",
    )(
        shares, final_gain.reshape(1, DV), embed_all, gain_slide, slide_query, slide_key,
        slide_value, q_base, kv_all, pos_col, pos_row, flag_col, flag_row, ml, acc, base_rows,
        offsets, here,
    )
    swapped = [outs[0]] + [trade(outs[mask], "seg", mask) for mask in range(1, 4)]
    return call(
        out_kernel,
        out_shape=sds((count, DS), BF16),
        in_specs=[VMEM] * 6 + [SMEM],
        out_specs=VMEM,
        compiler_params=params(),
        name="slide_next",
    )(*swapped, slide_out_all, outs[4], here)


def solution(mesh):
    return jax.shard_map(
        shards,
        mesh=mesh,
        in_specs=(
            P("tile", None, None), P(), P("tile", "seg"), P("tile", "seg"), P("tile", "seg"),
            P("seg", None), P(), P(), P(None, "seg"), P("seg"), P(), P("tile", None), P("tile"),
            P(), P(), P(None, "seg"), P(None, "seg"), P(None, "seg"), P("seg", None), P(),
        ),
        out_specs=P(("tile", "seg"), None),
        check_vma=False,
    )
```

time: 539 us -> 154 us (0.29)
  other arithmetic: 187 us -> 1.97 us
  waiting for transfers between devices: 147 us -> 50.1 us
  local copies, waits for them, and re-layouts: 107 us -> 23.9 us
  Pallas kernels: 0 us -> 30.3 us
  blocking collectives: 45.2 us -> 25.9 us
  matrix products: 18.3 us -> 0 us
  starting transfers between devices: 15.4 us -> 8.14 us
    scatter x74 -> x0, other arithmetic: 171 us -> none
    scatter x132 -> x1, local copies, waits for them, and re-layouts: 84.8 us -> 0.88 us  [shards(): posrow = jnp.full((1, width), -1, I32).at[0, cut:cut + fresh].set(slide_pos)]
    all_gather x3 -> x4, waiting for transfers between devices: 116 us -> 35.8 us  [the longest x1 17.7 us: shards(): embed_all = lax.all_gather(embed_proj, 'seg', axis=0)]
    unnamed x1 -> x0, blocking collectives: 39.3 us -> none
    pallas_call x0 -> x8, Pallas kernels: none -> 30.3 us  [the longest x1 8.88 us: shards(): call(functools.partial(fresh_kernel, span, total), out_shape=(sds((count,...]
    all_to_all x0 -> x2, blocking collectives: none -> 25.9 us  [the longest x1 13.6 us: shards(): pack = lax.all_to_all(pack, 'tile', 0, 0, tiled=True)]
    reduce_scatter x1 -> x0, waiting for transfers between devices: 22.8 us -> none  [shards(): lax.psum_scatter(jnp.dot(attended_slide, slide_out, preferred_element_typ...]
    dot_general x25 -> x0, matrix products: 18.3 us -> none  [the longest x5 3.57 us: shards(): jnp.einsum('hqk,hkd->hqd', exponent_seg.astype(jnp.bfloat16), values_seg,...]
  transfers between devices with their start and end apart: 17 -> 9, of which waited for: 8 -> 5; matrix products, arithmetic and copies ran while one was open for 41% -> 16% of each run, Pallas kernels for 0% -> 18%
where the time goes in v1:
time: 154 us
  waiting for transfers between devices  50.1 us (33%)
  Pallas kernels  30.3 us (20%)
  blocking collectives  25.9 us (17%)
  local copies, waits for them, and re-layouts  23.9 us (16%)
  between operations  13.2 us (9%)
  starting transfers between devices  8.14 us (5%)
  other arithmetic  1.97 us (1%)
    all_gather x1, waiting for transfers between devices, shards(): embed_all = lax.all_gather(embed_proj, 'seg', axis=0)  17.7 us
    all_gather x2, waiting for transfers between devices, gather_tile(): return lax.all_gather(block, 'tile', axis=0, tiled=True)  13.7 us
    all_to_all x1, blocking collectives, shards(): pack = lax.all_to_all(pack, 'tile', 0, 0, tiled=True)  13.6 us
    all_to_all x1, blocking collectives, shards(): part = lax.all_to_all(part, 'tile', 0, 0, tiled=True)  12.3 us
    pallas_call x1, Pallas kernels, shards(): call(functools.partial(fresh_kernel, span, total), out_shape=(sds((count,...  8.88 us
    unnamed x31, local copies, waits for them, and re-layouts  7.32 us
    all_to_all x1, waiting for transfers between devices, shards(): shares = lax.all_to_all(sent, ('tile', 'seg'), 0, 0, tiled=True)  6.54 us
    pallas_call x1, Pallas kernels, shards(): call(functools.partial(base_attention_kernel, span, total), out_shape=(sd...  6.18 us
  transfers between devices with their start and end apart: 9, of which 5 were waited for; matrix products, arithmetic and copies ran while one was open for 16% of the time, Pallas kernels for 18%

profile of v1, /device:TPU:0, one launch (start us, length us, event | category | flops | bytes accessed | tf_op | source)
XLA Modules:
  0.0 153.5 jit_solution(1538664224359729473)
XLA Ops:
  6.5 0.7 all-gather.7.cloned.1.call-update
  7.3 1.5 copy.45.kept_ref
  8.8 1.3 reshape.75.gain_ref
  10.1 1.9 %copy.55.wq_ref = bf16[768,192]{1,0:T(8,128)(2,1)} copy(bf16[768,192]{0,1:T(8,128)(2,1)} %param.37) | data formatting | bytes 589824 | tf_op args[15]
  12.0 1.9 %copy.56.wk_ref = bf16[768,192]{1,0:T(8,128)(2,1)} copy(bf16[768,192]{0,1:T(8,128)(2,1)} %param.38) | data formatting | bytes 589824 | tf_op args[16]
  13.9 0.9 copy.57.wv_ref
  14.8 0.6 reshape.76.mask_ref
  15.4 3.0 %base_rows.1 = (bf16[256,768]{1,0:T(8,128)(2,1)}, bf16[256,256]{1,0:T(8,128)(2,1)}, bf16[256,384]{1,0:T(8,128)(2,1)}) custom-call(bf16[256,768]{1,0:T(8,128)(2,1)} %cached_ref.1, s32[256,1]{1,0:T(8,128)} %copy.45.kept_ref, f32[1,768]{1,0:T(1,128)} %reshape.76.mask_ref, f32[1,768]{1,0:T(1,128)} %reshape.75.gain_ref, bf16[768,192]{1,0:T(8,128)(2,1)} %copy.55.wq_ref, ...), custom_call_target="tpu_custom_call" | custom-call | tf_op jit(solution)/shard_map/base_rows/pallas_call | solution.py:344
  18.5 0.7 all-gather.11.cloned.1.call-update
  19.2 0.5 all-gather.13.cloned.1.call-update
  19.8 0.6 reshape.68.gain_ref
  20.4 0.6 slice.23
  21.0 0.6 and_reduce_fusion
  21.6 0.6 fusion
  22.3 0.9 scatter.4.pos_ref
  23.2 0.6 pad_add_fusion.where_ref
  23.8 1.8 %class_row.1 = f32[8,256]{1,0:T(8,128)} custom-call(bf16[1,257,1536]{2,1,0:T(8,128)(2,1)} %patch_ref.3, f32[1,1536]{1,0:T(1,128)} %reshape.68.gain_ref, s32[1,256]{1,0:T(1,128)} %copy-done.11, s32[256,1]{1,0:T(8,128)} %copy.45.kept_ref, s32[2]{0:T(128)} %pad_add_fusion.where_ref), custom_call_target="tpu_custom_call" | custom-call | tf_op jit(solution)/shard_map/class_row/pallas_call | solution.py:355
  25.6 0.7 copy.46
  26.3 13.6 %all_to_all.32 = f32[8,1,256]{2,1,0:T(1,128)S(1)} all-to-all(f32[8,1,256]{2,1,0:T(1,128)S(1)} %copy.46), channel_id=1, replica_groups=mesh['tile'=8,'seg'=4] {'tile'}, dimensions={0} | all-to-all | bytes 16384 | tf_op jit(solution)/shard_map/all_to_all | solution.py:366
  39.9 0.6 copy.65
  40.5 1.7 %query_share.1 = f32[8,8,384]{2,1,0:T(8,128)} custom-call(f32[8,256]{1,0:T(8,128)} %bitcast.29, bf16[192,384]{1,0:T(8,128)(2,1)} %wq_ref.3), custom_call_target="tpu_custom_call" | custom-call | tf_op jit(solution)/shard_map/query_share/pallas_call | solution.py:380
  42.2 12.3 %all_to_all.33.part_ref = f32[8,8,384]{2,1,0:T(8,128)} all-to-all(f32[8,8,384]{2,1,0:T(8,128)} %query_share.1), channel_id=1, replica_groups=mesh['tile'=8,'seg'=4] {'tile'}, dimensions={0} | all-to-all | bytes 196608 | tf_op jit(solution)/shard_map/all_to_all | solution.py:389
  54.5 1.8 %fold_key.1 = f32[8,8,256]{2,1,0:T(8,128)} custom-call(f32[8,8,384]{2,1,0:T(8,128)} %all_to_all.33.part_ref, bf16[192,384]{1,0:T(8,128)(2,1)} %wk_ref.3), custom_call_target="tpu_custom_call" | custom-call | tf_op jit(solution)/shard_map/fold_key/pallas_call | solution.py:392
  56.3 3.4 %all-to-all-start.2 = ((f32[8,8,256]{2,1,0:T(8,128)}), f32[8,8,256]{2,1,0:T(8,128)S(1)}, u32[]{:S(2)}, u32[]{:S(2)}) async-start(f32[8,8,256]{2,1,0:T(8,128)} %fold_key.1), calls=%async_computation.2 | async-start | bytes 131072 | tf_op jit(solution)/shard_map/all_to_all | solution.py:400
  59.6 0.6 reshape.72.scale_ref
  60.2 0.5 pad.15
  60.8 5.8 %all-to-all-done.2.fold_ref = f32[8,8,256]{2,1,0:T(8,128)S(1)} async-done(((f32[8,8,256]{2,1,0:T(8,128)}), f32[8,8,256]{2,1,0:T(8,128)S(1)}, u32[]{:S(2)}, u32[]{:S(2)}) %all-to-all-start.2) | async-done | bytes 65568 | tf_op jit(solution)/shard_map/all_to_all | solution.py:400
  66.6 0.6 copy-done.1
  67.2 4.5 %tile_attention.1 = f32[32,1792]{1,0:T(8,128)} custom-call(bf16[1,257,1536]{2,1,0:T(8,128)(2,1)} %patch_ref.3, f32[1,1536]{1,0:T(1,128)} %reshape.68.gain_ref, f32[8,8,256]{2,1,0:T(8,128)} %copy-done.1, bf16[1536,384]{1,0:T(8,128)(2,1)} %all-gather.7.cloned.1.call-done.wv_ref, bf16[384,1536]{1,0:T(8,128)(2,1)} %wo_ref.1, f32[1,1536]{1,0:T(1,128)} %reshape.72.scale_ref, ...), custom_call_target="tpu_custom_call" | custom-call | tf_op jit(solution)/shard_map/tile_attention/pallas_call | solution.py:403
  71.7 1.9 %copy.47 = f32[32,1,1792]{2,1,0:T(1,128)} copy(f32[32,1,1792]{2,0,1:T(8,128)} %bitcast.28) | data formatting | bytes 458752 | tf_op jit(solution)/shard_map/all_to_all | solution.py:414
  73.6 2.8 %all-to-all-start.3 = ((f32[32,1,1792]{2,1,0:T(1,128)}), f32[32,1,1792]{2,1,0:T(1,128)S(1)}, u32[]{:S(2)}, u32[]{:S(2)}) async-start(f32[32,1,1792]{2,1,0:T(1,128)} %copy.47), calls=%async_computation.3 | async-start | bytes 458752 | tf_op jit(solution)/shard_map/all_to_all | solution.py:414
  76.4 0.6 reshape.74.final_ref
  77.0 0.5 pad_bitcast_fusion.2
  77.5 0.7 copy.58.pos_ref
  78.3 0.5 pad_bitcast_fusion
  78.8 0.7 copy.59.flag_ref
  79.5 6.5 %all-to-all-done.3 = f32[32,1,1792]{2,1,0:T(1,128)S(1)} async-done(((f32[32,1,1792]{2,1,0:T(1,128)}), f32[32,1,1792]{2,1,0:T(1,128)S(1)}, u32[]{:S(2)}, u32[]{:S(2)}) %all-to-all-start.3) | async-done | bytes 229408 | tf_op jit(solution)/shard_map/all_to_all | solution.py:414
  86.0 0.7 copy.64
  86.7 13.7 %all-gather.9.cloned.1.call-done.kv_ref = bf16[2048,384]{1,0:T(8,128)(2,1)} async-done(((bf16[256,384]{1,0:T(8,128)(2,1)}), bf16[2048,384]{1,0:T(8,128)(2,1)}) %all-gather.9.cloned.1.call-update) | async-done | bytes 1572880 | tf_op jit(solution)/shard_map/all_gather | solution.py:320
  100.5 6.2 %base_attention.1 = (f32[256,128]{1,0:T(8,128)}, f32[256,256]{1,0:T(8,128)}) custom-call(bf16[256,256]{1,0:T(8,128)(2,1)} %get-tuple-element.27.q_ref, bf16[2048,384]{1,0:T(8,128)(2,1)} %all-gather.9.cloned.1.call-done.kv_ref, s32[16,1]{1,0:T(8,128)} %copy.58.pos_ref, f32[16,1]{1,0:T(8,128)} %copy.59.flag_ref, s32[5,12]{1,0:T(8,128)} %offset_ref.3, ...), custom_call_target="tpu_custom_call" | custom-call | tf_op jit(solution)/shard_map/base_attention/pallas_call | solution.py:419
  106.7 17.7 %all-gather.11.cloned.1.call-done = bf16[6144,192]{0,1:T(8,128)(2,1)} async-done(((bf16[1536,192]{0,1:T(8,128)(2,1)}), bf16[6144,192]{0,1:T(8,128)(2,1)}) %all-gather.11.cloned.1.call-update) | async-done | bytes 2359312 | tf_op jit(solution)/shard_map/all_gather | solution.py:369
  124.3 4.5 %copy.48 = bf16[6144,192]{1,0:T(8,128)(2,1)} copy(bf16[6144,192]{0,1:T(8,128)(2,1)} %all-gather.11.cloned.1.call-done) | data formatting | bytes 4718592 | tf_op jit(solution)/shard_map/all_gather | solution.py:369
  128.8 8.9 %fresh_attention.1 = (bf16[64,256]{1,0:T(8,128)(2,1)}, bf16[64,256]{1,0:T(8,128)(2,1)}, bf16[64,256]{1,0:T(8,128)(2,1)}, bf16[64,256]{1,0:T(8,128)(2,1)}, f32[64,768]{1,0:T(8,128)}) custom-call(f32[32,1792]{1,0:T(8,128)} %bitcast.27, f32[1,1536]{1,0:T(1,128)} %reshape.74.final_ref, bf16[4,1536,192]{2,1,0:T(8,128)(2,1)} %bitcast.25, ...), custom_call_target="tpu_custom_call" | custom-call | tf_op jit(solution)/shard_map/fresh_attention/pallas_call | solution.py:430
  138.0 0.3 collective-permute-start.1
  138.3 1.4 collective-permute-start.2
  139.6 4.3 %all-gather.13.cloned.1.call-done = bf16[768,768]{1,0:T(8,128)(2,1)} async-done(((bf16[192,768]{1,0:T(8,128)(2,1)}), bf16[768,768]{1,0:T(8,128)(2,1)}) %all-gather.13.cloned.1.call-update) | async-done | bytes 1179664 | tf_op jit(solution)/shard_map/all_gather | solution.py:370
  144.0 0.6 copy-done.3
  144.6 2.4 %slide_next.1 = bf16[64,768]{1,0:T(8,128)(2,1)} custom-call(bf16[64,256]{1,0:T(8,128)(2,1)} %get-tuple-element.32.a0_ref, bf16[64,256]{1,0:T(8,128)(2,1)} %copy-done.3, bf16[64,256]{1,0:T(8,128)(2,1)} %copy-done.4, bf16[64,256]{1,0:T(8,128)(2,1)} %copy-done.5, bf16[4,192,768]{2,1,0:T(8,128)(2,1)} %bitcast.26, f32[64,768]{1,0:T(8,128)} %get-tuple-element.36.mine_ref, ...), custom_call_target="tpu_custom_call" | custom-call | tf_op jit(solution)/shard_map/slide_next/pallas_call | solution.py:452
  (37 shorter events, 0.6 us)
Async XLA Ops:
  6.5 7.3 %copy-start = (bf16[768,192]{0,1:T(8,128)(2,1)S(1)}, bf16[768,192]{0,1:T(8,128)(2,1)}, u32[]{:S(2)}) copy-start(bf16[768,192]{0,1:T(8,128)(2,1)} %param.39) | copy-start | bytes 884740
  6.5 8.3 %copy-start.9 = (f32[768]{0:T(1024)S(1)}, f32[768]{0:T(1024)}, u32[]{:S(2)}) copy-start(f32[768]{0:T(1024)} %param.35) | copy-start | bytes 9220
  6.5 60.0 %all-gather.7.cloned.1.call-start = ((), (), s32[]{:S(2)}) async-start(), calls=%async_computation.4 | async-start | bytes 1327104 | tf_op jit(solution)/shard_map/all_gather | solution.py:320
  7.3 93.2 %all-gather.9.cloned.1.call-start = ((), (), s32[]{:S(2)}) async-start(), calls=%async_computation.5 | async-start | bytes 1769472 | tf_op jit(solution)/shard_map/all_gather | solution.py:320
  14.8 4.9 %copy-start.6 = (f32[1536]{0:T(1024)S(1)}, f32[1536]{0:T(1024)}, u32[]{:S(2)}) copy-start(f32[1536]{0:T(1024)} %param.23) | copy-start | bytes 18436
  14.8 6.8 %copy-start.12 = (s32[8]{0:T(128)S(1)}, s32[8]{0:T(128)}, u32[]{:S(2)}) copy-start(s32[8]{0:T(128)} %param.32) | copy-start | bytes 100
  18.4 41.2 %copy-start.7 = (f32[1536]{0:T(1024)S(1)}, f32[1536]{0:T(1024)}, u32[]{:S(2)}) copy-start(f32[1536]{0:T(1024)} %param.28) | copy-start | bytes 18436
  18.4 41.8 %copy-start.10 = (f32[192]{0:T(256)S(1)}, f32[192]{0:T(256)}, u32[]{:S(2)}) copy-start(f32[192]{0:T(256)} %param.31) | copy-start | bytes 2308
  18.4 105.9 %all-gather.11.cloned.1.call-start = ((), (), s32[]{:S(2)}) async-start(), calls=%async_computation.6 | async-start | bytes 2949120 | tf_op jit(solution)/shard_map/all_gather | solution.py:369
  19.2 124.8 %all-gather.13.cloned.1.call-start = ((), (), s32[]{:S(2)}) async-start(), calls=%async_computation.7 | async-start | bytes 1474560 | tf_op jit(solution)/shard_map/all_gather | solution.py:370
  23.2 0.6 copy-start.11
  56.3 10.3 %all-to-all-start.2 = ((f32[8,8,256]{2,1,0:T(8,128)}), f32[8,8,256]{2,1,0:T(8,128)S(1)}, u32[]{:S(2)}, u32[]{:S(2)}) async-start(f32[8,8,256]{2,1,0:T(8,128)} %fold_key.1), calls=%async_computation.2 | async-start | bytes 131072 | tf_op jit(solution)/shard_map/all_to_all | solution.py:400
  66.6 0.6 copy-start.1
  67.2 9.2 %copy-start.8 = (f32[1536]{0:T(1024)S(1)}, f32[1536]{0:T(1024)}, u32[]{:S(2)}) copy-start(f32[1536]{0:T(1024)} %param.29) | copy-start | bytes 18436
  67.2 11.0 %copy-start.2 = (f32[8,1,256]{2,0,1:T(8,128)S(1)}, f32[8,1,256]{2,0,1:T(8,128)}, u32[]{:S(2)}) copy-start(f32[8,1,256]{2,0,1:T(8,128)} %copy.65) | copy-start | bytes 24580
  73.6 12.4 %all-to-all-start.3 = ((f32[32,1,1792]{2,1,0:T(1,128)}), f32[32,1,1792]{2,1,0:T(1,128)S(1)}, u32[]{:S(2)}, u32[]{:S(2)}) async-start(f32[32,1,1792]{2,1,0:T(1,128)} %copy.47), calls=%async_computation.3 | async-start | bytes 458752 | tf_op jit(solution)/shard_map/all_to_all | solution.py:414
  137.7 6.2 %collective-permute-start = (bf16[64,256]{1,0:T(8,128)(2,1)}, bf16[64,256]{1,0:T(8,128)(2,1)S(1)}, u32[]{:S(2)}, u32[]{:S(2)}) collective-permute-start(bf16[64,256]{1,0:T(8,128)(2,1)} %get-tuple-element.33), channel_id=1, source_target_pairs={{0,1},{1,0},{2,3},{3,2},{4,5},{5,4},{6,7},{7,6},{8,9},{9,8},{10,11... | collective-permute-start | bytes 98312 | tf_op jit(solution)/shard_map/ppermute | solution.py:316
  138.0 6.0 %collective-permute-start.1 = (bf16[64,256]{1,0:T(8,128)(2,1)}, bf16[64,256]{1,0:T(8,128)(2,1)S(1)}, u32[]{:S(2)}, u32[]{:S(2)}) collective-permute-start(bf16[64,256]{1,0:T(8,128)(2,1)} %get-tuple-element.34), channel_id=1, source_target_pairs={{0,2},{1,3},{2,0},{3,1},{4,6},{5,7},{6,4},{7,5},{8,10},{9,11},{10,... | collective-permute-start | bytes 98312 | tf_op jit(solution)/shard_map/ppermute | solution.py:316
  138.3 5.7 %collective-permute-start.2 = (bf16[64,256]{1,0:T(8,128)(2,1)}, bf16[64,256]{1,0:T(8,128)(2,1)S(1)}, u32[]{:S(2)}, u32[]{:S(2)}) collective-permute-start(bf16[64,256]{1,0:T(8,128)(2,1)} %get-tuple-element.35), channel_id=1, source_target_pairs={{0,3},{1,2},{2,1},{3,0},{4,7},{5,6},{6,5},{7,4},{8,11},{9,10},{10,... | collective-permute-start | bytes 98312 | tf_op jit(solution)/shard_map/ppermute | solution.py:316
  144.0 0.6 copy-start.3
  144.0 0.6 copy-start.4
  144.0 0.6 copy-start.5
Sparse Core Ops, SparseCore 0:
  9.5 45.0 all-gather.6
  56.8 43.5 all-gather.8
  102.0 22.2 all-gather.10
  125.8 18.1 all-gather.12

commit v2 on v1

v2 whole, which is shorter than its diff:
```python
import functools
import math

import jax
import jax.numpy as jnp
from jax import lax
from jax.experimental import pallas as pl
from jax.experimental.pallas import tpu as pltpu
from jax.sharding import PartitionSpec as P

DV = 1536
HV = 24
DS = 768
HS = 12
HEAD = 64

EPS = 1e-06
LOW = -1e30
F32 = jnp.float32
BF16 = jnp.bfloat16
I32 = jnp.int32
VMEM = pl.BlockSpec(memory_space=pltpu.VMEM)
SMEM = pl.BlockSpec(memory_space=pltpu.SMEM)
NT = (((1,), (1,)), ((), ()))
ROOM = 56 * 1024 * 1024


def params():
    return pltpu.CompilerParams(vmem_limit_bytes=ROOM)


def round_up(value, unit):
    return -(-value // unit) * unit


def layer_norm(values, scaling):
    center = values - jnp.mean(values, axis=-1, keepdims=True)
    spread = jnp.mean(center * center, axis=-1, keepdims=True)
    return center * lax.rsqrt(spread + EPS) * scaling


def dot(a, b):
    return jnp.dot(a, b, preferred_element_type=F32)


def dot_nt(a, b):
    return lax.dot_general(a, b, NT, preferred_element_type=F32)


def class_kernel(fresh, patch_ref, gain_ref, pos_ref, kept_ref, pack_ref):
    parts, _, width = pack_ref.shape
    cut = DV // parts
    rows = kept_ref.shape[0]
    row = patch_ref[0, 0:1].astype(F32)
    normed = layer_norm(row, gain_ref[...].reshape(1, DV)).astype(BF16).astype(F32)
    place = lax.broadcasted_iota(I32, (1, rows), 1) + lax.axis_index("tile") * rows
    kept = kept_ref[...].reshape(1, rows) != 0
    lane = lax.broadcasted_iota(I32, (1, width), 1)
    flags = jnp.zeros((1, width), F32)
    for index in range(fresh):
        hit = jnp.where((place == pos_ref[index]) & kept, 1.0, 0.0)
        flags = jnp.where(lane == index, jnp.max(hit, axis=1, keepdims=True), flags)
    for part in range(parts):
        pack_ref[part] = jnp.broadcast_to(flags, pack_ref.shape[1:])
        pack_ref[part, 0:1, 0:cut] = normed[:, part * cut : (part + 1) * cut]


def column(row, rows):
    width = row.shape[1]
    same = lax.broadcasted_iota(I32, (rows, width), 0) == lax.broadcasted_iota(
        I32, (rows, width), 1
    )
    return jnp.sum(jnp.where(same, row, 0.0), axis=1, keepdims=True)


def base_kernel(
    cached_ref, kept_ref, mask_ref, gain_ref, wq_ref, wk_ref, wv_ref, rows_ref, q_ref, kv_ref
):
    span = kept_ref.shape[0]
    kept = column(jnp.where(kept_ref[...].reshape(1, span) != 0, 1.0, 0.0), span)
    mask_row = mask_ref[...].reshape(1, DS).astype(BF16).astype(F32)
    rows = jnp.where(kept < 0.5, mask_row, cached_ref[...].astype(F32))
    rows_ref[...] = rows.astype(BF16)
    normed = layer_norm(rows, gain_ref[...].reshape(1, DS)).astype(BF16)
    project(normed, wq_ref, wk_ref, wv_ref, q_ref, kv_ref)


def project(normed, wq_ref, wk_ref, wv_ref, q_ref, kv_ref):
    q = dot_nt(normed, wq_ref[...]).astype(BF16) * BF16(1.0 / math.sqrt(HEAD))
    k = dot_nt(normed, wk_ref[...]).astype(BF16)
    v = dot_nt(normed, wv_ref[...]).astype(BF16)
    q_ref[:, 0:192] = q
    q_ref[:, 192:256] = jnp.zeros((q.shape[0], 64), BF16)
    kv_ref[:, 0:192] = k
    kv_ref[:, 192:256] = v[:, 128:192]
    kv_ref[:, 256:384] = v[:, 0:128]


def query_kernel(cut, pack_ref, wq_ref, part_ref):
    rows = pack_ref[:, 0, 0:cut].astype(BF16)
    part = dot(rows, wq_ref[...])
    if len(part_ref.shape) == 3:
        part_ref[...] = jnp.broadcast_to(part[None], part_ref.shape)
    else:
        part_ref[...] = part


def fold_kernel(part_ref, wk_ref, fold_ref):
    if len(part_ref.shape) == 3:
        queries = part_ref[0]
        for index in range(1, part_ref.shape[0]):
            queries = queries + part_ref[index]
    else:
        queries = part_ref[...]
    tiles, width = queries.shape
    queries = queries.astype(BF16).astype(F32)
    spread = jnp.broadcast_to(queries[:, None], (tiles, 8, width))
    head = lax.broadcasted_iota(I32, spread.shape, 1)
    lane = lax.broadcasted_iota(I32, spread.shape, 2)
    spread = jnp.where(lane // HEAD == head, spread, 0.0).reshape(tiles * 8, width).astype(BF16)
    cut = wk_ref.shape[0]
    result = dot_nt(spread, wk_ref[...]).reshape(tiles, 8, cut)
    fold_ref[:, :, 0:cut] = result
    if cut < fold_ref.shape[2]:
        fold_ref[:, :, cut:] = jnp.zeros((tiles, 8, fold_ref.shape[2] - cut), F32)


def tile_kernel(cut, patch_ref, gain_ref, fold_ref, scale_ref, bias_ref, wo_ref, *refs):
    *wv_refs, sent_ref, fold_s, mixed_s = refs
    parts = fold_ref.shape[0]
    for part in range(parts):
        fold_s[:, part * cut : (part + 1) * cut] = fold_ref[part, :, 0:cut]
    tokens = patch_ref[0].astype(F32)
    normed = layer_norm(tokens, gain_ref[...].reshape(1, DV)).astype(BF16)
    scores = dot_nt(fold_s[...].astype(BF16), normed) * (1.0 / math.sqrt(HEAD))
    highest = jnp.max(scores, axis=-1, keepdims=True)
    exponent = jnp.exp(scores - highest)
    prob = (exponent / jnp.sum(exponent, axis=-1, keepdims=True)).astype(BF16)
    mixed = dot(prob, normed)
    if len(wv_refs) == 1:
        values = dot(mixed.astype(BF16), wv_refs[0][...])
    else:
        for part in range(parts):
            mixed_s[part, :, 0:cut] = mixed[:, part * cut : (part + 1) * cut]
        values = jnp.zeros((8, wo_ref.shape[0]), F32)
        me = lax.axis_index("tile")
        for low, ref in enumerate(wv_refs):
            for high in range(parts // 2):
                piece = mixed_s[me ^ (2 * high + low)][:, 0:cut].astype(BF16)
                values = values + dot(piece, ref[high * cut : (high + 1) * cut])
    head = lax.broadcasted_iota(I32, values.shape, 0)
    lane = lax.broadcasted_iota(I32, values.shape, 1)
    tmix = jnp.sum(jnp.where(lane // HEAD == head, values, 0.0), axis=0, keepdims=True)
    tmix = jnp.broadcast_to(tmix, (8, tmix.shape[1])).astype(BF16)
    share = dot(tmix, wo_ref[...])[0:1] * scale_ref[...].reshape(1, DV)
    share = share + jnp.where(lax.axis_index("seg") == 0, tokens[0:1], 0.0)
    devices = sent_ref.shape[0]
    for row in range(DV // 256):
        piece = share[:, None, row * 256 : (row + 1) * 256]
        sent_ref[:, row : row + 1, :] = jnp.broadcast_to(piece, (devices, 1, 256))
    width = bias_ref.shape[0]
    bias = bias_ref[...].reshape(1, 1, width)
    sent_ref[:, 6:8, :] = jnp.zeros((devices, 2, 256), F32)
    sent_ref[:, 6:7, 0:width] = jnp.broadcast_to(bias, (devices, 1, width))


def branch_rows(position, axis, offset_ref, head, span, total):
    shape = (1, 8) if axis == 1 else (8, 1)
    branch = lax.broadcasted_iota(I32, shape, axis)
    residue = jnp.full(shape, -1, I32)
    shift = jnp.zeros(shape, I32)
    for b in range(offset_ref.shape[0]):
        residue = jnp.where(branch == b, offset_ref[b, lax.axis_index("seg") * 3 + head], residue)
        length = min(2 * span * 4**b, total)
        shift = jnp.where(branch == b, length.bit_length() - 1, shift)
    below = jnp.left_shift(jnp.int32(1), branch) - 1
    mine = jnp.right_shift(jnp.zeros(shape, I32) + lax.axis_index("tile") * span, shift)
    return ((position & below) == residue) & (jnp.right_shift(position, shift) == mine)


def value_lanes(head):
    group = {0: 2, 1: 3, 2: 1}[head]
    lane = lax.broadcasted_iota(I32, (1, 256), 1)
    return lane // HEAD == group


def attend(q, q_rows, kv_ref, k_rows, head):
    lane = lax.broadcasted_iota(I32, (1, 256), 1)
    q_head = jnp.where(lane // HEAD == head, q, jnp.zeros_like(q))
    scores = dot_nt(q_head, kv_ref[:, 0:256])
    count = dot(q_rows, k_rows)
    scores = jnp.where(count > 0.5, scores, LOW)
    highest = jnp.max(scores, axis=-1, keepdims=True)
    weight = jnp.exp(scores - highest) * count
    denom = jnp.sum(weight, axis=-1, keepdims=True)
    numer = dot(weight.astype(BF16), kv_ref[:, 128:384])
    return highest, denom, numer


def as_bf16(condition):
    return jnp.where(condition, 1.0, 0.0).astype(BF16)


def merge(old, new):
    old_max, old_den, old_num = old
    new_max, new_den, new_num = new
    top = jnp.maximum(old_max, new_max)
    keep = jnp.exp(old_max - top)
    take = jnp.exp(new_max - top)
    return top, old_den * keep + new_den * take, old_num * keep + new_num * take


def store_state(state, head, ml_ref, acc_ref):
    highest, denom, numer = state
    lane = lax.broadcasted_iota(I32, (1, 128), 1)
    ml = jnp.where(lane == head, highest, ml_ref[...])
    ml_ref[...] = jnp.where(lane == head + 8, denom, ml)
    acc_ref[...] = jnp.where(value_lanes(head), numer, acc_ref[...])


def load_state(head, ml_ref, acc_ref):
    return ml_ref[:, head : head + 1], ml_ref[:, head + 8 : head + 9], acc_ref[...]


def fresh_places(padded, pack_ref, pos_ref):
    flags = pack_ref[0, 1:2, :]
    for part in range(1, pack_ref.shape[0]):
        flags = flags + pack_ref[part, 1:2, :]
    flag_col = column(flags, padded)
    lane = lax.broadcasted_iota(I32, (1, padded), 1)
    sub = lax.broadcasted_iota(I32, (padded, 1), 0)
    row = jnp.full((1, padded), -1, I32)
    col = jnp.full((padded, 1), -1, I32)
    for index in range(pos_ref.shape[0]):
        row = jnp.where(lane == index, pos_ref[index], row)
        col = jnp.where(sub == index, pos_ref[index], col)
    return row, col, flags[:, 0:padded] > 0.5, flag_col > 0.5


def key_places(swapped, low, block, span, step):
    place = lax.broadcasted_iota(I32, (1, block), 1)
    if not swapped:
        return place + step * block
    source = lax.axis_index("tile") ^ (2 * (place // span) + low)
    return source * span + (place & (span - 1))


def key_rows(place, pos_col, flag_col, offset_ref, head, span, total):
    rows = branch_rows(place, 0, offset_ref, head, span, total)
    taken = jnp.where((place == pos_col) & flag_col, 1.0, 0.0)
    taken = jnp.max(taken, axis=0, keepdims=True)
    return as_bf16(rows & (taken < 0.5))


def base_attention_kernel(span, total, padded, pos_ref, offset_ref, pack_ref, q_ref, *refs):
    *kv_refs, ml_ref, acc_ref = refs
    step = pl.program_id(0)
    rows = q_ref.shape[0]

    @pl.when(step == 0)
    def _():
        lane = lax.broadcasted_iota(I32, (rows, 128), 1)
        ml_ref[...] = jnp.where(lane < 8, LOW, 0.0)
        acc_ref[...] = jnp.zeros_like(acc_ref)

    _, pos_col, _, flag_col = fresh_places(padded, pack_ref, pos_ref)
    place = lax.broadcasted_iota(I32, (rows, 1), 0) + lax.axis_index("tile") * span
    for head in range(3):
        q_rows = as_bf16(branch_rows(place, 1, offset_ref, head, span, total))
        for low, kv_ref in enumerate(kv_refs):
            keys = key_places(len(kv_refs) > 1, low, kv_ref.shape[0], span, step)
            k_rows = key_rows(keys, pos_col, flag_col, offset_ref, head, span, total)
            new = attend(q_ref[...], q_rows, kv_ref, k_rows, head)
            store_state(merge(load_state(head, ml_ref, acc_ref), new), head, ml_ref, acc_ref)


def fresh_kernel(
    span, total, parts, pos_ref, offset_ref, pack_ref, q_ref, shares_ref, final_ref, gain_ref,
    wq_ref, wk_ref, wv_ref, ml_ref, acc_ref, rows_ref, *refs,
):
    embed_refs, refs = refs[:4], refs[4:]
    kv_refs, refs = refs[:parts], refs[parts:]
    outs, refs = refs[:4], refs[4:]
    mine_ref, fresh_s, qf_s, kvf_s, mlf_s, accf_s, att_s = refs
    step = pl.program_id(0)
    rows = q_ref.shape[0]
    padded = fresh_s.shape[0]
    seg = lax.axis_index("seg")
    pos_row, pos_col, flag_row, flag_col = fresh_places(padded, pack_ref, pos_ref)

    @pl.when(step == 0)
    def _():
        groups = shares_ref.shape[0] // 4
        pooled = []
        for row in range(DV // 256):
            pooled.append(jnp.sum(shares_ref[:, row, :].reshape(groups, 4, 256), axis=1))
        pooled = jnp.concatenate(pooled, axis=1)
        summary = layer_norm(pooled, final_ref[...].reshape(1, DV)).astype(BF16)
        fresh_s[...] = jnp.zeros_like(fresh_s)
        pieces = [dot_nt(summary, ref[...]) for ref in embed_refs]
        for part in range(4):
            piece = pieces[0]
            for mask in range(1, 4):
                piece = jnp.where((seg ^ part) == mask, pieces[mask], piece)
            piece = piece + shares_ref[part, 6:7, 0:192]
            fresh_s[0:groups, part * 192 : (part + 1) * 192] = piece.astype(BF16).astype(F32)
        normed = layer_norm(fresh_s[...], gain_ref[...].reshape(1, DS)).astype(BF16)
        project(normed, wq_ref, wk_ref, wv_ref, qf_s, kvf_s)
        lane = lax.broadcasted_iota(I32, (padded, 128), 1)
        mlf_s[...] = jnp.where(lane < 8, LOW, 0.0)
        accf_s[...] = jnp.zeros_like(accf_s)

    for head in range(3):
        q_rows = as_bf16(branch_rows(pos_col, 1, offset_ref, head, span, total))
        for low, kv_ref in enumerate(kv_refs):
            keys = key_places(parts > 1, low, kv_ref.shape[0], span, step)
            k_rows = key_rows(keys, pos_col, flag_col, offset_ref, head, span, total)
            new = attend(qf_s[...], q_rows, kv_ref, k_rows, head)
            store_state(merge(load_state(head, mlf_s, accf_s), new), head, mlf_s, accf_s)

    @pl.when(step == pl.num_programs(0) - 1)
    def _():
        first = lax.axis_index("tile") * span
        place = lax.broadcasted_iota(I32, (rows, 1), 0) + first
        base = jnp.zeros((rows, 256), F32)
        fresh = jnp.zeros((padded, 256), F32)
        for head in range(3):
            q_rows = as_bf16(branch_rows(place, 1, offset_ref, head, span, total))
            f_rows = as_bf16(branch_rows(pos_col, 1, offset_ref, head, span, total))
            k_rows = as_bf16(branch_rows(pos_row, 0, offset_ref, head, span, total) & flag_row)
            lanes = value_lanes(head)
            new = attend(q_ref[...], q_rows, kvf_s, k_rows, head)
            top, den, num = merge(load_state(head, ml_ref, acc_ref), new)
            base = jnp.where(lanes, num / den, base)
            new = attend(qf_s[...], f_rows, kvf_s, k_rows, head)
            top, den, num = merge(load_state(head, mlf_s, accf_s), new)
            fresh = jnp.where(lanes, num / jnp.where(den > 0.0, den, 1.0), fresh)
        chosen = as_bf16((place == pos_row) & flag_row)
        hit = jnp.sum(chosen.astype(F32), axis=1, keepdims=True) > 0.5
        att_s[...] = jnp.where(hit, dot(chosen, fresh.astype(BF16)), base)
        count = rows // 4
        for mask in range(4):
            start = pl.multiple_of((seg ^ mask) * count, count)
            outs[mask][...] = att_s[pl.ds(start, count), :].astype(BF16)
        start = pl.multiple_of(seg * count, count)
        place = lax.broadcasted_iota(I32, (count, 1), 0) + first + start
        chosen = as_bf16((place == pos_row) & flag_row)
        hit = jnp.sum(chosen.astype(F32), axis=1, keepdims=True) > 0.5
        placed = dot(chosen, fresh_s[...].astype(BF16))
        old = rows_ref[pl.ds(start, count), :].astype(F32)
        mine_ref[...] = jnp.where(hit, placed, old)


def out_kernel(mine_ref, *refs):
    out_ref = refs[8]
    total = mine_ref[...]
    for mask in range(4):
        att, weight = refs[mask][...], refs[4 + mask]
        total = total + dot(att[:, 128:256], weight[0:128])
        total = total + dot(att[:, 64:128], weight[128:192])
    out_ref[...] = total.astype(BF16)


def trade(block, axis, mask):
    count = lax.axis_size(axis)
    return lax.ppermute(block, axis, [(i, i ^ mask) for i in range(count)])


def gather_tile(block):
    count = lax.axis_size("tile")
    if count > 8:
        return [lax.all_gather(block, "tile", axis=0, tiled=True)]
    parts = [block] + [trade(block, "tile", mask) for mask in range(2, count, 2)]
    even = jnp.concatenate(parts, axis=0)
    return [even, trade(even, "tile", 1)]


def gather_seg(block):
    return [block] + [trade(block, "seg", mask) for mask in range(1, 4)]


def shards(
    patches, vit_norm_gain, vit_query, vit_key, vit_value, vit_out, layer_scale, final_gain,
    embed_proj, embed_bias, slide_pos, cached, kept, mask_token, slide_gain, slide_query,
    slide_key, slide_value, slide_out, offsets,
):
    tiles = lax.axis_size("tile")
    segs = lax.axis_size("seg")
    devices = tiles * segs
    span = cached.shape[0]
    total = span * tiles
    cut, local_cols = vit_query.shape
    fresh = slide_pos.shape[0]
    padded = max(16, fresh)
    call = pl.pallas_call
    sds = jax.ShapeDtypeStruct
    weights = (slide_query.T, slide_key.T, slide_value.T)

    pack = call(
        functools.partial(class_kernel, fresh),
        out_shape=sds((tiles, 8, 256), F32),
        grid=(1,),
        in_specs=[pl.BlockSpec((1, 16, DV), lambda i: (0, 0, 0)), VMEM, SMEM, VMEM],
        out_specs=VMEM,
        compiler_params=params(),
        name="class_row",
    )(patches, vit_norm_gain, slide_pos, kept)
    pack = lax.all_to_all(pack, "tile", 0, 0, tiled=True)

    base_rows, q_base, kv_base = call(
        base_kernel,
        out_shape=(sds((span, DS), BF16), sds((span, 256), BF16), sds((span, 384), BF16)),
        in_specs=[VMEM] * 7,
        out_specs=(VMEM,) * 3,
        compiler_params=params(),
        name="base_rows",
    )(cached, kept, mask_token, slide_gain, *weights)
    wv_all = gather_tile(vit_value)
    kv_all = gather_tile(kv_base)
    embed_all = gather_seg(embed_proj.T)
    slide_out_all = gather_seg(slide_out)

    small = tiles <= 8
    part_shape = (tiles, fresh, local_cols) if small else (fresh, local_cols)
    part = call(
        functools.partial(query_kernel, cut),
        out_shape=sds(part_shape, F32),
        in_specs=[VMEM] * 2,
        out_specs=VMEM,
        compiler_params=params(),
        name="query_share",
    )(pack, vit_query)
    if small:
        part = lax.all_to_all(part, "tile", 0, 0, tiled=True)
    else:
        part = lax.psum(part, "tile")
    folded = call(
        fold_kernel,
        out_shape=sds((fresh, 8, round_up(cut, 128)), F32),
        in_specs=[VMEM] * 2,
        out_specs=VMEM,
        compiler_params=params(),
        name="fold_key",
    )(part, vit_key)
    folded = lax.all_to_all(folded, "tile", 0, 0, tiled=True)

    sent = call(
        functools.partial(tile_kernel, cut),
        out_shape=sds((devices, 8, 256), F32),
        in_specs=[VMEM] * (6 + len(wv_all)),
        out_specs=VMEM,
        scratch_shapes=[
            pltpu.VMEM((8, DV), F32), pltpu.VMEM((tiles, 8, round_up(cut, 128)), F32),
        ],
        compiler_params=params(),
        name="tile_attention",
    )(patches, vit_norm_gain, folded, layer_scale, embed_bias, vit_out, *wv_all)
    shares = lax.all_to_all(sent, ("tile", "seg"), 0, 0, tiled=True)

    parts = len(kv_all)
    block = min(kv_all[0].shape[0], 2048)
    steps = kv_all[0].shape[0] // block
    kv_specs = [pl.BlockSpec((block, 384), lambda i: (i, 0))] * parts
    ml, acc = call(
        functools.partial(base_attention_kernel, span, total, padded),
        out_shape=(sds((span, 128), F32), sds((span, 256), F32)),
        grid=(steps,),
        in_specs=[SMEM, SMEM, VMEM, VMEM] + kv_specs,
        out_specs=(VMEM, VMEM),
        compiler_params=params(),
        name="base_attention",
    )(slide_pos, offsets, pack, q_base, *kv_all)

    count = span // segs
    outs = call(
        functools.partial(fresh_kernel, span, total, parts),
        out_shape=(sds((count, 256), BF16),) * 4 + (sds((count, DS), F32),),
        grid=(steps,),
        in_specs=[SMEM] * 2 + [VMEM] * 15 + kv_specs,
        out_specs=(VMEM,) * 5,
        scratch_shapes=[
            pltpu.VMEM((padded, DS), F32),
            pltpu.VMEM((padded, 256), BF16),
            pltpu.VMEM((padded, 384), BF16),
            pltpu.VMEM((padded, 128), F32),
            pltpu.VMEM((padded, 256), F32),
            pltpu.VMEM((span, 256), F32),
        ],
        compiler_params=params(),
        name="fresh_attention",
    )(
        slide_pos, offsets, pack, q_base, shares, final_gain, slide_gain, *weights, ml, acc,
        base_rows, *embed_all, *kv_all,
    )
    swapped = [outs[0]] + [trade(outs[mask], "seg", mask) for mask in range(1, 4)]
    return call(
        out_kernel,
        out_shape=sds((count, DS), BF16),
        in_specs=[VMEM] * 9,
        out_specs=VMEM,
        compiler_params=params(),
        name="slide_next",
    )(outs[4], *swapped, *slide_out_all)


def solution(mesh):
    return jax.shard_map(
        shards,
        mesh=mesh,
        in_specs=(
            P("tile", None, None), P(), P("tile", "seg"), P("tile", "seg"), P("tile", "seg"),
            P("seg", None), P(), P(), P(None, "seg"), P("seg"), P(), P("tile", None), P("tile"),
            P(), P(), P(None, "seg"), P(None, "seg"), P(None, "seg"), P("seg", None), P(),
        ),
        out_specs=P(("tile", "seg"), None),
        check_vma=False,
    )
```

time: 154 us -> 134 us (0.87)
  starting transfers between devices: 8.14 us -> 32.5 us
  local copies, waits for them, and re-layouts: 23.9 us -> 4.37 us
  between operations: 13.2 us -> 0.22 us
  blocking collectives: 25.9 us -> 14.1 us
  Pallas kernels: 30.3 us -> 33.2 us
  other arithmetic: 1.97 us -> 0 us
    all_gather x4 -> x0, waiting for transfers between devices: 35.8 us -> none  [the longest x1 17.7 us: shards(): embed_all = lax.all_gather(embed_proj, 'seg', axis=0)]
    ppermute x3 -> x17, waiting for transfers between devices: 0.01 us -> 23.1 us  [trade(): return lax.ppermute(block, axis, [(i, i ^ mask) for i in range(count)])]
    all_to_all x0 -> x1, waiting for transfers between devices: none -> 20.5 us  [shards(): pack = lax.all_to_all(pack, 'tile', 0, 0, tiled=True)]
    ppermute x3 -> x17, starting transfers between devices: 1.91 us -> 20.9 us  [trade(): return lax.ppermute(block, axis, [(i, i ^ mask) for i in range(count)])]
    all_to_all x1 -> x0, blocking collectives: 13.6 us -> none  [shards(): pack = lax.all_to_all(pack, 'tile', 0, 0, tiled=True)]
    reshape x9 -> x0, local copies, waits for them, and re-layouts: 6.83 us -> none  [the longest x1 1.47 us: shards(): kept_col = kept.reshape(span, 1)]
    all_to_all x1, waiting for transfers between devices: 6.54 us -> 0.06 us  [shards(): shares = lax.all_to_all(sent, ('tile', 'seg'), 0, 0, tiled=True)]
    all_to_all x0 -> x1, starting transfers between devices: none -> 5.49 us  [shards(): pack = lax.all_to_all(pack, 'tile', 0, 0, tiled=True)]
  transfers between devices with their start and end apart: 9 -> 20, of which waited for: 5 -> 7; matrix products, arithmetic and copies ran while one was open for 16% -> 1% of each run, Pallas kernels for 18% -> 21%
where the time goes in v2:
time: 134 us; the launch traced here: 133 us
  waiting for transfers between devices  48.9 us (36%)
  Pallas kernels  33.2 us (25%)
  starting transfers between devices  32.5 us (24%)
  blocking collectives  14.1 us (11%)
  local copies, waits for them, and re-layouts  4.37 us (3%)
    ppermute x17, waiting for transfers between devices, trade(): return lax.ppermute(block, axis, [(i, i ^ mask) for i in range(count)])  23.1 us
    ppermute x17, starting transfers between devices, trade(): return lax.ppermute(block, axis, [(i, i ^ mask) for i in range(count)])  20.9 us
    all_to_all x1, waiting for transfers between devices, shards(): pack = lax.all_to_all(pack, 'tile', 0, 0, tiled=True)  20.5 us
    all_to_all x1, blocking collectives, shards(): part = lax.all_to_all(part, 'tile', 0, 0, tiled=True)  14.1 us
    pallas_call x1, Pallas kernels, shards(): call(functools.partial(fresh_kernel, span, total, parts), out_shape=(sds(...  9.97 us
    pallas_call x1, Pallas kernels, shards(): call(functools.partial(base_attention_kernel, span, total, padded), out_s...  7.73 us
    all_to_all x1, starting transfers between devices, shards(): pack = lax.all_to_all(pack, 'tile', 0, 0, tiled=True)  5.49 us
    all_to_all x1, waiting for transfers between devices, shards(): folded = lax.all_to_all(folded, 'tile', 0, 0, tiled=True)  5.21 us
  transfers between devices with their start and end apart: 20, of which 7 were waited for; matrix products, arithmetic and copies ran while one was open for 1% of the time, Pallas kernels for 21%

profile of v2, /device:TPU:0, one launch (start us, length us, event | category | flops | bytes accessed | tf_op | source)
XLA Modules:
  0.0 133.3 jit_solution(15002410268948591079)
XLA Ops:
  0.0 2.9 %base_rows.1 = (bf16[256,768]{1,0:T(8,128)(2,1)}, bf16[256,256]{1,0:T(8,128)(2,1)}, bf16[256,384]{1,0:T(8,128)(2,1)}) custom-call(bf16[256,768]{1,0:T(8,128)(2,1)} %cached_ref.1, s32[256]{0:T(256)} %kept_ref.3, f32[768]{0:T(1024)} %mask_ref.1, f32[768]{0:T(1024)} %gain_ref.7, bf16[192,768]{1,0:T(8,128)(2,1)} %bitcast.4, bf16[192,768]{1,0:T(8,128)(2,1)} %bitcast.6, ...), custom_call_target="tpu_custom_call" | custom-call | tf_op jit(solution)/shard_map/base_rows/pallas_call | solution.py:410
  2.9 3.0 %collective-permute-start.4 = (bf16[256,384]{1,0:T(8,128)(2,1)}, bf16[256,384]{1,0:T(8,128)(2,1)S(1)}, u32[]{:S(2)}, u32[]{:S(2)}) collective-permute-start(bf16[256,384]{1,0:T(8,128)(2,1)} %get-tuple-element.16), channel_id=1, source_target_pairs={{0,8},{4,12},{8,0},{12,4},{16,24},{20,28},{24,16},{28,20},{1,9},{5... | collective-permute-start | bytes 589832 | tf_op jit(solution)/shard_map/ppermute | solution.py:366
  5.9 2.6 %collective-permute-start.5 = (bf16[256,384]{1,0:T(8,128)(2,1)}, bf16[256,384]{1,0:T(8,128)(2,1)S(1)}, u32[]{:S(2)}, u32[]{:S(2)}) collective-permute-start(bf16[256,384]{1,0:T(8,128)(2,1)} %get-tuple-element.16), channel_id=1, source_target_pairs={{0,16},{4,20},{8,24},{12,28},{16,0},{20,4},{24,8},{28,12},{1,17},{... | collective-permute-start | bytes 589832 | tf_op jit(solution)/shard_map/ppermute | solution.py:366
  8.5 0.0 collective-permute-start.6
  8.5 0.9 collective-permute-start
  9.4 3.5 %collective-permute-start.1 = (bf16[192,384]{1,0:T(8,128)(2,1)S(1)}, bf16[192,384]{1,0:T(8,128)(2,1)S(1)}, u32[]{:S(2)}, u32[]{:S(2)}) collective-permute-start(bf16[192,384]{1,0:T(8,128)(2,1)S(1)} %copy-done.10), channel_id=1, source_target_pairs={{0,16},{4,20},{8,24},{12,28},{16,0},{20,4},{24,8},{28,12},{1,17},{... | collective-permute-start | bytes 442376 | tf_op jit(solution)/shard_map/ppermute | solution.py:366
  12.9 0.9 constant_dynamic-update-slice_fusion.7
  13.8 9.2 %collective-permute-done = bf16[192,384]{1,0:T(8,128)(2,1)S(1)} collective-permute-done((bf16[192,384]{1,0:T(8,128)(2,1)S(1)}, bf16[192,384]{1,0:T(8,128)(2,1)S(1)}, u32[]{:S(2)}, u32[]{:S(2)}) %collective-permute-start) | collective-permute-done | bytes 147488 | tf_op jit(solution)/shard_map/ppermute | solution.py:366
  23.1 3.2 %collective-permute-start.2 = (bf16[192,384]{1,0:T(8,128)(2,1)S(1)}, bf16[192,384]{1,0:T(8,128)(2,1)S(1)}, u32[]{:S(2)}, u32[]{:S(2)}) collective-permute-start(bf16[192,384]{1,0:T(8,128)(2,1)S(1)} %copy-done.10), channel_id=1, source_target_pairs={{0,24},{4,28},{8,16},{12,20},{16,8},{20,12},{24,0},{28,4},{1,25},{... | collective-permute-start | bytes 442376 | tf_op jit(solution)/shard_map/ppermute | solution.py:366
  26.3 10.7 %collective-permute-done.1 = bf16[192,384]{1,0:T(8,128)(2,1)S(1)} collective-permute-done((bf16[192,384]{1,0:T(8,128)(2,1)S(1)}, bf16[192,384]{1,0:T(8,128)(2,1)S(1)}, u32[]{:S(2)}, u32[]{:S(2)}) %collective-permute-start.1) | collective-permute-done | bytes 147488 | tf_op jit(solution)/shard_map/ppermute | solution.py:366
  37.0 0.0 copy-start.5
  37.0 0.0 collective-permute-done.2
  37.1 1.6 %collective-permute-start.3 = (bf16[768,384]{1,0:T(8,128)(2,1)S(1)}, bf16[768,384]{1,0:T(8,128)(2,1)}, u32[]{:S(2)}, u32[]{:S(2)}) collective-permute-start(bf16[768,384]{1,0:T(8,128)(2,1)S(1)} %constant_dynamic-update-slice_fusion.refs_0_), channel_id=1, source_target_pairs={{0,4},{4,0},{8,12},{12,8},{16,20},{20,16},{24,28},{28,24},{1,5},{5... | collective-permute-start | bytes 1769480 | tf_op jit(solution)/shard_map/ppermute | solution.py:366
  38.7 0.0 collective-permute-done.4
  38.8 0.6 collective-permute-start.7
  39.4 1.7 %class_row.1 = f32[8,8,256]{2,1,0:T(8,128)} custom-call(bf16[1,257,1536]{2,1,0:T(8,128)(2,1)} %patch_ref.3, f32[1536]{0:T(1024)} %gain_ref.6, s32[8]{0:T(128)} %pos_ref.5, s32[256]{0:T(256)} %kept_ref.3), custom_call_target="tpu_custom_call" | custom-call | tf_op jit(solution)/shard_map/class_row/pallas_call | solution.py:399
  41.1 5.5 %all-to-all-start = ((f32[8,8,256]{2,1,0:T(8,128)}), f32[8,8,256]{2,1,0:T(8,128)S(1)}, u32[]{:S(2)}, u32[]{:S(2)}) async-start(f32[8,8,256]{2,1,0:T(8,128)} %class_row.1), calls=%async_computation | async-start | bytes 131072 | tf_op jit(solution)/shard_map/all_to_all | solution.py:408
  46.6 0.1 collective-permute-start.10
  46.7 20.5 %all-to-all-done.pack_ref = f32[8,8,256]{2,1,0:T(8,128)S(1)} async-done(((f32[8,8,256]{2,1,0:T(8,128)}), f32[8,8,256]{2,1,0:T(8,128)S(1)}, u32[]{:S(2)}, u32[]{:S(2)}) %all-to-all-start) | async-done | bytes 65568 | tf_op jit(solution)/shard_map/all_to_all | solution.py:408
  67.2 0.6 copy-done.2
  67.8 1.7 %query_share.1 = f32[8,8,384]{2,1,0:T(8,128)} custom-call(f32[8,8,256]{2,1,0:T(8,128)} %copy-done.2, bf16[192,384]{1,0:T(8,128)(2,1)} %wq_ref.1), custom_call_target="tpu_custom_call" | custom-call | tf_op jit(solution)/shard_map/query_share/pallas_call | solution.py:425
  69.6 14.1 %all_to_all.20.part_ref = f32[8,8,384]{2,1,0:T(8,128)} all-to-all(f32[8,8,384]{2,1,0:T(8,128)} %query_share.1), channel_id=1, replica_groups=mesh['tile'=8,'seg'=4] {'tile'}, dimensions={0} | all-to-all | bytes 196608 | tf_op jit(solution)/shard_map/all_to_all | solution.py:434
  83.7 1.8 %fold_key.1 = f32[8,8,256]{2,1,0:T(8,128)} custom-call(f32[8,8,384]{2,1,0:T(8,128)} %all_to_all.20.part_ref, bf16[192,384]{1,0:T(8,128)(2,1)} %wk_ref.1), custom_call_target="tpu_custom_call" | custom-call | tf_op jit(solution)/shard_map/fold_key/pallas_call | solution.py:437
  85.5 3.4 %all-to-all-start.2 = ((f32[8,8,256]{2,1,0:T(8,128)}), f32[8,8,256]{2,1,0:T(8,128)S(1)}, u32[]{:S(2)}, u32[]{:S(2)}) async-start(f32[8,8,256]{2,1,0:T(8,128)} %fold_key.1), calls=%async_computation.2 | async-start | bytes 131072 | tf_op jit(solution)/shard_map/all_to_all | solution.py:445
  88.8 0.1 collective-permute-start.8
  88.9 1.5 %collective-permute-start.9 = (bf16[192,1536]{1,0:T(8,128)(2,1)S(1)}, bf16[192,1536]{1,0:T(8,128)(2,1)}, u32[]{:S(2)}, u32[]{:S(2)}) collective-permute-start(bf16[192,1536]{1,0:T(8,128)(2,1)S(1)} %bitcast.13), channel_id=1, source_target_pairs={{0,2},{1,3},{2,0},{3,1},{4,6},{5,7},{6,4},{7,5},{8,10},{9,11},{10,... | collective-permute-start | bytes 1769480 | tf_op jit(solution)/shard_map/ppermute | solution.py:366
  90.5 5.2 %all-to-all-done.2.fold_ref = f32[8,8,256]{2,1,0:T(8,128)S(1)} async-done(((f32[8,8,256]{2,1,0:T(8,128)}), f32[8,8,256]{2,1,0:T(8,128)S(1)}, u32[]{:S(2)}, u32[]{:S(2)}) %all-to-all-start.2) | async-done | bytes 65568 | tf_op jit(solution)/shard_map/all_to_all | solution.py:445
  95.7 0.0 collective-permute-done.3.refs_1_
  95.7 0.6 copy-done.9
  96.3 5.0 %tile_attention.1 = f32[32,8,256]{2,1,0:T(8,128)} custom-call(bf16[1,257,1536]{2,1,0:T(8,128)(2,1)} %patch_ref.3, f32[1536]{0:T(1024)} %gain_ref.6, f32[8,8,256]{2,1,0:T(8,128)} %copy-done.9, f32[1536]{0:T(1024)} %scale_ref.1, f32[192]{0:T(256)} %bias_ref.1, bf16[384,1536]{1,0:T(8,128)(2,1)} %wo_ref.1, bf16[768,384]{1,0:T(8,128)(2,1)} %copy-done.4, ...), custom_call_target="tpu_custom_call" | custom-call | tf_op jit(solution)/shard_map/tile_attention/pallas_call | solution.py:447
  101.4 2.8 %all-to-all-start.3 = ((f32[32,8,256]{2,1,0:T(8,128)}), f32[32,8,256]{2,1,0:T(8,128)S(1)}, u32[]{:S(2)}, u32[]{:S(2)}) async-start(f32[32,8,256]{2,1,0:T(8,128)} %tile_attention.1), calls=%async_computation.3 | async-start | bytes 524288 | tf_op jit(solution)/shard_map/all_to_all | solution.py:458
  104.1 0.1 collective-permute-start.14
  104.2 0.0 collective-permute-done.10.refs_3_
  104.2 1.6 %collective-permute-start.15 = (bf16[192,768]{1,0:T(8,128)(2,1)S(1)}, bf16[192,768]{1,0:T(8,128)(2,1)}, u32[]{:S(2)}, u32[]{:S(2)}) collective-permute-start(bf16[192,768]{1,0:T(8,128)(2,1)S(1)} %copy-done.7), channel_id=1, source_target_pairs={{0,2},{1,3},{2,0},{3,1},{4,6},{5,7},{6,4},{7,5},{8,10},{9,11},{10,... | collective-permute-start | bytes 884744 | tf_op jit(solution)/shard_map/ppermute | solution.py:366
  105.8 0.2 collective-permute-start.16
  106.1 0.7 copy-done.1
  106.7 7.7 %base_attention.1 = (f32[256,128]{1,0:T(8,128)}, f32[256,256]{1,0:T(8,128)}) custom-call(s32[8]{0:T(128)} %pos_ref.5, s32[5,12]{1,0:T(8,128)} %offset_ref.3, f32[8,8,256]{2,1,0:T(8,128)} %copy-done.2, bf16[256,256]{1,0:T(8,128)(2,1)} %get-tuple-element.15.q_ref, bf16[1024,384]{1,0:T(8,128)(2,1)} %copy-done, bf16[1024,384]{1,0:T(8,128)(2,1)} %copy-done.1), custom_call_target="tpu_custom_call" | custom-call | tf_op jit(solution)/shard_map/base_attention/pallas_call | solution.py:464
  114.5 0.0 collective-permute-done.8.refs_1_
  114.5 0.1 all-to-all-done.3.shares_ref
  114.6 0.7 copy-done.3
  115.3 10.0 %fresh_attention.1 = (bf16[64,256]{1,0:T(8,128)(2,1)}, bf16[64,256]{1,0:T(8,128)(2,1)}, bf16[64,256]{1,0:T(8,128)(2,1)}, bf16[64,256]{1,0:T(8,128)(2,1)}, f32[64,768]{1,0:T(8,128)}) custom-call(s32[8]{0:T(128)} %pos_ref.5, s32[5,12]{1,0:T(8,128)} %offset_ref.3, f32[8,8,256]{2,1,0:T(8,128)} %copy-done.2, bf16[256,256]{1,0:T(8,128)(2,1)} %get-tuple-element.15.q_ref, ...), custom_call_target="tpu_custom_call" | custom-call | tf_op jit(solution)/shard_map/fresh_attention/pallas_call | solution.py:475
  125.2 0.0 collective-permute-start.11
  125.3 1.2 collective-permute-start.12
  126.4 0.7 collective-permute-start.13
  127.1 2.3 %collective-permute-done.12.refs_2_ = bf16[64,256]{1,0:T(8,128)(2,1)S(1)} collective-permute-done((bf16[64,256]{1,0:T(8,128)(2,1)}, bf16[64,256]{1,0:T(8,128)(2,1)S(1)}, u32[]{:S(2)}, u32[]{:S(2)}) %collective-permute-start.12) | collective-permute-done | bytes 32800 | tf_op jit(solution)/shard_map/ppermute | solution.py:366
  129.4 0.9 collective-permute-done.13.refs_3_
  130.3 0.6 copy-done.13
  130.9 2.4 %slide_next.1 = bf16[64,768]{1,0:T(8,128)(2,1)} custom-call(f32[64,768]{1,0:T(8,128)} %get-tuple-element.20.mine_ref, bf16[64,256]{1,0:T(8,128)(2,1)} %get-tuple-element.21.refs_0_, bf16[64,256]{1,0:T(8,128)(2,1)} %copy-done.11, bf16[64,256]{1,0:T(8,128)(2,1)} %copy-done.12, bf16[64,256]{1,0:T(8,128)(2,1)} %copy-done.13, bf16[192,768]{1,0:T(8,128)(2,1)} %refs_4_.1, ...), custom_call_target="tpu_custom_call" | custom-call | tf_op jit(solution)/shard_map/slide_next/pallas_call | solution.py:496
  (37 shorter events, 0.3 us)
Async XLA Ops:
  0.0 8.5 %copy-start.10 = (bf16[192,384]{1,0:T(8,128)(2,1)S(1)}, bf16[192,384]{1,0:T(8,128)(2,1)}, u32[]{:S(2)}) copy-start(bf16[192,384]{1,0:T(8,128)(2,1)} %param.24) | copy-start | bytes 442372
  2.9 35.8 %collective-permute-start.4 = (bf16[256,384]{1,0:T(8,128)(2,1)}, bf16[256,384]{1,0:T(8,128)(2,1)S(1)}, u32[]{:S(2)}, u32[]{:S(2)}) collective-permute-start(bf16[256,384]{1,0:T(8,128)(2,1)} %get-tuple-element.16), channel_id=1, source_target_pairs={{0,8},{4,12},{8,0},{12,4},{16,24},{20,28},{24,16},{28,20},{1,9},{5... | collective-permute-start | bytes 589832 | tf_op jit(solution)/shard_map/ppermute | solution.py:366
  5.9 32.8 %collective-permute-start.5 = (bf16[256,384]{1,0:T(8,128)(2,1)}, bf16[256,384]{1,0:T(8,128)(2,1)S(1)}, u32[]{:S(2)}, u32[]{:S(2)}) collective-permute-start(bf16[256,384]{1,0:T(8,128)(2,1)} %get-tuple-element.16), channel_id=1, source_target_pairs={{0,16},{4,20},{8,24},{12,28},{16,0},{20,4},{24,8},{28,12},{1,17},{... | collective-permute-start | bytes 589832 | tf_op jit(solution)/shard_map/ppermute | solution.py:366
  8.5 30.3 %collective-permute-start.6 = (bf16[256,384]{1,0:T(8,128)(2,1)}, bf16[256,384]{1,0:T(8,128)(2,1)S(1)}, u32[]{:S(2)}, u32[]{:S(2)}) collective-permute-start(bf16[256,384]{1,0:T(8,128)(2,1)} %get-tuple-element.16), channel_id=1, source_target_pairs={{0,24},{4,28},{8,16},{12,20},{16,8},{20,12},{24,0},{28,4},{1,25},{... | collective-permute-start | bytes 589832 | tf_op jit(solution)/shard_map/ppermute | solution.py:366
  8.5 14.6 %collective-permute-start = (bf16[192,384]{1,0:T(8,128)(2,1)S(1)}, bf16[192,384]{1,0:T(8,128)(2,1)S(1)}, u32[]{:S(2)}, u32[]{:S(2)}) collective-permute-start(bf16[192,384]{1,0:T(8,128)(2,1)S(1)} %copy-done.10), channel_id=1, source_target_pairs={{0,8},{4,12},{8,0},{12,4},{16,24},{20,28},{24,16},{28,20},{1,9},{5... | collective-permute-start | bytes 442376 | tf_op jit(solution)/shard_map/ppermute | solution.py:366
  9.4 27.6 %collective-permute-start.1 = (bf16[192,384]{1,0:T(8,128)(2,1)S(1)}, bf16[192,384]{1,0:T(8,128)(2,1)S(1)}, u32[]{:S(2)}, u32[]{:S(2)}) collective-permute-start(bf16[192,384]{1,0:T(8,128)(2,1)S(1)} %copy-done.10), channel_id=1, source_target_pairs={{0,16},{4,20},{8,24},{12,28},{16,0},{20,4},{24,8},{28,12},{1,17},{... | collective-permute-start | bytes 442376 | tf_op jit(solution)/shard_map/ppermute | solution.py:366
  23.1 14.0 %collective-permute-start.2 = (bf16[192,384]{1,0:T(8,128)(2,1)S(1)}, bf16[192,384]{1,0:T(8,128)(2,1)S(1)}, u32[]{:S(2)}, u32[]{:S(2)}) collective-permute-start(bf16[192,384]{1,0:T(8,128)(2,1)S(1)} %copy-done.10), channel_id=1, source_target_pairs={{0,24},{4,28},{8,16},{12,20},{16,8},{20,12},{24,0},{28,4},{1,25},{... | collective-permute-start | bytes 442376 | tf_op jit(solution)/shard_map/ppermute | solution.py:366
  37.0 9.6 %copy-start.5 = (bf16[1536,192]{0,1:T(8,128)(2,1)S(1)}, bf16[1536,192]{0,1:T(8,128)(2,1)}, u32[]{:S(2)}) copy-start(bf16[1536,192]{0,1:T(8,128)(2,1)} %param.28) | copy-start | bytes 1769476
  37.1 32.5 %copy-start.4 = (bf16[768,384]{1,0:T(8,128)(2,1)}, bf16[768,384]{1,0:T(8,128)(2,1)S(1)}, u32[]{:S(2)}) copy-start(bf16[768,384]{1,0:T(8,128)(2,1)S(1)} %constant_dynamic-update-slice_fusion.refs_0_) | copy-start | bytes 1769476
  37.1 58.6 %collective-permute-start.3 = (bf16[768,384]{1,0:T(8,128)(2,1)S(1)}, bf16[768,384]{1,0:T(8,128)(2,1)}, u32[]{:S(2)}, u32[]{:S(2)}) collective-permute-start(bf16[768,384]{1,0:T(8,128)(2,1)S(1)} %constant_dynamic-update-slice_fusion.refs_0_), channel_id=1, source_target_pairs={{0,4},{4,0},{8,12},{12,8},{16,20},{20,16},{24,28},{28,24},{1,5},{5... | collective-permute-start | bytes 1769480 | tf_op jit(solution)/shard_map/ppermute | solution.py:366
  38.8 62.6 %copy-start = (bf16[1024,384]{1,0:T(8,128)(2,1)}, bf16[1024,384]{1,0:T(8,128)(2,1)S(1)}, u32[]{:S(2)}) copy-start(bf16[1024,384]{1,0:T(8,128)(2,1)S(1)} %constant_dynamic-update-slice_fusion.4.refs_0_.refs_4_) | copy-start | bytes 2359300
  38.8 67.0 %collective-permute-start.7 = (bf16[1024,384]{1,0:T(8,128)(2,1)S(1)}, bf16[1024,384]{1,0:T(8,128)(2,1)S(1)}, u32[]{:S(2)}, u32[]{:S(2)}) collective-permute-start(bf16[1024,384]{1,0:T(8,128)(2,1)S(1)} %constant_dynamic-update-slice_fusion.4.refs_0_.refs_4_), channel_id=1, source_target_pairs={{0,4},{4,0},{8,12},{12,8},{16,20},{20,16},{24,28},{28,24},{1,5},{5... | collective-permute-start | bytes 2359304 | tf_op jit(solution)/shard_map/ppermute | solution.py:366
  41.1 26.1 %all-to-all-start = ((f32[8,8,256]{2,1,0:T(8,128)}), f32[8,8,256]{2,1,0:T(8,128)S(1)}, u32[]{:S(2)}, u32[]{:S(2)}) async-start(f32[8,8,256]{2,1,0:T(8,128)} %class_row.1), calls=%async_computation | async-start | bytes 131072 | tf_op jit(solution)/shard_map/all_to_all | solution.py:408
  46.6 57.6 %collective-permute-start.10 = (bf16[192,1536]{1,0:T(8,128)(2,1)S(1)}, bf16[192,1536]{1,0:T(8,128)(2,1)S(1)}, u32[]{:S(2)}, u32[]{:S(2)}) collective-permute-start(bf16[192,1536]{1,0:T(8,128)(2,1)S(1)} %bitcast.11), channel_id=1, source_target_pairs={{0,3},{1,2},{2,1},{3,0},{4,7},{5,6},{6,5},{7,4},{8,11},{9,10},{10,... | collective-permute-start | bytes 1769480 | tf_op jit(solution)/shard_map/ppermute | solution.py:366
  67.2 0.6 copy-start.2
  85.5 10.2 %all-to-all-start.2 = ((f32[8,8,256]{2,1,0:T(8,128)}), f32[8,8,256]{2,1,0:T(8,128)S(1)}, u32[]{:S(2)}, u32[]{:S(2)}) async-start(f32[8,8,256]{2,1,0:T(8,128)} %fold_key.1), calls=%async_computation.2 | async-start | bytes 131072 | tf_op jit(solution)/shard_map/all_to_all | solution.py:445
  88.8 25.6 %collective-permute-start.8 = (bf16[192,1536]{1,0:T(8,128)(2,1)S(1)}, bf16[192,1536]{1,0:T(8,128)(2,1)}, u32[]{:S(2)}, u32[]{:S(2)}) collective-permute-start(bf16[192,1536]{1,0:T(8,128)(2,1)S(1)} %bitcast.12), channel_id=1, source_target_pairs={{0,1},{1,0},{2,3},{3,2},{4,5},{5,4},{6,7},{7,6},{8,9},{9,8},{10,11... | collective-permute-start | bytes 1769480 | tf_op jit(solution)/shard_map/ppermute | solution.py:366
  88.9 25.6 %collective-permute-start.9 = (bf16[192,1536]{1,0:T(8,128)(2,1)S(1)}, bf16[192,1536]{1,0:T(8,128)(2,1)}, u32[]{:S(2)}, u32[]{:S(2)}) collective-permute-start(bf16[192,1536]{1,0:T(8,128)(2,1)S(1)} %bitcast.13), channel_id=1, source_target_pairs={{0,2},{1,3},{2,0},{3,1},{4,6},{5,7},{6,4},{7,5},{8,10},{9,11},{10,... | collective-permute-start | bytes 1769480 | tf_op jit(solution)/shard_map/ppermute | solution.py:366
  95.7 0.6 copy-start.9
  96.3 7.8 %copy-start.7 = (bf16[192,768]{1,0:T(8,128)(2,1)S(1)}, bf16[192,768]{1,0:T(8,128)(2,1)}, u32[]{:S(2)}) copy-start(bf16[192,768]{1,0:T(8,128)(2,1)} %refs_4_.1) | copy-start | bytes 884740
  101.4 13.2 %all-to-all-start.3 = ((f32[32,8,256]{2,1,0:T(8,128)}), f32[32,8,256]{2,1,0:T(8,128)S(1)}, u32[]{:S(2)}, u32[]{:S(2)}) async-start(f32[32,8,256]{2,1,0:T(8,128)} %tile_attention.1), calls=%async_computation.3 | async-start | bytes 524288 | tf_op jit(solution)/shard_map/all_to_all | solution.py:458
  104.1 22.3 %collective-permute-start.14 = (bf16[192,768]{1,0:T(8,128)(2,1)S(1)}, bf16[192,768]{1,0:T(8,128)(2,1)}, u32[]{:S(2)}, u32[]{:S(2)}) collective-permute-start(bf16[192,768]{1,0:T(8,128)(2,1)S(1)} %copy-done.7), channel_id=1, source_target_pairs={{0,1},{1,0},{2,3},{3,2},{4,5},{5,4},{6,7},{7,6},{8,9},{9,8},{10,11... | collective-permute-start | bytes 884744 | tf_op jit(solution)/shard_map/ppermute | solution.py:366
  104.2 10.3 %copy-start.6 = (bf16[192,1536]{1,0:T(8,128)(2,1)}, bf16[192,1536]{1,0:T(8,128)(2,1)S(1)}, u32[]{:S(2)}) copy-start(bf16[192,1536]{1,0:T(8,128)(2,1)S(1)} %collective-permute-done.10.refs_3_) | copy-start | bytes 1769476
  104.2 22.9 %collective-permute-start.15 = (bf16[192,768]{1,0:T(8,128)(2,1)S(1)}, bf16[192,768]{1,0:T(8,128)(2,1)}, u32[]{:S(2)}, u32[]{:S(2)}) collective-permute-start(bf16[192,768]{1,0:T(8,128)(2,1)S(1)} %copy-done.7), channel_id=1, source_target_pairs={{0,2},{1,3},{2,0},{3,1},{4,6},{5,7},{6,4},{7,5},{8,10},{9,11},{10,... | collective-permute-start | bytes 884744 | tf_op jit(solution)/shard_map/ppermute | solution.py:366
  105.8 0.9 copy-start.1
  105.8 21.3 %collective-permute-start.16 = (bf16[192,768]{1,0:T(8,128)(2,1)S(1)}, bf16[192,768]{1,0:T(8,128)(2,1)S(1)}, u32[]{:S(2)}, u32[]{:S(2)}) collective-permute-start(bf16[192,768]{1,0:T(8,128)(2,1)S(1)} %copy-done.7), channel_id=1, source_target_pairs={{0,3},{1,2},{2,1},{3,0},{4,7},{5,6},{6,5},{7,4},{8,11},{9,10},{10,... | collective-permute-start | bytes 884744 | tf_op jit(solution)/shard_map/ppermute | solution.py:366
  114.5 0.7 copy-start.3
  125.2 1.9 %collective-permute-start.11 = (bf16[64,256]{1,0:T(8,128)(2,1)}, bf16[64,256]{1,0:T(8,128)(2,1)S(1)}, u32[]{:S(2)}, u32[]{:S(2)}) collective-permute-start(bf16[64,256]{1,0:T(8,128)(2,1)} %get-tuple-element.22), channel_id=1, source_target_pairs={{0,1},{1,0},{2,3},{3,2},{4,5},{5,4},{6,7},{7,6},{8,9},{9,8},{10,11... | collective-permute-start | bytes 98312 | tf_op jit(solution)/shard_map/ppermute | solution.py:366
  125.3 4.2 %collective-permute-start.12 = (bf16[64,256]{1,0:T(8,128)(2,1)}, bf16[64,256]{1,0:T(8,128)(2,1)S(1)}, u32[]{:S(2)}, u32[]{:S(2)}) collective-permute-start(bf16[64,256]{1,0:T(8,128)(2,1)} %get-tuple-element.23), channel_id=1, source_target_pairs={{0,2},{1,3},{2,0},{3,1},{4,6},{5,7},{6,4},{7,5},{8,10},{9,11},{10,... | collective-permute-start | bytes 98312 | tf_op jit(solution)/shard_map/ppermute | solution.py:366
  126.4 3.9 %collective-permute-start.13 = (bf16[64,256]{1,0:T(8,128)(2,1)}, bf16[64,256]{1,0:T(8,128)(2,1)S(1)}, u32[]{:S(2)}, u32[]{:S(2)}) collective-permute-start(bf16[64,256]{1,0:T(8,128)(2,1)} %get-tuple-element.24), channel_id=1, source_target_pairs={{0,3},{1,2},{2,1},{3,0},{4,7},{5,6},{6,5},{7,4},{8,11},{9,10},{10,... | collective-permute-start | bytes 98312 | tf_op jit(solution)/shard_map/ppermute | solution.py:366
  127.1 3.2 %copy-start.8 = (bf16[192,768]{1,0:T(8,128)(2,1)}, bf16[192,768]{1,0:T(8,128)(2,1)S(1)}, u32[]{:S(2)}) copy-start(bf16[192,768]{1,0:T(8,128)(2,1)S(1)} %collective-permute-done.16.refs_7_) | copy-start | bytes 884740
  127.1 3.2 %copy-start.11 = (bf16[64,256]{1,0:T(8,128)(2,1)}, bf16[64,256]{1,0:T(8,128)(2,1)S(1)}, u32[]{:S(2)}) copy-start(bf16[64,256]{1,0:T(8,128)(2,1)S(1)} %collective-permute-done.11.refs_1_) | copy-start | bytes 98308
  129.4 0.9 copy-start.12
  130.3 0.6 copy-start.13

commit v3 on v2

--- a/solution.py
+++ b/solution.py
@@ -22,11 +22,11 @@
 VMEM = pl.BlockSpec(memory_space=pltpu.VMEM)
 SMEM = pl.BlockSpec(memory_space=pltpu.SMEM)
 NT = (((1,), (1,)), ((), ()))
-ROOM = 56 * 1024 * 1024
-
-
-def params():
-    return pltpu.CompilerParams(vmem_limit_bytes=ROOM)
+MIB = 1024 * 1024
+
+
+def params(room):
+    return pltpu.CompilerParams(vmem_limit_bytes=room * MIB)
 
 
 def round_up(value, unit):
@@ -144,10 +144,10 @@
             mixed_s[part, :, 0:cut] = mixed[:, part * cut : (part + 1) * cut]
         values = jnp.zeros((8, wo_ref.shape[0]), F32)
         me = lax.axis_index("tile")
-        for low, ref in enumerate(wv_refs):
-            for high in range(parts // 2):
-                piece = mixed_s[me ^ (2 * high + low)][:, 0:cut].astype(BF16)
-                values = values + dot(piece, ref[high * cut : (high + 1) * cut])
+        for masks, ref in zip(GROUPS, wv_refs):
+            for index, mask in enumerate(masks):
+                piece = mixed_s[me ^ mask][:, 0:cut].astype(BF16)
+                values = values + dot(piece, ref[index * cut : (index + 1) * cut])
     head = lax.broadcasted_iota(I32, values.shape, 0)
     lane = lax.broadcasted_iota(I32, values.shape, 1)
     tmix = jnp.sum(jnp.where(lane // HEAD == head, values, 0.0), axis=0, keepdims=True)
@@ -164,13 +164,16 @@
     sent_ref[:, 6:7, 0:width] = jnp.broadcast_to(bias, (devices, 1, width))
 
 
-def branch_rows(position, axis, offset_ref, head, span, total):
-    shape = (1, 8) if axis == 1 else (8, 1)
-    branch = lax.broadcasted_iota(I32, shape, axis)
+def branch_rows(position, axis, offset_ref, span, total):
+    shape = (1, 24) if axis == 1 else (24, 1)
+    index = lax.broadcasted_iota(I32, shape, axis)
+    branch = index % 8
     residue = jnp.full(shape, -1, I32)
     shift = jnp.zeros(shape, I32)
     for b in range(offset_ref.shape[0]):
-        residue = jnp.where(branch == b, offset_ref[b, lax.axis_index("seg") * 3 + head], residue)
+        for head in range(3):
+            offset = offset_ref[b, lax.axis_index("seg") * 3 + head]
+            residue = jnp.where(index == head * 8 + b, offset, residue)
         length = min(2 * span * 4**b, total)
         shift = jnp.where(branch == b, length.bit_length() - 1, shift)
     below = jnp.left_shift(jnp.int32(1), branch) - 1
@@ -178,27 +181,27 @@
     return ((position & below) == residue) & (jnp.right_shift(position, shift) == mine)
 
 
-def value_lanes(head):
-    group = {0: 2, 1: 3, 2: 1}[head]
-    lane = lax.broadcasted_iota(I32, (1, 256), 1)
-    return lane // HEAD == group
-
-
-def attend(q, q_rows, kv_ref, k_rows, head):
-    lane = lax.broadcasted_iota(I32, (1, 256), 1)
-    q_head = jnp.where(lane // HEAD == head, q, jnp.zeros_like(q))
-    scores = dot_nt(q_head, kv_ref[:, 0:256])
-    count = dot(q_rows, k_rows)
+def as_bf16(condition):
+    return jnp.where(condition, 1.0, 0.0).astype(BF16)
+
+
+def stack_heads(values, size):
+    lane = lax.broadcasted_iota(I32, (1, values.shape[1]), 1)
+    zero = jnp.zeros_like(values)
+    return jnp.concatenate(
+        [jnp.where(lane // size == head, values, zero) for head in range(3)], axis=0
+    )
+
+
+def attend(q, q_rows, kv_ref, k_rows):
+    scores = dot_nt(stack_heads(q, HEAD), kv_ref[:, 0:256])
+    count = dot(stack_heads(as_bf16(q_rows), 8), k_rows)
     scores = jnp.where(count > 0.5, scores, LOW)
     highest = jnp.max(scores, axis=-1, keepdims=True)
     weight = jnp.exp(scores - highest) * count
     denom = jnp.sum(weight, axis=-1, keepdims=True)
     numer = dot(weight.astype(BF16), kv_ref[:, 128:384])
     return highest, denom, numer
-
-
-def as_bf16(condition):
-    return jnp.where(condition, 1.0, 0.0).astype(BF16)
 
 
 def merge(old, new):
@@ -210,16 +213,31 @@
     return top, old_den * keep + new_den * take, old_num * keep + new_num * take
 
 
-def store_state(state, head, ml_ref, acc_ref):
+def clear_state(ml_ref, acc_ref):
+    lane = lax.broadcasted_iota(I32, ml_ref.shape, 1)
+    ml_ref[...] = jnp.where(lane == 0, LOW, 0.0)
+    acc_ref[...] = jnp.zeros_like(acc_ref)
+
+
+def store_state(state, ml_ref, acc_ref):
     highest, denom, numer = state
-    lane = lax.broadcasted_iota(I32, (1, 128), 1)
-    ml = jnp.where(lane == head, highest, ml_ref[...])
-    ml_ref[...] = jnp.where(lane == head + 8, denom, ml)
-    acc_ref[...] = jnp.where(value_lanes(head), numer, acc_ref[...])
-
-
-def load_state(head, ml_ref, acc_ref):
-    return ml_ref[:, head : head + 1], ml_ref[:, head + 8 : head + 9], acc_ref[...]
+    lane = lax.broadcasted_iota(I32, ml_ref.shape, 1)
+    ml_ref[...] = jnp.where(lane == 0, highest, denom)
+    acc_ref[...] = numer
+
+
+def load_state(ml_ref, acc_ref):
+    return ml_ref[:, 0:1], ml_ref[:, 1:2], acc_ref[...]
+
+
+def finish(state):
+    _, den, num = state
+    result = num / jnp.where(den > 0.0, den, 1.0)
+    rows = num.shape[0] // 3
+    group = lax.broadcasted_iota(I32, (1, 256), 1) // HEAD
+    joined = jnp.where(group == 1, result[2 * rows :], 0.0)
+    joined = jnp.where(group == 2, result[0:rows], joined)
+    return jnp.where(group == 3, result[rows : 2 * rows], joined)
 
 
 def fresh_places(padded, pack_ref, pos_ref):
@@ -237,49 +255,54 @@
     return row, col, flags[:, 0:padded] > 0.5, flag_col > 0.5
 
 
-def key_places(swapped, low, block, span, step):
+def key_places(swapped, block, span, step):
     place = lax.broadcasted_iota(I32, (1, block), 1)
     if not swapped:
         return place + step * block
-    source = lax.axis_index("tile") ^ (2 * (place // span) + low)
-    return source * span + (place & (span - 1))
-
-
-def key_rows(place, pos_col, flag_col, offset_ref, head, span, total):
-    rows = branch_rows(place, 0, offset_ref, head, span, total)
+    part = place // span
+    mask = jnp.where(part < 4, 2 * part, 2 * part - 7)
+    return (lax.axis_index("tile") ^ mask) * span + (place & (span - 1))
+
+
+def key_rows(place, pos_col, flag_col, offset_ref, span, total):
+    rows = branch_rows(place, 0, offset_ref, span, total)
     taken = jnp.where((place == pos_col) & flag_col, 1.0, 0.0)
     taken = jnp.max(taken, axis=0, keepdims=True)
     return as_bf16(rows & (taken < 0.5))
 
 
 def base_attention_kernel(span, total, padded, pos_ref, offset_ref, pack_ref, q_ref, *refs):
-    *kv_refs, ml_ref, acc_ref = refs
+    *kv_refs, krows_ref, ml_ref, acc_ref = refs
+    swapped = len(kv_refs) > 1
+    kv_ref = kv_refs.pop()
     step = pl.program_id(0)
     rows = q_ref.shape[0]
+    block = kv_ref.shape[0]
 
     @pl.when(step == 0)
     def _():
-        lane = lax.broadcasted_iota(I32, (rows, 128), 1)
-        ml_ref[...] = jnp.where(lane < 8, LOW, 0.0)
-        acc_ref[...] = jnp.zeros_like(acc_ref)
-
+        clear_state(ml_ref, acc_ref)
+
+    start = 0
+    for ref in kv_refs:
+        kv_ref[start : start + ref.shape[0], :] = ref[...]
+        start += ref.shape[0]
     _, pos_col, _, flag_col = fresh_places(padded, pack_ref, pos_ref)
     place = lax.broadcasted_iota(I32, (rows, 1), 0) + lax.axis_index("tile") * span
-    for head in range(3):
-        q_rows = as_bf16(branch_rows(place, 1, offset_ref, head, span, total))
-        for low, kv_ref in enumerate(kv_refs):
-            keys = key_places(len(kv_refs) > 1, low, kv_ref.shape[0], span, step)
-            k_rows = key_rows(keys, pos_col, flag_col, offset_ref, head, span, total)
-            new = attend(q_ref[...], q_rows, kv_ref, k_rows, head)
-            store_state(merge(load_state(head, ml_ref, acc_ref), new), head, ml_ref, acc_ref)
+    q_rows = branch_rows(place, 1, offset_ref, span, total)
+    keys = key_places(swapped, block, span, step)
+    k_rows = key_rows(keys, pos_col, flag_col, offset_ref, span, total)
+    krows_ref[...] = k_rows
+    new = attend(q_ref[...], q_rows, kv_ref, k_rows)
+    store_state(merge(load_state(ml_ref, acc_ref), new), ml_ref, acc_ref)
 
 
 def fresh_kernel(
-    span, total, parts, pos_ref, offset_ref, pack_ref, q_ref, shares_ref, final_ref, gain_ref,
+    span, total, pos_ref, offset_ref, pack_ref, q_ref, shares_ref, final_ref, gain_ref,
     wq_ref, wk_ref, wv_ref, ml_ref, acc_ref, rows_ref, *refs,
 ):
     embed_refs, refs = refs[:4], refs[4:]
-    kv_refs, refs = refs[:parts], refs[parts:]
+    kv_ref, krows_ref, *refs = refs
     outs, refs = refs[:4], refs[4:]
     mine_ref, fresh_s, qf_s, kvf_s, mlf_s, accf_s, att_s = refs
     step = pl.program_id(0)
@@ -287,6 +310,7 @@
     padded = fresh_s.shape[0]
     seg = lax.axis_index("seg")
     pos_row, pos_col, flag_row, flag_col = fresh_places(padded, pack_ref, pos_ref)
+    f_rows = branch_rows(pos_col, 1, offset_ref, span, total)
 
     @pl.when(step == 0)
     def _():
@@ -306,35 +330,21 @@
             fresh_s[0:groups, part * 192 : (part + 1) * 192] = piece.astype(BF16).astype(F32)
         normed = layer_norm(fresh_s[...], gain_ref[...].reshape(1, DS)).astype(BF16)
         project(normed, wq_ref, wk_ref, wv_ref, qf_s, kvf_s)
-        lane = lax.broadcasted_iota(I32, (padded, 128), 1)
-        mlf_s[...] = jnp.where(lane < 8, LOW, 0.0)
-        accf_s[...] = jnp.zeros_like(accf_s)
-
-    for head in range(3):
-        q_rows = as_bf16(branch_rows(pos_col, 1, offset_ref, head, span, total))
-        for low, kv_ref in enumerate(kv_refs):
-            keys = key_places(parts > 1, low, kv_ref.shape[0], span, step)
-            k_rows = key_rows(keys, pos_col, flag_col, offset_ref, head, span, total)
-            new = attend(qf_s[...], q_rows, kv_ref, k_rows, head)
-            store_state(merge(load_state(head, mlf_s, accf_s), new), head, mlf_s, accf_s)
+        clear_state(mlf_s, accf_s)
+
+    new = attend(qf_s[...], f_rows, kv_ref, krows_ref[...])
+    store_state(merge(load_state(mlf_s, accf_s), new), mlf_s, accf_s)
 
     @pl.when(step == pl.num_programs(0) - 1)
     def _():
         first = lax.axis_index("tile") * span
         place = lax.broadcasted_iota(I32, (rows, 1), 0) + first
-        base = jnp.zeros((rows, 256), F32)
-        fresh = jnp.zeros((padded, 256), F32)
-        for head in range(3):
-            q_rows = as_bf16(branch_rows(place, 1, offset_ref, head, span, total))
-            f_rows = as_bf16(branch_rows(pos_col, 1, offset_ref, head, span, total))
-            k_rows = as_bf16(branch_rows(pos_row, 0, offset_ref, head, span, total) & flag_row)
-            lanes = value_lanes(head)
-            new = attend(q_ref[...], q_rows, kvf_s, k_rows, head)
-            top, den, num = merge(load_state(head, ml_ref, acc_ref), new)
-            base = jnp.where(lanes, num / den, base)
-            new = attend(qf_s[...], f_rows, kvf_s, k_rows, head)
-            top, den, num = merge(load_state(head, mlf_s, accf_s), new)
-            fresh = jnp.where(lanes, num / jnp.where(den > 0.0, den, 1.0), fresh)
+        q_rows = branch_rows(place, 1, offset_ref, span, total)
+        k_rows = as_bf16(branch_rows(pos_row, 0, offset_ref, span, total) & flag_row)
+        new = attend(q_ref[...], q_rows, kvf_s, k_rows)
+        base = finish(merge(load_state(ml_ref, acc_ref), new))
+        new = attend(qf_s[...], f_rows, kvf_s, k_rows)
+        fresh = finish(merge(load_state(mlf_s, accf_s), new))
         chosen = as_bf16((place == pos_row) & flag_row)
         hit = jnp.sum(chosen.astype(F32), axis=1, keepdims=True) > 0.5
         att_s[...] = jnp.where(hit, dot(chosen, fresh.astype(BF16)), base)
@@ -366,17 +376,11 @@
     return lax.ppermute(block, axis, [(i, i ^ mask) for i in range(count)])
 
 
-def gather_tile(block):
-    count = lax.axis_size("tile")
-    if count > 8:
-        return [lax.all_gather(block, "tile", axis=0, tiled=True)]
-    parts = [block] + [trade(block, "tile", mask) for mask in range(2, count, 2)]
-    even = jnp.concatenate(parts, axis=0)
-    return [even, trade(even, "tile", 1)]
-
-
-def gather_seg(block):
-    return [block] + [trade(block, "seg", mask) for mask in range(1, 4)]
+GROUPS = ((0,), (2, 4, 6), (1,), (3, 5, 7))
+
+
+def together(*values):
+    return lax.optimization_barrier(values)
 
 
 def shards(
@@ -392,9 +396,11 @@
     cut, local_cols = vit_query.shape
     fresh = slide_pos.shape[0]
     padded = max(16, fresh)
+    small = tiles == 8
     call = pl.pallas_call
     sds = jax.ShapeDtypeStruct
     weights = (slide_query.T, slide_key.T, slide_value.T)
+    embed = embed_proj.T
 
     pack = call(
         functools.partial(class_kernel, fresh),
@@ -402,47 +408,65 @@
         grid=(1,),
         in_specs=[pl.BlockSpec((1, 16, DV), lambda i: (0, 0, 0)), VMEM, SMEM, VMEM],
         out_specs=VMEM,
-        compiler_params=params(),
+        compiler_params=params(8),
         name="class_row",
     )(patches, vit_norm_gain, slide_pos, kept)
+
+    pack, value, cached, embed, slide_out = together(pack, vit_value, cached, embed, slide_out)
     pack = lax.all_to_all(pack, "tile", 0, 0, tiled=True)
-
     base_rows, q_base, kv_base = call(
         base_kernel,
         out_shape=(sds((span, DS), BF16), sds((span, 256), BF16), sds((span, 384), BF16)),
         in_specs=[VMEM] * 7,
         out_specs=(VMEM,) * 3,
-        compiler_params=params(),
+        compiler_params=params(16),
         name="base_rows",
     )(cached, kept, mask_token, slide_gain, *weights)
-    wv_all = gather_tile(vit_value)
-    kv_all = gather_tile(kv_base)
-    embed_all = gather_seg(embed_proj.T)
-    slide_out_all = gather_seg(slide_out)
-
-    small = tiles <= 8
+    if small:
+        value_z = [trade(value, "tile", mask) for mask in (2, 4, 6)]
+        value_y = trade(value, "tile", 1)
+        kv_y = trade(kv_base, "tile", 1)
+    embed_x = trade(embed, "seg", 2)
+    out_x = trade(slide_out, "seg", 2)
+
     part_shape = (tiles, fresh, local_cols) if small else (fresh, local_cols)
     part = call(
         functools.partial(query_kernel, cut),
         out_shape=sds(part_shape, F32),
         in_specs=[VMEM] * 2,
         out_specs=VMEM,
-        compiler_params=params(),
+        compiler_params=params(8 if small else 16),
         name="query_share",
     )(pack, vit_query)
     if small:
+        value_z = jnp.concatenate(value_z, axis=0)
+        part, value_z, kv_own, embed, embed_x, slide_out, out_x = together(
+            part, value_z, kv_base, embed, embed_x, slide_out, out_x
+        )
         part = lax.all_to_all(part, "tile", 0, 0, tiled=True)
+        kv_z = [trade(kv_own, "tile", mask) for mask in (2, 4, 6)]
+        wv_all = [value, value_z, value_y, trade(value_z, "tile", 1)]
     else:
         part = lax.psum(part, "tile")
+        wv_all = [lax.all_gather(value, "tile", axis=0, tiled=True)]
+    embed_all = [embed, trade(embed, "seg", 1), embed_x, trade(embed_x, "seg", 1)]
+    slide_out_all = [slide_out, trade(slide_out, "seg", 1), out_x, trade(out_x, "seg", 1)]
     folded = call(
         fold_kernel,
         out_shape=sds((fresh, 8, round_up(cut, 128)), F32),
         in_specs=[VMEM] * 2,
         out_specs=VMEM,
-        compiler_params=params(),
+        compiler_params=params(8 if small else 16),
         name="fold_key",
     )(part, vit_key)
-    folded = lax.all_to_all(folded, "tile", 0, 0, tiled=True)
+    if small:
+        kv_z = jnp.concatenate(kv_z, axis=0)
+        folded, kv_z = together(folded, kv_z)
+        folded = lax.all_to_all(folded, "tile", 0, 0, tiled=True)
+        kv_all = [kv_own, kv_z, kv_y, trade(kv_z, "tile", 1)]
+    else:
+        folded = lax.all_to_all(folded, "tile", 0, 0, tiled=True)
+        kv_all = [lax.all_gather(kv_base, "tile", axis=0, tiled=True)]
 
     sent = call(
         functools.partial(tile_kernel, cut),
@@ -452,45 +476,50 @@
         scratch_shapes=[
             pltpu.VMEM((8, DV), F32), pltpu.VMEM((tiles, 8, round_up(cut, 128)), F32),
         ],
-        compiler_params=params(),
+        compiler_params=params(16 if small else 32),
         name="tile_attention",
     )(patches, vit_norm_gain, folded, layer_scale, embed_bias, vit_out, *wv_all)
     shares = lax.all_to_all(sent, ("tile", "seg"), 0, 0, tiled=True)
 
-    parts = len(kv_all)
-    block = min(kv_all[0].shape[0], 2048)
-    steps = kv_all[0].shape[0] // block
-    kv_specs = [pl.BlockSpec((block, 384), lambda i: (i, 0))] * parts
-    ml, acc = call(
+    block = min(total, 2048)
+    steps = total // block
+    kv_spec = pl.BlockSpec((block, 384), lambda i: (i, 0))
+    krows_spec = pl.BlockSpec((24, block), lambda i: (0, i))
+    kv_shape = [sds((total, 384), BF16)] if small else []
+    *kv_sorted, krows, ml, acc = call(
         functools.partial(base_attention_kernel, span, total, padded),
-        out_shape=(sds((span, 128), F32), sds((span, 256), F32)),
+        out_shape=(
+            *kv_shape, sds((24, total), BF16),
+            sds((3 * span, 128), F32), sds((3 * span, 256), F32),
+        ),
         grid=(steps,),
-        in_specs=[SMEM, SMEM, VMEM, VMEM] + kv_specs,
-        out_specs=(VMEM, VMEM),
-        compiler_params=params(),
+        in_specs=[SMEM, SMEM, VMEM, VMEM] + ([VMEM] * 4 if small else [kv_spec]),
+        out_specs=(*([kv_spec] if small else []), krows_spec, VMEM, VMEM),
+        compiler_params=params(40),
         name="base_attention",
     )(slide_pos, offsets, pack, q_base, *kv_all)
+    kv_sorted = kv_sorted[0] if small else kv_all[0]
 
     count = span // segs
     outs = call(
-        functools.partial(fresh_kernel, span, total, parts),
+        functools.partial(fresh_kernel, span, total),
         out_shape=(sds((count, 256), BF16),) * 4 + (sds((count, DS), F32),),
         grid=(steps,),
-        in_specs=[SMEM] * 2 + [VMEM] * 15 + kv_specs,
+        in_specs=[SMEM] * 2 + [VMEM] * 15 + [kv_spec, krows_spec],
         out_specs=(VMEM,) * 5,
         scratch_shapes=[
             pltpu.VMEM((padded, DS), F32),
             pltpu.VMEM((padded, 256), BF16),
             pltpu.VMEM((padded, 384), BF16),
-            pltpu.VMEM((padded, 128), F32),
-            pltpu.VMEM((padded, 256), F32),
+            pltpu.VMEM((3 * padded, 128), F32),
+            pltpu.VMEM((3 * padded, 256), F32),
             pltpu.VMEM((span, 256), F32),
         ],
-        compiler_params=params(),
+        compiler_params=params(24 if small else 48),
         name="fresh_attention",
     )(
         slide_pos, offsets, pack, q_base, shares, final_gain, slide_gain, *weights, ml, acc,
-        base_rows, *embed_all, *kv_all,
+        base_rows, *embed_all, kv_sorted, krows,
     )
     swapped = [outs[0]] + [trade(outs[mask], "seg", mask) for mask in range(1, 4)]
     return call(
@@ -498,7 +527,7 @@
         out_shape=sds((count, DS), BF16),
         in_specs=[VMEM] * 9,
         out_specs=VMEM,
-        compiler_params=params(),
+        compiler_params=params(8),
         name="slide_next",
     )(outs[4], *swapped, *slide_out_all)
 

time: 134 us -> 113 us (0.84)
  waiting for transfers between devices: 48.9 us -> 29.5 us
  blocking collectives: 14.1 us -> 0 us
  local copies, waits for them, and re-layouts: 4.37 us -> 17.4 us
  Pallas kernels: 33.2 us -> 22.4 us
  starting transfers between devices: 32.5 us -> 41.2 us
    all_to_all x1, waiting for transfers between devices: 20.5 us -> 2.93 us  [shards(): pack = lax.all_to_all(pack, 'tile', 0, 0, tiled=True)]
    all_to_all x1 -> x0, blocking collectives: 14.1 us -> none  [shards(): part = lax.all_to_all(part, 'tile', 0, 0, tiled=True)]
    unnamed x34 -> x78, local copies, waits for them, and re-layouts: 4.31 us -> 17.4 us
    ppermute x17 -> x19, waiting for transfers between devices: 23.1 us -> 12.1 us  [trade(): return lax.ppermute(block, axis, [(i, i ^ mask) for i in range(count)])]
    all_to_all x0 -> x1, waiting for transfers between devices: none -> 9.96 us  [shards(): part = lax.all_to_all(part, 'tile', 0, 0, tiled=True)]
    all_to_all x0 -> x1, starting transfers between devices: none -> 4.88 us  [shards(): part = lax.all_to_all(part, 'tile', 0, 0, tiled=True)]
    pallas_call x1, Pallas kernels: 9.97 us -> 6.44 us  [shards(): call(functools.partial(fresh_kernel, span, total), out_shape=(sds((count,...]
    pallas_call x1, Pallas kernels: 2.85 us -> 0.85 us  [shards(): call(base_kernel, out_shape=(sds((span, DS), BF16), sds((span, 256), BF16...]
  transfers between devices with their start and end apart: 20 -> 23, of which waited for: 7 -> 7; matrix products, arithmetic and copies ran while one was open for 1% -> 1% of each run, Pallas kernels for 21% -> 17%
where the time goes in v3:
time: 113 us; the launch traced here: 112 us
  starting transfers between devices  41.2 us (36%)
  waiting for transfers between devices  29.5 us (26%)
  Pallas kernels  22.4 us (20%)
  local copies, waits for them, and re-layouts  17.4 us (15%)
    ppermute x19, starting transfers between devices, trade(): return lax.ppermute(block, axis, [(i, i ^ mask) for i in range(count)])  22.1 us
    unnamed x78, local copies, waits for them, and re-layouts  17.4 us
    ppermute x19, waiting for transfers between devices, trade(): return lax.ppermute(block, axis, [(i, i ^ mask) for i in range(count)])  12.1 us
    all_to_all x1, waiting for transfers between devices, shards(): part = lax.all_to_all(part, 'tile', 0, 0, tiled=True)  9.96 us
    pallas_call x1, Pallas kernels, shards(): call(functools.partial(fresh_kernel, span, total), out_shape=(sds((count,...  6.44 us
    all_to_all x1, starting transfers between devices, shards(): pack = lax.all_to_all(pack, 'tile', 0, 0, tiled=True)  6.05 us
    pallas_call x1, Pallas kernels, shards(): call(functools.partial(base_attention_kernel, span, total, padded), out_s...  5.83 us
    all_to_all x1, starting transfers between devices, shards(): part = lax.all_to_all(part, 'tile', 0, 0, tiled=True)  4.88 us
  transfers between devices with their start and end apart: 23, of which 7 were waited for; matrix products, arithmetic and copies ran while one was open for 1% of the time, Pallas kernels for 17%

profile of v3, /device:TPU:0, one launch (start us, length us, event | category | flops | bytes accessed | tf_op | source)
XLA Modules:
  0.0 111.7 jit_solution(14545601953909584264)
XLA Ops:
  0.0 1.1 %copy-done = bf16[1,257,1536]{2,1,0:T(8,128)(2,1)S(1)} copy-done((bf16[1,257,1536]{2,1,0:T(8,128)(2,1)S(1)}, bf16[1,257,1536]{2,1,0:T(8,128)(2,1)}, u32[]{:S(2)}) %copy-start) | copy-done | bytes 789528
  1.1 0.7 copy-done.26
  1.8 0.7 copy-done.33
  2.5 0.7 copy-done.36
  3.2 1.4 %class_row.1 = f32[8,8,256]{2,1,0:T(8,128)} custom-call(bf16[1,257,1536]{2,1,0:T(8,128)(2,1)S(1)} %copy-done, f32[1536]{0:T(1024)S(1)} %copy-done.26, s32[8]{0:T(128)S(1)} %copy-done.33, s32[256]{0:T(256)S(1)} %copy-done.36), custom_call_target="tpu_custom_call" | custom-call | tf_op jit(solution)/shard_map/class_row/pallas_call | solution.py:405
  4.6 2.9 %collective-permute-start.3 = (bf16[192,1536]{1,0:T(8,128)(2,1)}, bf16[192,1536]{1,0:T(8,128)(2,1)}, u32[]{:S(2)}, u32[]{:S(2)}) collective-permute-start(bf16[192,1536]{1,0:T(8,128)(2,1)} %bitcast.refs_0_), channel_id=1, source_target_pairs={{0,2},{1,3},{2,0},{3,1},{4,6},{5,7},{6,4},{7,5},{8,10},{9,11},{10,... | collective-permute-start | bytes 1769480 | tf_op jit(solution)/shard_map/ppermute | solution.py:376
  7.6 4.1 %collective-permute-start.2 = (bf16[192,384]{1,0:T(8,128)(2,1)}, bf16[192,384]{1,0:T(8,128)(2,1)S(1)}, u32[]{:S(2)}, u32[]{:S(2)}) collective-permute-start(bf16[192,384]{1,0:T(8,128)(2,1)} %refs_0_), channel_id=1, source_target_pairs={{0,24},{4,28},{8,16},{12,20},{16,8},{20,12},{24,0},{28,4},{1,25},{... | collective-permute-start | bytes 442376 | tf_op jit(solution)/shard_map/ppermute | solution.py:376
  12.3 6.1 %all-to-all-start = ((f32[8,8,256]{2,1,0:T(8,128)}), f32[8,8,256]{2,1,0:T(8,128)S(1)}, u32[]{:S(2)}, u32[]{:S(2)}) async-start(f32[8,8,256]{2,1,0:T(8,128)} %class_row.1), calls=%async_computation | async-start | bytes 131072 | tf_op jit(solution)/shard_map/all_to_all | solution.py:416
  18.4 1.0 copy-done.16
  19.3 0.7 copy-done.29
  20.0 0.7 copy-done.35
  20.7 0.7 copy-done.37
  21.4 0.9 base_rows.1
  22.3 0.7 copy-done.12
  23.0 2.9 %all-to-all-done.pack_ref = f32[8,8,256]{2,1,0:T(8,128)S(1)} async-done(((f32[8,8,256]{2,1,0:T(8,128)}), f32[8,8,256]{2,1,0:T(8,128)S(1)}, u32[]{:S(2)}, u32[]{:S(2)}) %all-to-all-start) | async-done | bytes 65568 | tf_op jit(solution)/shard_map/all_to_all | solution.py:416
  25.9 0.8 query_share.1
  27.4 1.8 %collective-permute-start.9 = (bf16[576,384]{1,0:T(8,128)(2,1)S(1)}, bf16[576,384]{1,0:T(8,128)(2,1)S(1)}, u32[]{:S(2)}, u32[]{:S(2)}) collective-permute-start(bf16[576,384]{1,0:T(8,128)(2,1)S(1)} %pad_maximum_fusion.1.refs_1_), channel_id=1, source_target_pairs={{0,4},{4,0},{8,12},{12,8},{16,20},{20,16},{24,28},{28,24},{1,5},{5... | collective-permute-start | bytes 1327112 | tf_op jit(solution)/shard_map/ppermute | solution.py:376
  29.2 3.6 %collective-permute-start.7 = (bf16[256,384]{1,0:T(8,128)(2,1)S(1)}, bf16[256,384]{1,0:T(8,128)(2,1)S(1)}, u32[]{:S(2)}, u32[]{:S(2)}) collective-permute-start(bf16[256,384]{1,0:T(8,128)(2,1)S(1)} %get-tuple-element.39.refs_0_), channel_id=1, source_target_pairs={{0,24},{4,28},{8,16},{12,20},{16,8},{20,12},{24,0},{28,4},{1,25},{... | collective-permute-start | bytes 589832 | tf_op jit(solution)/shard_map/ppermute | solution.py:376
  32.8 0.8 collective-permute-start.5
  33.6 4.9 %all-to-all-start.1 = ((f32[8,8,384]{2,1,0:T(8,128)}), f32[8,8,384]{2,1,0:T(8,128)S(1)}, u32[]{:S(2)}, u32[]{:S(2)}) async-start(f32[8,8,384]{2,1,0:T(8,128)} %query_share.1), calls=%async_computation.1 | async-start | bytes 196608 | tf_op jit(solution)/shard_map/all_to_all | solution.py:446
  38.5 2.0 %collective-permute-start.8 = (bf16[192,384]{1,0:T(8,128)(2,1)}, bf16[192,384]{1,0:T(8,128)(2,1)}, u32[]{:S(2)}, u32[]{:S(2)}) collective-permute-start(bf16[192,384]{1,0:T(8,128)(2,1)} %refs_0_), channel_id=1, source_target_pairs={{0,4},{4,0},{8,12},{12,8},{16,20},{20,16},{24,28},{28,24},{1,5},{5... | collective-permute-start | bytes 442376 | tf_op jit(solution)/shard_map/ppermute | solution.py:376
  40.5 10.0 %all-to-all-done.1.part_ref = f32[8,8,384]{2,1,0:T(8,128)S(1)} async-done(((f32[8,8,384]{2,1,0:T(8,128)}), f32[8,8,384]{2,1,0:T(8,128)S(1)}, u32[]{:S(2)}, u32[]{:S(2)}) %all-to-all-start.1) | async-done | bytes 98336 | tf_op jit(solution)/shard_map/all_to_all | solution.py:446
  50.4 0.8 fold_key.1
  51.3 1.0 pad_maximum_fusion.refs_1_
  52.3 4.5 %all-to-all-start.2 = ((f32[8,8,256]{2,1,0:T(8,128)}), f32[8,8,256]{2,1,0:T(8,128)S(1)}, u32[]{:S(2)}, u32[]{:S(2)}) async-start(f32[8,8,256]{2,1,0:T(8,128)} %fold_key.1), calls=%async_computation.2 | async-start | bytes 131072 | tf_op jit(solution)/shard_map/all_to_all | solution.py:465
  56.8 2.0 %collective-permute-start.11 = (bf16[768,384]{1,0:T(8,128)(2,1)S(1)}, bf16[768,384]{1,0:T(8,128)(2,1)S(1)}, u32[]{:S(2)}, u32[]{:S(2)}) collective-permute-start(bf16[768,384]{1,0:T(8,128)(2,1)S(1)} %pad_maximum_fusion.refs_1_), channel_id=1, source_target_pairs={{0,4},{4,0},{8,12},{12,8},{16,20},{20,16},{24,28},{28,24},{1,5},{5... | collective-permute-start | bytes 1769480 | tf_op jit(solution)/shard_map/ppermute | solution.py:376
  59.4 4.5 %all-to-all-done.2.fold_ref = f32[8,8,256]{2,1,0:T(8,128)S(1)} async-done(((f32[8,8,256]{2,1,0:T(8,128)}), f32[8,8,256]{2,1,0:T(8,128)S(1)}, u32[]{:S(2)}, u32[]{:S(2)}) %all-to-all-start.2) | async-done | bytes 65568 | tf_op jit(solution)/shard_map/all_to_all | solution.py:465
  63.9 1.3 %copy-done.7 = bf16[384,1536]{1,0:T(8,128)(2,1)S(1)} copy-done((bf16[384,1536]{1,0:T(8,128)(2,1)S(1)}, bf16[384,1536]{1,0:T(8,128)(2,1)}, u32[]{:S(2)}) %copy-start.7) | copy-done | bytes 1179672
  65.2 4.1 %tile_attention.1 = f32[32,8,256]{2,1,0:T(8,128)} custom-call(bf16[1,257,1536]{2,1,0:T(8,128)(2,1)S(1)} %copy-done.1, f32[1536]{0:T(1024)S(1)} %copy-done.27, f32[8,8,256]{2,1,0:T(8,128)S(1)} %all-to-all-done.2.fold_ref, f32[1536]{0:T(1024)S(1)} %copy-done.32, f32[192]{0:T(256)S(1)} %copy-done.38, bf16[384,1536]{1,0:T(8,128)(2,1)S(1)} %copy-done.7, ...), custom_call_target="tpu_custom_call" | custom-call | tf_op jit(solution)/shard_map/tile_attention/pallas_call | solution.py:471
  69.3 3.6 %all-to-all-start.3 = ((f32[32,8,256]{2,1,0:T(8,128)}), f32[32,8,256]{2,1,0:T(8,128)}, u32[]{:S(2)}, u32[]{:S(2)}) async-start(f32[32,8,256]{2,1,0:T(8,128)} %tile_attention.1), calls=%async_computation.3 | async-start | bytes 524288 | tf_op jit(solution)/shard_map/all_to_all | solution.py:482
  72.9 1.5 %collective-permute-start.10 = (bf16[256,384]{1,0:T(8,128)(2,1)}, bf16[256,384]{1,0:T(8,128)(2,1)S(1)}, u32[]{:S(2)}, u32[]{:S(2)}) collective-permute-start(bf16[256,384]{1,0:T(8,128)(2,1)} %copy-done.20), channel_id=1, source_target_pairs={{0,4},{4,0},{8,12},{12,8},{16,20},{20,16},{24,28},{28,24},{1,5},{5... | collective-permute-start | bytes 589832 | tf_op jit(solution)/shard_map/ppermute | solution.py:376
  74.4 7.8 %collective-permute-done.10.refs_2_ = bf16[256,384]{1,0:T(8,128)(2,1)S(1)} collective-permute-done((bf16[256,384]{1,0:T(8,128)(2,1)}, bf16[256,384]{1,0:T(8,128)(2,1)S(1)}, u32[]{:S(2)}, u32[]{:S(2)}) %collective-permute-start.10) | collective-permute-done | bytes 196640 | tf_op jit(solution)/shard_map/ppermute | solution.py:376
  82.2 0.8 copy-done.10
  83.1 1.1 copy-done.11
  84.1 0.9 copy-done.21
  85.1 5.8 %base_attention.1 = (bf16[2048,384]{1,0:T(8,128)(2,1)S(1)}, bf16[24,2048]{1,0:T(8,128)(2,1)S(1)}, f32[768,128]{1,0:T(8,128)S(1)}, f32[768,256]{1,0:T(8,128)S(1)}) custom-call(s32[8]{0:T(128)S(1)} %copy-done.34, s32[5,12]{1,0:T(8,128)S(1)} %copy-done.28, f32[8,8,256]{2,1,0:T(8,128)S(1)} %all-to-all-done.pack_ref, ...), custom_call_target="tpu_custom_call" | custom-call | tf_op jit(solution)/shard_map/base_attention/pallas_call | solution.py:489
  90.9 0.9 copy-done.8
  91.8 0.7 copy-done.14
  92.6 0.6 copy-done.24
  93.3 1.1 %copy-done.9 = f32[768,256]{1,0:T(8,128)S(1)} copy-done((f32[768,256]{1,0:T(8,128)S(1)}, f32[768,256]{1,0:T(8,128)}, u32[]{:S(2)}) %copy-start.9) | copy-done | bytes 786456
  94.4 1.0 copy-done.13
  95.4 1.0 copy-done.15
  96.4 0.9 copy-done.25
  97.3 6.4 %fresh_attention.1 = (bf16[64,256]{1,0:T(8,128)(2,1)S(1)}, bf16[64,256]{1,0:T(8,128)(2,1)S(1)}, bf16[64,256]{1,0:T(8,128)(2,1)S(1)}, bf16[64,256]{1,0:T(8,128)(2,1)S(1)}, f32[64,768]{1,0:T(8,128)S(1)}) custom-call(s32[8]{0:T(128)S(1)} %copy-done.34, s32[5,12]{1,0:T(8,128)S(1)} %copy-done.28, f32[8,8,256]{2,1,0:T(8,128)S(1)} %all-to-all-done.pack_ref, ...), custom_call_target="tpu_custom_call" | custom-call | tf_op jit(solution)/shard_map/fresh_attention/pallas_call | solution.py:504
  104.3 1.7 %collective-permute-start.15 = (bf16[64,256]{1,0:T(8,128)(2,1)S(1)}, bf16[64,256]{1,0:T(8,128)(2,1)S(1)}, u32[]{:S(2)}, u32[]{:S(2)}) collective-permute-start(bf16[64,256]{1,0:T(8,128)(2,1)S(1)} %get-tuple-element.53), channel_id=1, source_target_pairs={{0,2},{1,3},{2,0},{3,1},{4,6},{5,7},{6,4},{7,5},{8,10},{9,11},{10,... | collective-permute-start | bytes 98312 | tf_op jit(solution)/shard_map/ppermute | solution.py:376
  106.0 2.2 %collective-permute-done.15.refs_2_ = bf16[64,256]{1,0:T(8,128)(2,1)S(1)} collective-permute-done((bf16[64,256]{1,0:T(8,128)(2,1)S(1)}, bf16[64,256]{1,0:T(8,128)(2,1)S(1)}, u32[]{:S(2)}, u32[]{:S(2)}) %collective-permute-start.15) | collective-permute-done | bytes 32800 | tf_op jit(solution)/shard_map/ppermute | solution.py:376
  108.2 1.4 %collective-permute-done.16.refs_3_ = bf16[64,256]{1,0:T(8,128)(2,1)S(1)} collective-permute-done((bf16[64,256]{1,0:T(8,128)(2,1)S(1)}, bf16[64,256]{1,0:T(8,128)(2,1)S(1)}, u32[]{:S(2)}, u32[]{:S(2)}) %collective-permute-start.16) | collective-permute-done | bytes 32800 | tf_op jit(solution)/shard_map/ppermute | solution.py:376
  109.6 2.1 %slide_next.1 = bf16[64,768]{1,0:T(8,128)(2,1)} custom-call(f32[64,768]{1,0:T(8,128)S(1)} %get-tuple-element.50.mine_ref, bf16[64,256]{1,0:T(8,128)(2,1)S(1)} %get-tuple-element.51.refs_0_, bf16[64,256]{1,0:T(8,128)(2,1)S(1)} %collective-permute-done.14.refs_1_, bf16[64,256]{1,0:T(8,128)(2,1)S(1)} %collective-permute-done.15.refs_2_, ...), custom_call_target="tpu_custom_call" | custom-call | tf_op jit(solution)/shard_map/slide_next/pallas_call | solution.py:525
  (86 shorter events, 2.5 us)
Async XLA Ops:
  0.0 1.1 %copy-start = (bf16[1,257,1536]{2,1,0:T(8,128)(2,1)S(1)}, bf16[1,257,1536]{2,1,0:T(8,128)(2,1)}, u32[]{:S(2)}) copy-start(bf16[1,257,1536]{2,1,0:T(8,128)(2,1)} %patch_ref.3) | copy-start | bytes 2368516
  3.2 15.1 %copy-start.2 = (bf16[768,192]{0,1:T(8,128)(2,1)S(1)}, bf16[768,192]{0,1:T(8,128)(2,1)}, u32[]{:S(2)}) copy-start(bf16[768,192]{0,1:T(8,128)(2,1)} %param.35) | copy-start | bytes 884740
  3.2 15.1 %copy-start.3 = (bf16[768,192]{0,1:T(8,128)(2,1)S(1)}, bf16[768,192]{0,1:T(8,128)(2,1)}, u32[]{:S(2)}) copy-start(bf16[768,192]{0,1:T(8,128)(2,1)} %param.36) | copy-start | bytes 884740
  3.2 15.2 %copy-start.5 = (bf16[768,192]{0,1:T(8,128)(2,1)S(1)}, bf16[768,192]{0,1:T(8,128)(2,1)}, u32[]{:S(2)}) copy-start(bf16[768,192]{0,1:T(8,128)(2,1)} %param.37) | copy-start | bytes 884740
  4.6 22.8 %collective-permute-start.3 = (bf16[192,1536]{1,0:T(8,128)(2,1)}, bf16[192,1536]{1,0:T(8,128)(2,1)}, u32[]{:S(2)}, u32[]{:S(2)}) collective-permute-start(bf16[192,1536]{1,0:T(8,128)(2,1)} %bitcast.refs_0_), channel_id=1, source_target_pairs={{0,2},{1,3},{2,0},{3,1},{4,6},{5,7},{6,4},{7,5},{8,10},{9,11},{10,... | collective-permute-start | bytes 1769480 | tf_op jit(solution)/shard_map/ppermute | solution.py:376
  7.6 19.9 %collective-permute-start.4 = (bf16[192,768]{1,0:T(8,128)(2,1)}, bf16[192,768]{1,0:T(8,128)(2,1)S(1)}, u32[]{:S(2)}, u32[]{:S(2)}) collective-permute-start(bf16[192,768]{1,0:T(8,128)(2,1)} %refs_4_), channel_id=1, source_target_pairs={{0,2},{1,3},{2,0},{3,1},{4,6},{5,7},{6,4},{7,5},{8,10},{9,11},{10,... | collective-permute-start | bytes 884744 | tf_op jit(solution)/shard_map/ppermute | solution.py:376
  7.6 19.1 %collective-permute-start.2 = (bf16[192,384]{1,0:T(8,128)(2,1)}, bf16[192,384]{1,0:T(8,128)(2,1)S(1)}, u32[]{:S(2)}, u32[]{:S(2)}) collective-permute-start(bf16[192,384]{1,0:T(8,128)(2,1)} %refs_0_), channel_id=1, source_target_pairs={{0,24},{4,28},{8,16},{12,20},{16,8},{20,12},{24,0},{28,4},{1,25},{... | collective-permute-start | bytes 442376 | tf_op jit(solution)/shard_map/ppermute | solution.py:376
  11.7 15.0 %collective-permute-start.1 = (bf16[192,384]{1,0:T(8,128)(2,1)}, bf16[192,384]{1,0:T(8,128)(2,1)S(1)}, u32[]{:S(2)}, u32[]{:S(2)}) collective-permute-start(bf16[192,384]{1,0:T(8,128)(2,1)} %refs_0_), channel_id=1, source_target_pairs={{0,16},{4,20},{8,24},{12,28},{16,0},{20,4},{24,8},{28,12},{1,17},{... | collective-permute-start | bytes 442376 | tf_op jit(solution)/shard_map/ppermute | solution.py:376
  11.7 15.1 %collective-permute-start = (bf16[192,384]{1,0:T(8,128)(2,1)}, bf16[192,384]{1,0:T(8,128)(2,1)S(1)}, u32[]{:S(2)}, u32[]{:S(2)}) collective-permute-start(bf16[192,384]{1,0:T(8,128)(2,1)} %refs_0_), channel_id=1, source_target_pairs={{0,8},{4,12},{8,0},{12,4},{16,24},{20,28},{24,16},{28,20},{1,9},{5... | collective-permute-start | bytes 442376 | tf_op jit(solution)/shard_map/ppermute | solution.py:376
  12.3 13.7 %all-to-all-start = ((f32[8,8,256]{2,1,0:T(8,128)}), f32[8,8,256]{2,1,0:T(8,128)S(1)}, u32[]{:S(2)}, u32[]{:S(2)}) async-start(f32[8,8,256]{2,1,0:T(8,128)} %class_row.1), calls=%async_computation | async-start | bytes 131072 | tf_op jit(solution)/shard_map/all_to_all | solution.py:416
  18.3 1.0 copy-start.16
  21.4 4.5 %copy-start.22 = (bf16[192,384]{1,0:T(8,128)(2,1)S(1)}, bf16[192,384]{1,0:T(8,128)(2,1)}, u32[]{:S(2)}) copy-start(bf16[192,384]{1,0:T(8,128)(2,1)} %wq_ref.1) | copy-start | bytes 442372
  21.4 29.0 %copy-start.23 = (bf16[192,384]{1,0:T(8,128)(2,1)S(1)}, bf16[192,384]{1,0:T(8,128)(2,1)}, u32[]{:S(2)}) copy-start(bf16[192,384]{1,0:T(8,128)(2,1)} %wk_ref.1) | copy-start | bytes 442372
  23.0 28.3 %copy-start.20 = (bf16[256,384]{1,0:T(8,128)(2,1)}, bf16[256,384]{1,0:T(8,128)(2,1)S(1)}, u32[]{:S(2)}) copy-start(bf16[256,384]{1,0:T(8,128)(2,1)S(1)} %get-tuple-element.39.refs_0_) | copy-start | bytes 589828
  26.7 37.1 %copy-start.1 = (bf16[1,257,1536]{2,1,0:T(8,128)(2,1)S(1)}, bf16[1,257,1536]{2,1,0:T(8,128)(2,1)}, u32[]{:S(2)}) copy-start(bf16[1,257,1536]{2,1,0:T(8,128)(2,1)} %patch_ref.3) | copy-start | bytes 2368516
  26.7 37.1 %copy-start.27 = (f32[1536]{0:T(1024)S(1)}, f32[1536]{0:T(1024)}, u32[]{:S(2)}) copy-start(f32[1536]{0:T(1024)} %gain_ref.6) | copy-start | bytes 18436
  26.7 37.1 %copy-start.32 = (f32[1536]{0:T(1024)S(1)}, f32[1536]{0:T(1024)}, u32[]{:S(2)}) copy-start(f32[1536]{0:T(1024)} %scale_ref.1) | copy-start | bytes 18436
  26.7 37.2 %copy-start.38 = (f32[192]{0:T(256)S(1)}, f32[192]{0:T(256)}, u32[]{:S(2)}) copy-start(f32[192]{0:T(256)} %bias_ref.1) | copy-start | bytes 2308
  27.4 23.9 %copy-start.18 = (bf16[192,768]{1,0:T(8,128)(2,1)}, bf16[192,768]{1,0:T(8,128)(2,1)S(1)}, u32[]{:S(2)}) copy-start(bf16[192,768]{1,0:T(8,128)(2,1)S(1)} %collective-permute-done.4.refs_6_) | copy-start | bytes 884740
  27.4 36.4 %collective-permute-start.9 = (bf16[576,384]{1,0:T(8,128)(2,1)S(1)}, bf16[576,384]{1,0:T(8,128)(2,1)S(1)}, u32[]{:S(2)}, u32[]{:S(2)}) collective-permute-start(bf16[576,384]{1,0:T(8,128)(2,1)S(1)} %pad_maximum_fusion.1.refs_1_), channel_id=1, source_target_pairs={{0,4},{4,0},{8,12},{12,8},{16,20},{20,16},{24,28},{28,24},{1,5},{5... | collective-permute-start | bytes 1327112 | tf_op jit(solution)/shard_map/ppermute | solution.py:376
  29.2 22.1 %collective-permute-start.7 = (bf16[256,384]{1,0:T(8,128)(2,1)S(1)}, bf16[256,384]{1,0:T(8,128)(2,1)S(1)}, u32[]{:S(2)}, u32[]{:S(2)}) collective-permute-start(bf16[256,384]{1,0:T(8,128)(2,1)S(1)} %get-tuple-element.39.refs_0_), channel_id=1, source_target_pairs={{0,24},{4,28},{8,16},{12,20},{16,8},{20,12},{24,0},{28,4},{1,25},{... | collective-permute-start | bytes 589832 | tf_op jit(solution)/shard_map/ppermute | solution.py:376
  32.8 18.5 %collective-permute-start.6 = (bf16[256,384]{1,0:T(8,128)(2,1)S(1)}, bf16[256,384]{1,0:T(8,128)(2,1)S(1)}, u32[]{:S(2)}, u32[]{:S(2)}) collective-permute-start(bf16[256,384]{1,0:T(8,128)(2,1)S(1)} %get-tuple-element.39.refs_0_), channel_id=1, source_target_pairs={{0,16},{4,20},{8,24},{12,28},{16,0},{20,4},{24,8},{28,12},{1,17},{... | collective-permute-start | bytes 589832 | tf_op jit(solution)/shard_map/ppermute | solution.py:376
  32.8 18.5 %collective-permute-start.5 = (bf16[256,384]{1,0:T(8,128)(2,1)S(1)}, bf16[256,384]{1,0:T(8,128)(2,1)}, u32[]{:S(2)}, u32[]{:S(2)}) collective-permute-start(bf16[256,384]{1,0:T(8,128)(2,1)S(1)} %get-tuple-element.39.refs_0_), channel_id=1, source_target_pairs={{0,8},{4,12},{8,0},{12,4},{16,24},{20,28},{24,16},{28,20},{1,9},{5... | collective-permute-start | bytes 589832 | tf_op jit(solution)/shard_map/ppermute | solution.py:376
  33.6 16.9 %all-to-all-start.1 = ((f32[8,8,384]{2,1,0:T(8,128)}), f32[8,8,384]{2,1,0:T(8,128)S(1)}, u32[]{:S(2)}, u32[]{:S(2)}) async-start(f32[8,8,384]{2,1,0:T(8,128)} %query_share.1), calls=%async_computation.1 | async-start | bytes 196608 | tf_op jit(solution)/shard_map/all_to_all | solution.py:446
  38.5 20.9 %collective-permute-start.8 = (bf16[192,384]{1,0:T(8,128)(2,1)}, bf16[192,384]{1,0:T(8,128)(2,1)}, u32[]{:S(2)}, u32[]{:S(2)}) collective-permute-start(bf16[192,384]{1,0:T(8,128)(2,1)} %refs_0_), channel_id=1, source_target_pairs={{0,4},{4,0},{8,12},{12,8},{16,20},{20,16},{24,28},{28,24},{1,5},{5... | collective-permute-start | bytes 442376 | tf_op jit(solution)/shard_map/ppermute | solution.py:376
  52.3 30.8 %copy-start.28 = (s32[5,12]{1,0:T(8,128)S(1)}, s32[5,12]{1,0:T(8,128)}, u32[]{:S(2)}) copy-start(s32[5,12]{1,0:T(8,128)} %offset_ref.3) | copy-start | bytes 724
  52.3 30.8 %copy-start.34 = (s32[8]{0:T(128)S(1)}, s32[8]{0:T(128)}, u32[]{:S(2)}) copy-start(s32[8]{0:T(128)} %pos_ref.5) | copy-start | bytes 100
  52.3 11.5 %all-to-all-start.2 = ((f32[8,8,256]{2,1,0:T(8,128)}), f32[8,8,256]{2,1,0:T(8,128)S(1)}, u32[]{:S(2)}, u32[]{:S(2)}) async-start(f32[8,8,256]{2,1,0:T(8,128)} %fold_key.1), calls=%async_computation.2 | async-start | bytes 131072 | tf_op jit(solution)/shard_map/all_to_all | solution.py:465
  56.8 25.4 %collective-permute-start.11 = (bf16[768,384]{1,0:T(8,128)(2,1)S(1)}, bf16[768,384]{1,0:T(8,128)(2,1)S(1)}, u32[]{:S(2)}, u32[]{:S(2)}) collective-permute-start(bf16[768,384]{1,0:T(8,128)(2,1)S(1)} %pad_maximum_fusion.refs_1_), channel_id=1, source_target_pairs={{0,4},{4,0},{8,12},{12,8},{16,20},{20,16},{24,28},{28,24},{1,5},{5... | collective-permute-start | bytes 1769480 | tf_op jit(solution)/shard_map/ppermute | solution.py:376
  58.9 34.3 %collective-permute-start.12 = (bf16[192,1536]{1,0:T(8,128)(2,1)}, bf16[192,1536]{1,0:T(8,128)(2,1)}, u32[]{:S(2)}, u32[]{:S(2)}) collective-permute-start(bf16[192,1536]{1,0:T(8,128)(2,1)} %bitcast.refs_0_), channel_id=1, source_target_pairs={{0,1},{1,0},{2,3},{3,2},{4,5},{5,4},{6,7},{7,6},{8,9},{9,8},{10,11... | collective-permute-start | bytes 1769480 | tf_op jit(solution)/shard_map/ppermute | solution.py:376
  58.9 34.3 %collective-permute-start.13 = (bf16[192,1536]{1,0:T(8,128)(2,1)}, bf16[192,1536]{1,0:T(8,128)(2,1)}, u32[]{:S(2)}, u32[]{:S(2)}) collective-permute-start(bf16[192,1536]{1,0:T(8,128)(2,1)} %collective-permute-done.3.refs_2_), channel_id=1, source_target_pairs={{0,1},{1,0},{2,3},{3,2},{4,5},{5,4},{6,7},{7,6},{8,9},{9,8},{10,11... | collective-permute-start | bytes 1769480 | tf_op jit(solution)/shard_map/ppermute | solution.py:376
  63.9 1.3 %copy-start.7 = (bf16[384,1536]{1,0:T(8,128)(2,1)S(1)}, bf16[384,1536]{1,0:T(8,128)(2,1)}, u32[]{:S(2)}) copy-start(bf16[384,1536]{1,0:T(8,128)(2,1)} %wo_ref.1) | copy-start | bytes 3538948
  65.2 28.1 %copy-start.30 = (f32[768]{0:T(1024)S(1)}, f32[768]{0:T(1024)}, u32[]{:S(2)}) copy-start(f32[768]{0:T(1024)} %gain_ref.7) | copy-start | bytes 9220
  65.2 28.1 %copy-start.31 = (f32[1536]{0:T(1024)S(1)}, f32[1536]{0:T(1024)}, u32[]{:S(2)}) copy-start(f32[1536]{0:T(1024)} %final_ref.1) | copy-start | bytes 18436
  69.3 24.0 %copy-start.4 = (bf16[768,192]{0,1:T(8,128)(2,1)S(1)}, bf16[768,192]{0,1:T(8,128)(2,1)}, u32[]{:S(2)}) copy-start(bf16[768,192]{0,1:T(8,128)(2,1)} %param.36) | copy-start | bytes 884740
  69.3 24.0 %copy-start.6 = (bf16[768,192]{0,1:T(8,128)(2,1)S(1)}, bf16[768,192]{0,1:T(8,128)(2,1)}, u32[]{:S(2)}) copy-start(bf16[768,192]{0,1:T(8,128)(2,1)} %param.37) | copy-start | bytes 884740
  69.3 23.9 %all-to-all-start.3 = ((f32[32,8,256]{2,1,0:T(8,128)}), f32[32,8,256]{2,1,0:T(8,128)}, u32[]{:S(2)}, u32[]{:S(2)}) async-start(f32[32,8,256]{2,1,0:T(8,128)} %tile_attention.1), calls=%async_computation.3 | async-start | bytes 524288 | tf_op jit(solution)/shard_map/all_to_all | solution.py:482
  72.9 9.3 %collective-permute-start.10 = (bf16[256,384]{1,0:T(8,128)(2,1)}, bf16[256,384]{1,0:T(8,128)(2,1)S(1)}, u32[]{:S(2)}, u32[]{:S(2)}) collective-permute-start(bf16[256,384]{1,0:T(8,128)(2,1)} %copy-done.20), channel_id=1, source_target_pairs={{0,4},{4,0},{8,12},{12,8},{16,20},{20,16},{24,28},{28,24},{1,5},{5... | collective-permute-start | bytes 589832 | tf_op jit(solution)/shard_map/ppermute | solution.py:376
  74.4 31.6 %collective-permute-start.17 = (bf16[192,768]{1,0:T(8,128)(2,1)}, bf16[192,768]{1,0:T(8,128)(2,1)}, u32[]{:S(2)}, u32[]{:S(2)}) collective-permute-start(bf16[192,768]{1,0:T(8,128)(2,1)} %refs_4_), channel_id=1, source_target_pairs={{0,1},{1,0},{2,3},{3,2},{4,5},{5,4},{6,7},{7,6},{8,9},{9,8},{10,11... | collective-permute-start | bytes 884744 | tf_op jit(solution)/shard_map/ppermute | solution.py:376
  82.2 23.8 %collective-permute-start.18 = (bf16[192,768]{1,0:T(8,128)(2,1)}, bf16[192,768]{1,0:T(8,128)(2,1)}, u32[]{:S(2)}, u32[]{:S(2)}) collective-permute-start(bf16[192,768]{1,0:T(8,128)(2,1)} %copy-done.18), channel_id=1, source_target_pairs={{0,1},{1,0},{2,3},{3,2},{4,5},{5,4},{6,7},{7,6},{8,9},{9,8},{10,11... | collective-permute-start | bytes 884744 | tf_op jit(solution)/shard_map/ppermute | solution.py:376
  83.1 1.1 copy-start.11
  93.3 1.1 %copy-start.9 = (f32[768,256]{1,0:T(8,128)S(1)}, f32[768,256]{1,0:T(8,128)}, u32[]{:S(2)}) copy-start(f32[768,256]{1,0:T(8,128)} %copy-done.8) | copy-start | bytes 2359300
  94.4 1.0 copy-start.13
  97.3 12.4 %copy-start.17 = (bf16[192,768]{1,0:T(8,128)(2,1)S(1)}, bf16[192,768]{1,0:T(8,128)(2,1)}, u32[]{:S(2)}) copy-start(bf16[192,768]{1,0:T(8,128)(2,1)} %refs_4_) | copy-start | bytes 884740
  97.3 12.4 %copy-start.19 = (bf16[192,768]{1,0:T(8,128)(2,1)S(1)}, bf16[192,768]{1,0:T(8,128)(2,1)}, u32[]{:S(2)}) copy-start(bf16[192,768]{1,0:T(8,128)(2,1)} %copy-done.18) | copy-start | bytes 884740
  103.7 2.3 %collective-permute-start.14 = (bf16[64,256]{1,0:T(8,128)(2,1)S(1)}, bf16[64,256]{1,0:T(8,128)(2,1)S(1)}, u32[]{:S(2)}, u32[]{:S(2)}) collective-permute-start(bf16[64,256]{1,0:T(8,128)(2,1)S(1)} %get-tuple-element.52), channel_id=1, source_target_pairs={{0,1},{1,0},{2,3},{3,2},{4,5},{5,4},{6,7},{7,6},{8,9},{9,8},{10,11... | collective-permute-start | bytes 98312 | tf_op jit(solution)/shard_map/ppermute | solution.py:376
  104.3 3.9 %collective-permute-start.15 = (bf16[64,256]{1,0:T(8,128)(2,1)S(1)}, bf16[64,256]{1,0:T(8,128)(2,1)S(1)}, u32[]{:S(2)}, u32[]{:S(2)}) collective-permute-start(bf16[64,256]{1,0:T(8,128)(2,1)S(1)} %get-tuple-element.53), channel_id=1, source_target_pairs={{0,2},{1,3},{2,0},{3,1},{4,6},{5,7},{6,4},{7,5},{8,10},{9,11},{10,... | collective-permute-start | bytes 98312 | tf_op jit(solution)/shard_map/ppermute | solution.py:376
  106.0 3.7 %collective-permute-start.16 = (bf16[64,256]{1,0:T(8,128)(2,1)S(1)}, bf16[64,256]{1,0:T(8,128)(2,1)S(1)}, u32[]{:S(2)}, u32[]{:S(2)}) collective-permute-start(bf16[64,256]{1,0:T(8,128)(2,1)S(1)} %get-tuple-element.54), channel_id=1, source_target_pairs={{0,3},{1,2},{2,1},{3,0},{4,7},{5,6},{6,5},{7,4},{8,11},{9,10},{10,... | collective-permute-start | bytes 98312 | tf_op jit(solution)/shard_map/ppermute | solution.py:376
  (14 other events, 10.8 us)

commit v4 on v3

--- a/solution.py
+++ b/solution.py
@@ -125,13 +125,17 @@
         fold_ref[:, :, cut:] = jnp.zeros((tiles, 8, fold_ref.shape[2] - cut), F32)
 
 
-def tile_kernel(cut, patch_ref, gain_ref, fold_ref, scale_ref, bias_ref, wo_ref, *refs):
-    *wv_refs, sent_ref, fold_s, mixed_s = refs
+def token_kernel(patch_ref, gain_ref, normed_ref):
+    tokens = patch_ref[0].astype(F32)
+    normed_ref[...] = layer_norm(tokens, gain_ref[...].reshape(1, DV)).astype(BF16)
+
+
+def tile_kernel(cut, patch_ref, normed_ref, fold_ref, scale_ref, bias_ref, wo_ref, *refs):
+    *wv_refs, sent_ref, fold_s, mixed_s, share_s = refs
     parts = fold_ref.shape[0]
     for part in range(parts):
         fold_s[:, part * cut : (part + 1) * cut] = fold_ref[part, :, 0:cut]
-    tokens = patch_ref[0].astype(F32)
-    normed = layer_norm(tokens, gain_ref[...].reshape(1, DV)).astype(BF16)
+    normed = normed_ref[...]
     scores = dot_nt(fold_s[...].astype(BF16), normed) * (1.0 / math.sqrt(HEAD))
     highest = jnp.max(scores, axis=-1, keepdims=True)
     exponent = jnp.exp(scores - highest)
@@ -153,15 +157,17 @@
     tmix = jnp.sum(jnp.where(lane // HEAD == head, values, 0.0), axis=0, keepdims=True)
     tmix = jnp.broadcast_to(tmix, (8, tmix.shape[1])).astype(BF16)
     share = dot(tmix, wo_ref[...])[0:1] * scale_ref[...].reshape(1, DV)
-    share = share + jnp.where(lax.axis_index("seg") == 0, tokens[0:1], 0.0)
-    devices = sent_ref.shape[0]
-    for row in range(DV // 256):
-        piece = share[:, None, row * 256 : (row + 1) * 256]
-        sent_ref[:, row : row + 1, :] = jnp.broadcast_to(piece, (devices, 1, 256))
-    width = bias_ref.shape[0]
-    bias = bias_ref[...].reshape(1, 1, width)
-    sent_ref[:, 6:8, :] = jnp.zeros((devices, 2, 256), F32)
-    sent_ref[:, 6:7, 0:width] = jnp.broadcast_to(bias, (devices, 1, width))
+    class_token = patch_ref[0, 0:1].astype(F32)
+    share = share + jnp.where(lax.axis_index("seg") == 0, class_token, 0.0)
+    share_s[...] = jnp.zeros_like(share_s)
+    for row in range(DV // 128):
+        share_s[row : row + 1, :] = share[:, row * 128 : (row + 1) * 128]
+    bias = bias_ref[...].reshape(1, 192)
+    high = bias.astype(BF16).astype(F32)
+    for row, term in ((12, high), (14, bias - high)):
+        share_s[row : row + 1, :] = term[:, 0:128]
+        share_s[row + 1 : row + 2, 0:64] = term[:, 128:192]
+    sent_ref[...] = jnp.broadcast_to(share_s[...].astype(BF16)[None], sent_ref.shape)
 
 
 def branch_rows(position, axis, offset_ref, span, total):
@@ -194,8 +200,8 @@
 
 
 def attend(q, q_rows, kv_ref, k_rows):
-    scores = dot_nt(stack_heads(q, HEAD), kv_ref[:, 0:256])
-    count = dot(stack_heads(as_bf16(q_rows), 8), k_rows)
+    scores = dot_nt(q, kv_ref[:, 0:256])
+    count = dot(q_rows, k_rows)
     scores = jnp.where(count > 0.5, scores, LOW)
     highest = jnp.max(scores, axis=-1, keepdims=True)
     weight = jnp.exp(scores - highest) * count
@@ -215,29 +221,35 @@
 
 def clear_state(ml_ref, acc_ref):
     lane = lax.broadcasted_iota(I32, ml_ref.shape, 1)
-    ml_ref[...] = jnp.where(lane == 0, LOW, 0.0)
+    ml_ref[...] = jnp.where(lane < 8, LOW, 0.0)
     acc_ref[...] = jnp.zeros_like(acc_ref)
 
 
-def store_state(state, ml_ref, acc_ref):
-    highest, denom, numer = state
+def add_state(new, head, ml_ref, acc_ref):
+    old = ml_ref[:, head : head + 1], ml_ref[:, head + 8 : head + 9], acc_ref[...]
+    top, den, num = merge(old, new)
     lane = lax.broadcasted_iota(I32, ml_ref.shape, 1)
-    ml_ref[...] = jnp.where(lane == 0, highest, denom)
-    acc_ref[...] = numer
-
-
-def load_state(ml_ref, acc_ref):
-    return ml_ref[:, 0:1], ml_ref[:, 1:2], acc_ref[...]
-
-
-def finish(state):
-    _, den, num = state
-    result = num / jnp.where(den > 0.0, den, 1.0)
-    rows = num.shape[0] // 3
-    group = lax.broadcasted_iota(I32, (1, 256), 1) // HEAD
-    joined = jnp.where(group == 1, result[2 * rows :], 0.0)
-    joined = jnp.where(group == 2, result[0:rows], joined)
-    return jnp.where(group == 3, result[rows : 2 * rows], joined)
+    ml_ref[...] = jnp.where(lane == head, top, jnp.where(lane == head + 8, den, ml_ref[...]))
+    acc_ref[...] = jnp.where(value_lanes(head), num, acc_ref[...])
+
+
+def add_stacked(new, ml_ref, acc_ref):
+    rows = acc_ref.shape[0]
+    for head in range(3):
+        add_state([x[head * rows : (head + 1) * rows] for x in new], head, ml_ref, acc_ref)
+
+
+def value_lanes(head):
+    return lax.broadcasted_iota(I32, (1, 256), 1) // HEAD == (2, 3, 1)[head]
+
+
+def finish(ml_ref, acc_ref):
+    result = jnp.zeros(acc_ref.shape, F32)
+    for head in range(3):
+        den = ml_ref[:, head + 8 : head + 9]
+        den = jnp.where(den > 0.0, den, 1.0)
+        result = jnp.where(value_lanes(head), acc_ref[...] / den, result)
+    return result
 
 
 def fresh_places(padded, pack_ref, pos_ref):
@@ -255,12 +267,13 @@
     return row, col, flags[:, 0:padded] > 0.5, flag_col > 0.5
 
 
-def key_places(swapped, block, span, step):
+def key_places(masks, block, span, step):
     place = lax.broadcasted_iota(I32, (1, block), 1)
-    if not swapped:
+    if masks is None:
         return place + step * block
-    part = place // span
-    mask = jnp.where(part < 4, 2 * part, 2 * part - 7)
+    mask = jnp.zeros_like(place)
+    for index, value in enumerate(masks):
+        mask = jnp.where(place // span == index, value, mask)
     return (lax.axis_index("tile") ^ mask) * span + (place & (span - 1))
 
 
@@ -271,54 +284,59 @@
     return as_bf16(rows & (taken < 0.5))
 
 
-def base_attention_kernel(span, total, padded, pos_ref, offset_ref, pack_ref, q_ref, *refs):
-    *kv_refs, krows_ref, ml_ref, acc_ref = refs
-    swapped = len(kv_refs) > 1
-    kv_ref = kv_refs.pop()
+def base_attention_kernel(
+    span, total, padded, groups, state, pos_ref, offset_ref, pack_ref, q_ref, *refs
+):
+    kv_refs, refs = refs[: len(groups)], refs[len(groups) :]
+    ml_ref, acc_ref = refs[-2:]
     step = pl.program_id(0)
     rows = q_ref.shape[0]
-    block = kv_ref.shape[0]
 
     @pl.when(step == 0)
     def _():
-        clear_state(ml_ref, acc_ref)
-
-    start = 0
-    for ref in kv_refs:
-        kv_ref[start : start + ref.shape[0], :] = ref[...]
-        start += ref.shape[0]
+        if state:
+            ml_ref[...] = refs[0][...]
+            acc_ref[...] = refs[1][...]
+        else:
+            clear_state(ml_ref, acc_ref)
+
     _, pos_col, _, flag_col = fresh_places(padded, pack_ref, pos_ref)
     place = lax.broadcasted_iota(I32, (rows, 1), 0) + lax.axis_index("tile") * span
-    q_rows = branch_rows(place, 1, offset_ref, span, total)
-    keys = key_places(swapped, block, span, step)
-    k_rows = key_rows(keys, pos_col, flag_col, offset_ref, span, total)
-    krows_ref[...] = k_rows
-    new = attend(q_ref[...], q_rows, kv_ref, k_rows)
-    store_state(merge(load_state(ml_ref, acc_ref), new), ml_ref, acc_ref)
+    q_rows = as_bf16(branch_rows(place, 1, offset_ref, span, total))
+    q = q_ref[...]
+    lane = lax.broadcasted_iota(I32, (1, 256), 1)
+    branch = lax.broadcasted_iota(I32, (1, 24), 1)
+    for masks, kv_ref in zip(groups, kv_refs):
+        keys = key_places(masks, kv_ref.shape[0], span, step)
+        k_rows = key_rows(keys, pos_col, flag_col, offset_ref, span, total)
+        for head in range(3):
+            q_head = jnp.where(lane // HEAD == head, q, jnp.zeros_like(q))
+            r_head = jnp.where(branch // 8 == head, q_rows, jnp.zeros_like(q_rows))
+            add_state(attend(q_head, r_head, kv_ref, k_rows), head, ml_ref, acc_ref)
 
 
 def fresh_kernel(
-    span, total, pos_ref, offset_ref, pack_ref, q_ref, shares_ref, final_ref, gain_ref,
+    span, total, groups, pos_ref, offset_ref, pack_ref, q_ref, shares_ref, final_ref, gain_ref,
     wq_ref, wk_ref, wv_ref, ml_ref, acc_ref, rows_ref, *refs,
 ):
     embed_refs, refs = refs[:4], refs[4:]
-    kv_ref, krows_ref, *refs = refs
+    kv_refs, refs = refs[: len(groups)], refs[len(groups) :]
     outs, refs = refs[:4], refs[4:]
-    mine_ref, fresh_s, qf_s, kvf_s, mlf_s, accf_s, att_s = refs
+    mine_ref, fresh_s, qf_s, kvf_s, mlf_s, accf_s, mlb_s, att_s = refs
     step = pl.program_id(0)
     rows = q_ref.shape[0]
     padded = fresh_s.shape[0]
     seg = lax.axis_index("seg")
     pos_row, pos_col, flag_row, flag_col = fresh_places(padded, pack_ref, pos_ref)
-    f_rows = branch_rows(pos_col, 1, offset_ref, span, total)
+    f_rows = stack_heads(as_bf16(branch_rows(pos_col, 1, offset_ref, span, total)), 8)
 
     @pl.when(step == 0)
     def _():
-        groups = shares_ref.shape[0] // 4
-        pooled = []
-        for row in range(DV // 256):
-            pooled.append(jnp.sum(shares_ref[:, row, :].reshape(groups, 4, 256), axis=1))
-        pooled = jnp.concatenate(pooled, axis=1)
+        tiles = shares_ref.shape[0] // 4
+        shares = shares_ref[...].astype(F32)
+        bias = shares[0:4]
+        summed = jnp.sum(shares.reshape(tiles, 4, 16, 128), axis=1)
+        pooled = jnp.concatenate([summed[:, row, :] for row in range(DV // 128)], axis=1)
         summary = layer_norm(pooled, final_ref[...].reshape(1, DV)).astype(BF16)
         fresh_s[...] = jnp.zeros_like(fresh_s)
         pieces = [dot_nt(summary, ref[...]) for ref in embed_refs]
@@ -326,25 +344,33 @@
             piece = pieces[0]
             for mask in range(1, 4):
                 piece = jnp.where((seg ^ part) == mask, pieces[mask], piece)
-            piece = piece + shares_ref[part, 6:7, 0:192]
-            fresh_s[0:groups, part * 192 : (part + 1) * 192] = piece.astype(BF16).astype(F32)
+            own = bias[part]
+            own = own[12:14] + own[14:16]
+            own = jnp.concatenate([own[0:1], own[1:2, 0:64]], axis=1)
+            piece = (piece + own).astype(BF16).astype(F32)
+            fresh_s[0:tiles, part * 192 : (part + 1) * 192] = piece
         normed = layer_norm(fresh_s[...], gain_ref[...].reshape(1, DS)).astype(BF16)
         project(normed, wq_ref, wk_ref, wv_ref, qf_s, kvf_s)
         clear_state(mlf_s, accf_s)
 
-    new = attend(qf_s[...], f_rows, kv_ref, krows_ref[...])
-    store_state(merge(load_state(mlf_s, accf_s), new), mlf_s, accf_s)
+    qf = stack_heads(qf_s[...], HEAD)
+    for masks, kv_ref in zip(groups, kv_refs):
+        keys = key_places(masks, kv_ref.shape[0], span, step)
+        k_rows = key_rows(keys, pos_col, flag_col, offset_ref, span, total)
+        add_stacked(attend(qf, f_rows, kv_ref, k_rows), mlf_s, accf_s)
 
     @pl.when(step == pl.num_programs(0) - 1)
     def _():
         first = lax.axis_index("tile") * span
         place = lax.broadcasted_iota(I32, (rows, 1), 0) + first
-        q_rows = branch_rows(place, 1, offset_ref, span, total)
+        q_rows = stack_heads(as_bf16(branch_rows(place, 1, offset_ref, span, total)), 8)
         k_rows = as_bf16(branch_rows(pos_row, 0, offset_ref, span, total) & flag_row)
-        new = attend(q_ref[...], q_rows, kvf_s, k_rows)
-        base = finish(merge(load_state(ml_ref, acc_ref), new))
-        new = attend(qf_s[...], f_rows, kvf_s, k_rows)
-        fresh = finish(merge(load_state(mlf_s, accf_s), new))
+        mlb_s[...] = ml_ref[...]
+        att_s[...] = acc_ref[...]
+        add_stacked(attend(stack_heads(q_ref[...], HEAD), q_rows, kvf_s, k_rows), mlb_s, att_s)
+        base = finish(mlb_s, att_s)
+        add_stacked(attend(qf, f_rows, kvf_s, k_rows), mlf_s, accf_s)
+        fresh = finish(mlf_s, accf_s)
         chosen = as_bf16((place == pos_row) & flag_row)
         hit = jnp.sum(chosen.astype(F32), axis=1, keepdims=True) > 0.5
         att_s[...] = jnp.where(hit, dot(chosen, fresh.astype(BF16)), base)
@@ -408,11 +434,10 @@
         grid=(1,),
         in_specs=[pl.BlockSpec((1, 16, DV), lambda i: (0, 0, 0)), VMEM, SMEM, VMEM],
         out_specs=VMEM,
-        compiler_params=params(8),
+        compiler_params=params(60),
         name="class_row",
     )(patches, vit_norm_gain, slide_pos, kept)
-
-    pack, value, cached, embed, slide_out = together(pack, vit_value, cached, embed, slide_out)
+    pack, cached = together(pack, cached)
     pack = lax.all_to_all(pack, "tile", 0, 0, tiled=True)
     base_rows, q_base, kv_base = call(
         base_kernel,
@@ -422,12 +447,12 @@
         compiler_params=params(16),
         name="base_rows",
     )(cached, kept, mask_token, slide_gain, *weights)
+    value = vit_value
     if small:
-        value_z = [trade(value, "tile", mask) for mask in (2, 4, 6)]
+        kv_base, value = together(kv_base, value)
+        value_z = jnp.concatenate([trade(value, "tile", mask) for mask in GROUPS[1]], axis=0)
         value_y = trade(value, "tile", 1)
         kv_y = trade(kv_base, "tile", 1)
-    embed_x = trade(embed, "seg", 2)
-    out_x = trade(slide_out, "seg", 2)
 
     part_shape = (tiles, fresh, local_cols) if small else (fresh, local_cols)
     part = call(
@@ -438,19 +463,26 @@
         compiler_params=params(8 if small else 16),
         name="query_share",
     )(pack, vit_query)
+    part, patches = together(part, patches)
     if small:
-        value_z = jnp.concatenate(value_z, axis=0)
-        part, value_z, kv_own, embed, embed_x, slide_out, out_x = together(
-            part, value_z, kv_base, embed, embed_x, slide_out, out_x
-        )
         part = lax.all_to_all(part, "tile", 0, 0, tiled=True)
-        kv_z = [trade(kv_own, "tile", mask) for mask in (2, 4, 6)]
-        wv_all = [value, value_z, value_y, trade(value_z, "tile", 1)]
     else:
         part = lax.psum(part, "tile")
+    normed = call(
+        token_kernel,
+        out_shape=sds(patches.shape[1:], BF16),
+        in_specs=[VMEM] * 2,
+        out_specs=VMEM,
+        compiler_params=params(12),
+        name="token_norm",
+    )(patches, vit_norm_gain)
+    if small:
+        normed, value_z, kv_own = together(normed, value_z, kv_base)
+        wv_all = [value, value_z, value_y, trade(value_z, "tile", 1)]
+        kv_z = jnp.concatenate([trade(kv_own, "tile", mask) for mask in GROUPS[1]], axis=0)
+    else:
         wv_all = [lax.all_gather(value, "tile", axis=0, tiled=True)]
-    embed_all = [embed, trade(embed, "seg", 1), embed_x, trade(embed_x, "seg", 1)]
-    slide_out_all = [slide_out, trade(slide_out, "seg", 1), out_x, trade(out_x, "seg", 1)]
+
     folded = call(
         fold_kernel,
         out_shape=sds((fresh, 8, round_up(cut, 128)), F32),
@@ -460,66 +492,75 @@
         name="fold_key",
     )(part, vit_key)
     if small:
-        kv_z = jnp.concatenate(kv_z, axis=0)
         folded, kv_z = together(folded, kv_z)
-        folded = lax.all_to_all(folded, "tile", 0, 0, tiled=True)
         kv_all = [kv_own, kv_z, kv_y, trade(kv_z, "tile", 1)]
+        groups = GROUPS
     else:
-        folded = lax.all_to_all(folded, "tile", 0, 0, tiled=True)
         kv_all = [lax.all_gather(kv_base, "tile", axis=0, tiled=True)]
+        groups = (None,)
+    folded = lax.all_to_all(folded, "tile", 0, 0, tiled=True)
+    block = min(total, 2048)
+    steps = 1 if small else total // block
+    kv_spec = VMEM if small else pl.BlockSpec((block, 384), lambda i: (i, 0))
+
+    def attention(blocks, picked, state):
+        return call(
+            functools.partial(
+                base_attention_kernel, span, total, padded, picked, len(state) > 0
+            ),
+            out_shape=(sds((span, 128), F32), sds((span, 256), F32)),
+            grid=(steps,),
+            in_specs=[SMEM, SMEM, VMEM, VMEM] + [kv_spec] * len(blocks) + [VMEM] * len(state),
+            out_specs=(VMEM, VMEM),
+            compiler_params=params(16 if small else 32),
+            name="base_attention",
+        )(slide_pos, offsets, pack, q_base, *blocks, *state)
+
+    state = attention(kv_all[:2], groups[:2], ())
+    state, embed, slide_out = together(state, embed, slide_out)
+    embed_x = trade(embed, "seg", 2)
+    out_x = trade(slide_out, "seg", 2)
 
     sent = call(
         functools.partial(tile_kernel, cut),
-        out_shape=sds((devices, 8, 256), F32),
+        out_shape=sds((devices, 16, 128), BF16),
         in_specs=[VMEM] * (6 + len(wv_all)),
         out_specs=VMEM,
         scratch_shapes=[
             pltpu.VMEM((8, DV), F32), pltpu.VMEM((tiles, 8, round_up(cut, 128)), F32),
+            pltpu.VMEM((16, 128), F32),
         ],
         compiler_params=params(16 if small else 32),
         name="tile_attention",
-    )(patches, vit_norm_gain, folded, layer_scale, embed_bias, vit_out, *wv_all)
+    )(patches, normed, folded, layer_scale, embed_bias, vit_out, *wv_all)
+    sent, state, embed_x, out_x = together(sent, state, embed_x, out_x)
     shares = lax.all_to_all(sent, ("tile", "seg"), 0, 0, tiled=True)
-
-    block = min(total, 2048)
-    steps = total // block
-    kv_spec = pl.BlockSpec((block, 384), lambda i: (i, 0))
-    krows_spec = pl.BlockSpec((24, block), lambda i: (0, i))
-    kv_shape = [sds((total, 384), BF16)] if small else []
-    *kv_sorted, krows, ml, acc = call(
-        functools.partial(base_attention_kernel, span, total, padded),
-        out_shape=(
-            *kv_shape, sds((24, total), BF16),
-            sds((3 * span, 128), F32), sds((3 * span, 256), F32),
-        ),
-        grid=(steps,),
-        in_specs=[SMEM, SMEM, VMEM, VMEM] + ([VMEM] * 4 if small else [kv_spec]),
-        out_specs=(*([kv_spec] if small else []), krows_spec, VMEM, VMEM),
-        compiler_params=params(40),
-        name="base_attention",
-    )(slide_pos, offsets, pack, q_base, *kv_all)
-    kv_sorted = kv_sorted[0] if small else kv_all[0]
+    if small:
+        state = attention(kv_all[2:], groups[2:], state)
+    embed_all = [embed, trade(embed, "seg", 1), embed_x, trade(embed_x, "seg", 1)]
+    slide_out_all = [slide_out, trade(slide_out, "seg", 1), out_x, trade(out_x, "seg", 1)]
 
     count = span // segs
     outs = call(
-        functools.partial(fresh_kernel, span, total),
+        functools.partial(fresh_kernel, span, total, groups),
         out_shape=(sds((count, 256), BF16),) * 4 + (sds((count, DS), F32),),
         grid=(steps,),
-        in_specs=[SMEM] * 2 + [VMEM] * 15 + [kv_spec, krows_spec],
+        in_specs=[SMEM] * 2 + [VMEM] * 15 + [kv_spec] * len(kv_all),
         out_specs=(VMEM,) * 5,
         scratch_shapes=[
             pltpu.VMEM((padded, DS), F32),
             pltpu.VMEM((padded, 256), BF16),
             pltpu.VMEM((padded, 384), BF16),
-            pltpu.VMEM((3 * padded, 128), F32),
-            pltpu.VMEM((3 * padded, 256), F32),
+            pltpu.VMEM((padded, 128), F32),
+            pltpu.VMEM((padded, 256), F32),
+            pltpu.VMEM((span, 128), F32),
             pltpu.VMEM((span, 256), F32),
         ],
-        compiler_params=params(24 if small else 48),
+        compiler_params=params(16 if small else 48),
         name="fresh_attention",
     )(
-        slide_pos, offsets, pack, q_base, shares, final_gain, slide_gain, *weights, ml, acc,
-        base_rows, *embed_all, kv_sorted, krows,
+        slide_pos, offsets, pack, q_base, shares, final_gain, slide_gain, *weights, *state,
+        base_rows, *embed_all, *kv_all,
     )
     swapped = [outs[0]] + [trade(outs[mask], "seg", mask) for mask in range(1, 4)]
     return call(

time: 113 us -> 124 us (1.097)
  blocking collectives: 0 us -> 32.3 us
  waiting for transfers between devices: 29.5 us -> 17 us
  starting transfers between devices: 41.2 us -> 29.5 us
  Pallas kernels: 22.4 us -> 28.4 us
  local copies, waits for them, and re-layouts: 17.4 us -> 15.3 us
    all_to_all x0 -> x2, blocking collectives: none -> 32.3 us  [the longest x1 16.9 us: shards(): part = lax.all_to_all(part, 'tile', 0, 0, tiled=True)]
    all_to_all x2 -> x0, waiting for transfers between devices: 12.9 us -> none  [the longest x1 9.96 us: shards(): part = lax.all_to_all(part, 'tile', 0, 0, tiled=True)]
    all_to_all x2 -> x0, starting transfers between devices: 10.9 us -> none  [the longest x1 6.05 us: shards(): pack = lax.all_to_all(pack, 'tile', 0, 0, tiled=True)]
    pallas_call x3 -> x5, Pallas kernels: 16.4 us -> 22.5 us  [the longest x2 11.9 us: attention(): call(functools.partial(base_attention_kernel, span, total, padded, picked...]
    ppermute x19, waiting for transfers between devices: 12.1 us -> 17 us  [trade(): return lax.ppermute(block, axis, [(i, i ^ mask) for i in range(count)])]
    all_to_all x1, waiting for transfers between devices: 4.47 us -> 0.07 us  [shards(): folded = lax.all_to_all(folded, 'tile', 0, 0, tiled=True)]
    unnamed x78 -> x72, local copies, waits for them, and re-layouts: 17.4 us -> 15.3 us
    ppermute x19, starting transfers between devices: 22.1 us -> 20 us  [trade(): return lax.ppermute(block, axis, [(i, i ^ mask) for i in range(count)])]
  transfers between devices with their start and end apart: 23 -> 21, of which waited for: 7 -> 5; matrix products, arithmetic and copies ran while one was open for 1% -> 0% of each run, Pallas kernels for 17% -> 14%
where the time goes in v4:
time: 124 us; the launch traced here: 123 us
  blocking collectives  32.3 us (26%)
  starting transfers between devices  29.5 us (24%)
  Pallas kernels  28.4 us (23%)
  waiting for transfers between devices  17 us (14%)
  local copies, waits for them, and re-layouts  15.3 us (12%)
    ppermute x19, starting transfers between devices, trade(): return lax.ppermute(block, axis, [(i, i ^ mask) for i in range(count)])  20 us
    ppermute x19, waiting for transfers between devices, trade(): return lax.ppermute(block, axis, [(i, i ^ mask) for i in range(count)])  17 us
    all_to_all x1, blocking collectives, shards(): part = lax.all_to_all(part, 'tile', 0, 0, tiled=True)  16.9 us
    all_to_all x1, blocking collectives, shards(): pack = lax.all_to_all(pack, 'tile', 0, 0, tiled=True)  15.5 us
    unnamed x72, local copies, waits for them, and re-layouts  15.3 us
    pallas_call x2, Pallas kernels, attention(): call(functools.partial(base_attention_kernel, span, total, padded, picked...  11.9 us
    pallas_call x1, Pallas kernels, shards(): call(functools.partial(fresh_kernel, span, total, groups), out_shape=(sds...  6.88 us
    all_to_all x1, starting transfers between devices, shards(): shares = lax.all_to_all(sent, ('tile', 'seg'), 0, 0, tiled=True)  4.86 us
  transfers between devices with their start and end apart: 21, of which 5 were waited for; matrix products, arithmetic and copies ran while one was open for 0% of the time, Pallas kernels for 14%

profile of v4, /device:TPU:0, one launch (start us, length us, event | category | flops | bytes accessed | tf_op | source)
XLA Modules:
  0.0 123.0 jit_solution(14515911175230572696)
XLA Ops:
  0.0 1.8 %class_row.1 = f32[8,8,256]{2,1,0:T(8,128)} custom-call(bf16[1,257,1536]{2,1,0:T(8,128)(2,1)} %patch_ref.3, f32[1536]{0:T(1024)} %gain_ref.6, s32[8]{0:T(128)} %pos_ref.7, s32[256]{0:T(256)} %kept_ref.3), custom_call_target="tpu_custom_call" | custom-call | tf_op jit(solution)/shard_map/class_row/pallas_call | solution.py:431
  1.8 1.0 copy-done.2
  2.8 1.0 copy-done.4
  3.7 1.0 copy-done.6
  4.7 1.0 copy-done.14
  5.7 0.7 copy-done.27
  6.4 0.7 copy-done.32
  7.1 0.7 copy-done.33
  7.7 0.8 base_rows.1
  8.6 3.1 %collective-permute-start = (bf16[192,384]{1,0:T(8,128)(2,1)}, bf16[192,384]{1,0:T(8,128)(2,1)S(1)}, u32[]{:S(2)}, u32[]{:S(2)}) collective-permute-start(bf16[192,384]{1,0:T(8,128)(2,1)} %refs_0_), channel_id=1, source_target_pairs={{0,8},{4,12},{8,0},{12,4},{16,24},{20,28},{24,16},{28,20},{1,9},{5... | collective-permute-start | bytes 442376 | tf_op jit(solution)/shard_map/ppermute | solution.py:402
  11.7 2.6 %collective-permute-start.1 = (bf16[192,384]{1,0:T(8,128)(2,1)}, bf16[192,384]{1,0:T(8,128)(2,1)S(1)}, u32[]{:S(2)}, u32[]{:S(2)}) collective-permute-start(bf16[192,384]{1,0:T(8,128)(2,1)} %refs_0_), channel_id=1, source_target_pairs={{0,16},{4,20},{8,24},{12,28},{16,0},{20,4},{24,8},{28,12},{1,17},{... | collective-permute-start | bytes 442376 | tf_op jit(solution)/shard_map/ppermute | solution.py:402
  14.3 15.5 %all_to_all.20.pack_ref = f32[8,8,256]{2,1,0:T(8,128)S(1)} all-to-all(f32[8,8,256]{2,1,0:T(8,128)S(1)} %copy-done.35), channel_id=1, replica_groups=mesh['tile'=8,'seg'=4] {'tile'}, dimensions={0} | all-to-all | bytes 131072 | tf_op jit(solution)/shard_map/all_to_all | solution.py:441
  29.9 0.5 token_norm.1.normed_ref
  30.6 0.8 collective-permute-start.3
  31.4 2.3 %collective-permute-start.4 = (bf16[256,384]{1,0:T(8,128)(2,1)S(1)}, bf16[256,384]{1,0:T(8,128)(2,1)S(1)}, u32[]{:S(2)}, u32[]{:S(2)}) collective-permute-start(bf16[256,384]{1,0:T(8,128)(2,1)S(1)} %get-tuple-element.46.refs_0_.refs_4_), channel_id=1, source_target_pairs={{0,16},{4,20},{8,24},{12,28},{16,0},{20,4},{24,8},{28,12},{1,17},{... | collective-permute-start | bytes 589832 | tf_op jit(solution)/shard_map/ppermute | solution.py:402
  33.7 1.4 %collective-permute-start.5 = (bf16[256,384]{1,0:T(8,128)(2,1)S(1)}, bf16[256,384]{1,0:T(8,128)(2,1)S(1)}, u32[]{:S(2)}, u32[]{:S(2)}) collective-permute-start(bf16[256,384]{1,0:T(8,128)(2,1)S(1)} %get-tuple-element.46.refs_0_.refs_4_), channel_id=1, source_target_pairs={{0,24},{4,28},{8,16},{12,20},{16,8},{20,12},{24,0},{28,4},{1,25},{... | collective-permute-start | bytes 589832 | tf_op jit(solution)/shard_map/ppermute | solution.py:402
  35.1 16.9 %all_to_all.21.part_ref = f32[8,8,384]{2,1,0:T(8,128)S(1)} all-to-all(f32[8,8,384]{2,1,0:T(8,128)S(1)} %query_share.1), channel_id=1, replica_groups=mesh['tile'=8,'seg'=4] {'tile'}, dimensions={0} | all-to-all | bytes 196608 | tf_op jit(solution)/shard_map/all_to_all | solution.py:468
  51.9 0.8 fold_key.1
  52.9 6.0 %base_attention.2 = (f32[256,128]{1,0:T(8,128)S(1)}, f32[256,256]{1,0:T(8,128)S(1)}) custom-call(s32[8]{0:T(128)S(1)} %copy-done.29, s32[5,12]{1,0:T(8,128)S(1)} %copy-done.25, f32[8,8,256]{2,1,0:T(8,128)S(1)} %all_to_all.20.pack_ref, bf16[256,256]{1,0:T(8,128)(2,1)S(1)} %get-tuple-element.39.q_ref, bf16[256,384]{1,0:T(8,128)(2,1)S(1)} %get-tuple-element.46.refs_0_.refs_4_, ...), custom_call_target="tpu_custom_call" | custom-call | tf_op jit(solution)/shard_map/base_attention/pallas_call | solution.py:507
  58.9 0.7 copy-done.15
  59.6 0.6 copy-done.21
  60.2 1.5 %collective-permute-start.8 = (bf16[192,1536]{1,0:T(8,128)(2,1)}, bf16[192,1536]{1,0:T(8,128)(2,1)}, u32[]{:S(2)}, u32[]{:S(2)}) collective-permute-start(bf16[192,1536]{1,0:T(8,128)(2,1)} %bitcast.3.refs_0_), channel_id=1, source_target_pairs={{0,2},{1,3},{2,0},{3,1},{4,6},{5,7},{6,4},{7,5},{8,10},{9,11},{10,... | collective-permute-start | bytes 1769480 | tf_op jit(solution)/shard_map/ppermute | solution.py:402
  61.7 1.3 %collective-permute-start.7 = (bf16[576,384]{1,0:T(8,128)(2,1)S(1)}, bf16[576,384]{1,0:T(8,128)(2,1)}, u32[]{:S(2)}, u32[]{:S(2)}) collective-permute-start(bf16[576,384]{1,0:T(8,128)(2,1)S(1)} %pad_maximum_fusion.1.refs_1_), channel_id=1, source_target_pairs={{0,4},{4,0},{8,12},{12,8},{16,20},{20,16},{24,28},{28,24},{1,5},{5... | collective-permute-start | bytes 1327112 | tf_op jit(solution)/shard_map/ppermute | solution.py:402
  63.0 0.5 collective-permute-start.9
  63.6 0.7 collective-permute-start.6
  64.3 4.7 %all-to-all-start.2 = ((f32[8,8,256]{2,1,0:T(8,128)}), f32[8,8,256]{2,1,0:T(8,128)S(1)}, u32[]{:S(2)}, u32[]{:S(2)}) async-start(f32[8,8,256]{2,1,0:T(8,128)} %fold_key.1), calls=%async_computation.2 | async-start | bytes 131072 | tf_op jit(solution)/shard_map/all_to_all | solution.py:501
  68.9 2.0 %collective-permute-start.11 = (bf16[768,384]{1,0:T(8,128)(2,1)S(1)}, bf16[768,384]{1,0:T(8,128)(2,1)S(1)}, u32[]{:S(2)}, u32[]{:S(2)}) collective-permute-start(bf16[768,384]{1,0:T(8,128)(2,1)S(1)} %pad_maximum_fusion.refs_1_.refs_5_), channel_id=1, source_target_pairs={{0,4},{4,0},{8,12},{12,8},{16,20},{20,16},{24,28},{28,24},{1,5},{5... | collective-permute-start | bytes 1769480 | tf_op jit(solution)/shard_map/ppermute | solution.py:402
  71.0 7.6 %collective-permute-done.6.refs_2_ = bf16[192,384]{1,0:T(8,128)(2,1)} collective-permute-done((bf16[192,384]{1,0:T(8,128)(2,1)}, bf16[192,384]{1,0:T(8,128)(2,1)}, u32[]{:S(2)}, u32[]{:S(2)}) %collective-permute-start.6) | collective-permute-done | bytes 147488 | tf_op jit(solution)/shard_map/ppermute | solution.py:402
  78.7 1.3 %copy-done.1 = bf16[384,1536]{1,0:T(8,128)(2,1)S(1)} copy-done((bf16[384,1536]{1,0:T(8,128)(2,1)S(1)}, bf16[384,1536]{1,0:T(8,128)(2,1)}, u32[]{:S(2)}) %copy-start.1) | copy-done | bytes 1179672
  80.0 3.2 %tile_attention.1 = bf16[32,16,128]{2,1,0:T(8,128)(2,1)S(1)} custom-call(bf16[1,257,1536]{2,1,0:T(8,128)(2,1)S(1)} %copy-done, bf16[257,1536]{1,0:T(8,128)(2,1)S(1)} %token_norm.1.normed_ref, f32[8,8,256]{2,1,0:T(8,128)S(1)} %all-to-all-done.2.fold_ref, f32[1536]{0:T(1024)S(1)} %copy-done.30, f32[192]{0:T(256)S(1)} %copy-done.34, ...), custom_call_target="tpu_custom_call" | custom-call | tf_op jit(solution)/shard_map/tile_attention/pallas_call | solution.py:524
  83.2 0.6 copy-done.11
  83.9 0.5 collective-permute-start.13
  84.4 1.3 %collective-permute-start.10 = (bf16[256,384]{1,0:T(8,128)(2,1)S(1)}, bf16[256,384]{1,0:T(8,128)(2,1)S(1)}, u32[]{:S(2)}, u32[]{:S(2)}) collective-permute-start(bf16[256,384]{1,0:T(8,128)(2,1)S(1)} %copy-done.9), channel_id=1, source_target_pairs={{0,4},{4,0},{8,12},{12,8},{16,20},{20,16},{24,28},{28,24},{1,5},{5... | collective-permute-start | bytes 589832 | tf_op jit(solution)/shard_map/ppermute | solution.py:402
  85.7 6.0 %collective-permute-done.10.refs_0_.refs_6_ = bf16[256,384]{1,0:T(8,128)(2,1)S(1)} collective-permute-done((bf16[256,384]{1,0:T(8,128)(2,1)S(1)}, bf16[256,384]{1,0:T(8,128)(2,1)S(1)}, u32[]{:S(2)}, u32[]{:S(2)}) %collective-permute-start.10) | collective-permute-done | bytes 196640 | tf_op jit(solution)/shard_map/ppermute | solution.py:402
  91.7 4.9 %all-to-all-start.3 = ((bf16[32,16,128]{2,1,0:T(8,128)(2,1)}), bf16[32,16,128]{2,1,0:T(8,128)(2,1)}, u32[]{:S(2)}, u32[]{:S(2)}) async-start(bf16[32,16,128]{2,1,0:T(8,128)(2,1)} %copy-done.11), calls=%async_computation.3 | async-start | bytes 262144 | tf_op jit(solution)/shard_map/all_to_all | solution.py:537
  96.6 0.9 copy-done.16
  97.6 0.9 copy-done.22
  98.5 5.9 %base_attention.3 = (f32[256,128]{1,0:T(8,128)S(1)}, f32[256,256]{1,0:T(8,128)S(1)}) custom-call(s32[8]{0:T(128)S(1)} %copy-done.29, s32[5,12]{1,0:T(8,128)S(1)} %copy-done.25, f32[8,8,256]{2,1,0:T(8,128)S(1)} %all_to_all.20.pack_ref, bf16[256,256]{1,0:T(8,128)(2,1)S(1)} %get-tuple-element.39.q_ref, ...), custom_call_target="tpu_custom_call" | custom-call | tf_op jit(solution)/shard_map/base_attention/pallas_call | solution.py:507
  104.4 0.7 copy-done.17
  105.1 0.6 copy-done.23
  105.8 1.0 copy-done.13
  106.8 0.9 copy-done.18
  107.8 0.9 copy-done.24
  108.7 6.9 %fresh_attention.1 = (bf16[64,256]{1,0:T(8,128)(2,1)S(1)}, bf16[64,256]{1,0:T(8,128)(2,1)S(1)}, bf16[64,256]{1,0:T(8,128)(2,1)S(1)}, bf16[64,256]{1,0:T(8,128)(2,1)S(1)}, f32[64,768]{1,0:T(8,128)S(1)}) custom-call(s32[8]{0:T(128)S(1)} %copy-done.29, s32[5,12]{1,0:T(8,128)S(1)} %copy-done.25, f32[8,8,256]{2,1,0:T(8,128)S(1)} %all_to_all.20.pack_ref, ...), custom_call_target="tpu_custom_call" | custom-call | tf_op jit(solution)/shard_map/fresh_attention/pallas_call | solution.py:544
  115.7 1.7 %collective-permute-start.15 = (bf16[64,256]{1,0:T(8,128)(2,1)S(1)}, bf16[64,256]{1,0:T(8,128)(2,1)S(1)}, u32[]{:S(2)}, u32[]{:S(2)}) collective-permute-start(bf16[64,256]{1,0:T(8,128)(2,1)S(1)} %get-tuple-element.66), channel_id=1, source_target_pairs={{0,2},{1,3},{2,0},{3,1},{4,6},{5,7},{6,4},{7,5},{8,10},{9,11},{10,... | collective-permute-start | bytes 98312 | tf_op jit(solution)/shard_map/ppermute | solution.py:402
  117.5 2.1 %collective-permute-done.15.refs_2_ = bf16[64,256]{1,0:T(8,128)(2,1)S(1)} collective-permute-done((bf16[64,256]{1,0:T(8,128)(2,1)S(1)}, bf16[64,256]{1,0:T(8,128)(2,1)S(1)}, u32[]{:S(2)}, u32[]{:S(2)}) %collective-permute-start.15) | collective-permute-done | bytes 32800 | tf_op jit(solution)/shard_map/ppermute | solution.py:402
  119.6 1.1 collective-permute-done.16.refs_3_
  120.8 2.3 %slide_next.1 = bf16[64,768]{1,0:T(8,128)(2,1)} custom-call(f32[64,768]{1,0:T(8,128)S(1)} %get-tuple-element.63.mine_ref, bf16[64,256]{1,0:T(8,128)(2,1)S(1)} %get-tuple-element.64.refs_0_, bf16[64,256]{1,0:T(8,128)(2,1)S(1)} %collective-permute-done.14.refs_1_, bf16[64,256]{1,0:T(8,128)(2,1)S(1)} %collective-permute-done.15.refs_2_, ...), custom_call_target="tpu_custom_call" | custom-call | tf_op jit(solution)/shard_map/slide_next/pallas_call | solution.py:566
  (80 shorter events, 0.7 us)
Async XLA Ops:
  0.0 29.9 %copy-start = (bf16[1,257,1536]{2,1,0:T(8,128)(2,1)S(1)}, bf16[1,257,1536]{2,1,0:T(8,128)(2,1)}, u32[]{:S(2)}) copy-start(bf16[1,257,1536]{2,1,0:T(8,128)(2,1)} %patch_ref.3) | copy-start | bytes 2368516
  0.0 29.9 %copy-start.26 = (f32[1536]{0:T(1024)S(1)}, f32[1536]{0:T(1024)}, u32[]{:S(2)}) copy-start(f32[1536]{0:T(1024)} %gain_ref.6) | copy-start | bytes 18436
  1.8 1.0 copy-start.2
  2.8 1.0 copy-start.4
  3.7 1.0 copy-start.6
  4.7 1.0 copy-start.14
  7.7 6.6 %copy-start.35 = (f32[8,8,256]{2,1,0:T(8,128)S(1)}, f32[8,8,256]{2,1,0:T(8,128)}, u32[]{:S(2)}) copy-start(f32[8,8,256]{2,1,0:T(8,128)} %class_row.1) | copy-start | bytes 196612
  7.7 22.0 %copy-start.19 = (bf16[192,384]{1,0:T(8,128)(2,1)S(1)}, bf16[192,384]{1,0:T(8,128)(2,1)}, u32[]{:S(2)}) copy-start(bf16[192,384]{1,0:T(8,128)(2,1)} %wq_ref.1) | copy-start | bytes 442372
  8.6 22.0 %copy-start.12 = (bf16[256,768]{1,0:T(8,128)(2,1)}, bf16[256,768]{1,0:T(8,128)(2,1)S(1)}, u32[]{:S(2)}) copy-start(bf16[256,768]{1,0:T(8,128)(2,1)S(1)} %get-tuple-element.61.rows_ref) | copy-start | bytes 1179652
  8.6 44.2 %copy-start.8 = (bf16[256,384]{1,0:T(8,128)(2,1)}, bf16[256,384]{1,0:T(8,128)(2,1)S(1)}, u32[]{:S(2)}) copy-start(bf16[256,384]{1,0:T(8,128)(2,1)S(1)} %get-tuple-element.46.refs_0_.refs_4_) | copy-start | bytes 589828
  8.6 21.9 %collective-permute-start = (bf16[192,384]{1,0:T(8,128)(2,1)}, bf16[192,384]{1,0:T(8,128)(2,1)S(1)}, u32[]{:S(2)}, u32[]{:S(2)}) collective-permute-start(bf16[192,384]{1,0:T(8,128)(2,1)} %refs_0_), channel_id=1, source_target_pairs={{0,8},{4,12},{8,0},{12,4},{16,24},{20,28},{24,16},{28,20},{1,9},{5... | collective-permute-start | bytes 442376 | tf_op jit(solution)/shard_map/ppermute | solution.py:402
  11.7 18.8 %collective-permute-start.1 = (bf16[192,384]{1,0:T(8,128)(2,1)}, bf16[192,384]{1,0:T(8,128)(2,1)S(1)}, u32[]{:S(2)}, u32[]{:S(2)}) collective-permute-start(bf16[192,384]{1,0:T(8,128)(2,1)} %refs_0_), channel_id=1, source_target_pairs={{0,16},{4,20},{8,24},{12,28},{16,0},{20,4},{24,8},{28,12},{1,17},{... | collective-permute-start | bytes 442376 | tf_op jit(solution)/shard_map/ppermute | solution.py:402
  14.3 16.2 %collective-permute-start.2 = (bf16[192,384]{1,0:T(8,128)(2,1)}, bf16[192,384]{1,0:T(8,128)(2,1)S(1)}, u32[]{:S(2)}, u32[]{:S(2)}) collective-permute-start(bf16[192,384]{1,0:T(8,128)(2,1)} %refs_0_), channel_id=1, source_target_pairs={{0,24},{4,28},{8,16},{12,20},{16,8},{20,12},{24,0},{28,4},{1,25},{... | collective-permute-start | bytes 442376 | tf_op jit(solution)/shard_map/ppermute | solution.py:402
  29.9 22.0 %copy-start.20 = (bf16[192,384]{1,0:T(8,128)(2,1)S(1)}, bf16[192,384]{1,0:T(8,128)(2,1)}, u32[]{:S(2)}) copy-start(bf16[192,384]{1,0:T(8,128)(2,1)} %wk_ref.1) | copy-start | bytes 442372
  30.5 22.4 %copy-start.25 = (s32[5,12]{1,0:T(8,128)S(1)}, s32[5,12]{1,0:T(8,128)}, u32[]{:S(2)}) copy-start(s32[5,12]{1,0:T(8,128)} %offset_ref.5) | copy-start | bytes 724
  30.5 22.4 %copy-start.29 = (s32[8]{0:T(128)S(1)}, s32[8]{0:T(128)}, u32[]{:S(2)}) copy-start(s32[8]{0:T(128)} %pos_ref.7) | copy-start | bytes 100
  30.6 22.2 %collective-permute-start.3 = (bf16[256,384]{1,0:T(8,128)(2,1)S(1)}, bf16[256,384]{1,0:T(8,128)(2,1)S(1)}, u32[]{:S(2)}, u32[]{:S(2)}) collective-permute-start(bf16[256,384]{1,0:T(8,128)(2,1)S(1)} %get-tuple-element.46.refs_0_.refs_4_), channel_id=1, source_target_pairs={{0,8},{4,12},{8,0},{12,4},{16,24},{20,28},{24,16},{28,20},{1,9},{5... | collective-permute-start | bytes 589832 | tf_op jit(solution)/shard_map/ppermute | solution.py:402
  31.4 21.4 %collective-permute-start.4 = (bf16[256,384]{1,0:T(8,128)(2,1)S(1)}, bf16[256,384]{1,0:T(8,128)(2,1)S(1)}, u32[]{:S(2)}, u32[]{:S(2)}) collective-permute-start(bf16[256,384]{1,0:T(8,128)(2,1)S(1)} %get-tuple-element.46.refs_0_.refs_4_), channel_id=1, source_target_pairs={{0,16},{4,20},{8,24},{12,28},{16,0},{20,4},{24,8},{28,12},{1,17},{... | collective-permute-start | bytes 589832 | tf_op jit(solution)/shard_map/ppermute | solution.py:402
  33.7 19.1 %collective-permute-start.5 = (bf16[256,384]{1,0:T(8,128)(2,1)S(1)}, bf16[256,384]{1,0:T(8,128)(2,1)S(1)}, u32[]{:S(2)}, u32[]{:S(2)}) collective-permute-start(bf16[256,384]{1,0:T(8,128)(2,1)S(1)} %get-tuple-element.46.refs_0_.refs_4_), channel_id=1, source_target_pairs={{0,24},{4,28},{8,16},{12,20},{16,8},{20,12},{24,0},{28,4},{1,25},{... | collective-permute-start | bytes 589832 | tf_op jit(solution)/shard_map/ppermute | solution.py:402
  52.8 25.9 %copy-start.30 = (f32[1536]{0:T(1024)S(1)}, f32[1536]{0:T(1024)}, u32[]{:S(2)}) copy-start(f32[1536]{0:T(1024)} %scale_ref.1) | copy-start | bytes 18436
  52.8 25.9 %copy-start.34 = (f32[192]{0:T(256)S(1)}, f32[192]{0:T(256)}, u32[]{:S(2)}) copy-start(f32[192]{0:T(256)} %bias_ref.1) | copy-start | bytes 2308
  60.2 23.6 %collective-permute-start.8 = (bf16[192,1536]{1,0:T(8,128)(2,1)}, bf16[192,1536]{1,0:T(8,128)(2,1)}, u32[]{:S(2)}, u32[]{:S(2)}) collective-permute-start(bf16[192,1536]{1,0:T(8,128)(2,1)} %bitcast.3.refs_0_), channel_id=1, source_target_pairs={{0,2},{1,3},{2,0},{3,1},{4,6},{5,7},{6,4},{7,5},{8,10},{9,11},{10,... | collective-permute-start | bytes 1769480 | tf_op jit(solution)/shard_map/ppermute | solution.py:402
  61.7 17.0 %collective-permute-start.7 = (bf16[576,384]{1,0:T(8,128)(2,1)S(1)}, bf16[576,384]{1,0:T(8,128)(2,1)}, u32[]{:S(2)}, u32[]{:S(2)}) collective-permute-start(bf16[576,384]{1,0:T(8,128)(2,1)S(1)} %pad_maximum_fusion.1.refs_1_), channel_id=1, source_target_pairs={{0,4},{4,0},{8,12},{12,8},{16,20},{20,16},{24,28},{28,24},{1,5},{5... | collective-permute-start | bytes 1327112 | tf_op jit(solution)/shard_map/ppermute | solution.py:402
  63.0 20.8 %collective-permute-start.9 = (bf16[192,768]{1,0:T(8,128)(2,1)}, bf16[192,768]{1,0:T(8,128)(2,1)}, u32[]{:S(2)}, u32[]{:S(2)}) collective-permute-start(bf16[192,768]{1,0:T(8,128)(2,1)} %refs_4_), channel_id=1, source_target_pairs={{0,2},{1,3},{2,0},{3,1},{4,6},{5,7},{6,4},{7,5},{8,10},{9,11},{10,... | collective-permute-start | bytes 884744 | tf_op jit(solution)/shard_map/ppermute | solution.py:402
  63.6 15.0 %collective-permute-start.6 = (bf16[192,384]{1,0:T(8,128)(2,1)}, bf16[192,384]{1,0:T(8,128)(2,1)}, u32[]{:S(2)}, u32[]{:S(2)}) collective-permute-start(bf16[192,384]{1,0:T(8,128)(2,1)} %refs_0_), channel_id=1, source_target_pairs={{0,4},{4,0},{8,12},{12,8},{16,20},{20,16},{24,28},{28,24},{1,5},{5... | collective-permute-start | bytes 442376 | tf_op jit(solution)/shard_map/ppermute | solution.py:402
  64.3 14.4 %all-to-all-start.2 = ((f32[8,8,256]{2,1,0:T(8,128)}), f32[8,8,256]{2,1,0:T(8,128)S(1)}, u32[]{:S(2)}, u32[]{:S(2)}) async-start(f32[8,8,256]{2,1,0:T(8,128)} %fold_key.1), calls=%async_computation.2 | async-start | bytes 131072 | tf_op jit(solution)/shard_map/all_to_all | solution.py:501
  68.9 27.7 %collective-permute-start.11 = (bf16[768,384]{1,0:T(8,128)(2,1)S(1)}, bf16[768,384]{1,0:T(8,128)(2,1)S(1)}, u32[]{:S(2)}, u32[]{:S(2)}) collective-permute-start(bf16[768,384]{1,0:T(8,128)(2,1)S(1)} %pad_maximum_fusion.refs_1_.refs_5_), channel_id=1, source_target_pairs={{0,4},{4,0},{8,12},{12,8},{16,20},{20,16},{24,28},{28,24},{1,5},{5... | collective-permute-start | bytes 1769480 | tf_op jit(solution)/shard_map/ppermute | solution.py:402
  78.6 27.1 %collective-permute-start.12 = (bf16[192,1536]{1,0:T(8,128)(2,1)}, bf16[192,1536]{1,0:T(8,128)(2,1)}, u32[]{:S(2)}, u32[]{:S(2)}) collective-permute-start(bf16[192,1536]{1,0:T(8,128)(2,1)} %bitcast.3.refs_0_), channel_id=1, source_target_pairs={{0,1},{1,0},{2,3},{3,2},{4,5},{5,4},{6,7},{7,6},{8,9},{9,8},{10,11... | collective-permute-start | bytes 1769480 | tf_op jit(solution)/shard_map/ppermute | solution.py:402
  78.7 1.3 %copy-start.1 = (bf16[384,1536]{1,0:T(8,128)(2,1)S(1)}, bf16[384,1536]{1,0:T(8,128)(2,1)}, u32[]{:S(2)}) copy-start(bf16[384,1536]{1,0:T(8,128)(2,1)} %wo_ref.1) | copy-start | bytes 3538948
  80.0 4.4 %copy-start.9 = (bf16[256,384]{1,0:T(8,128)(2,1)S(1)}, bf16[256,384]{1,0:T(8,128)(2,1)}, u32[]{:S(2)}) copy-start(bf16[256,384]{1,0:T(8,128)(2,1)} %copy-done.8) | copy-start | bytes 589828
  80.0 25.8 %copy-start.28 = (f32[768]{0:T(1024)S(1)}, f32[768]{0:T(1024)}, u32[]{:S(2)}) copy-start(f32[768]{0:T(1024)} %gain_ref.7) | copy-start | bytes 9220
  80.0 25.8 %copy-start.31 = (f32[1536]{0:T(1024)S(1)}, f32[1536]{0:T(1024)}, u32[]{:S(2)}) copy-start(f32[1536]{0:T(1024)} %final_ref.1) | copy-start | bytes 18436
  83.8 22.0 %copy-start.3 = (bf16[768,192]{0,1:T(8,128)(2,1)S(1)}, bf16[768,192]{0,1:T(8,128)(2,1)}, u32[]{:S(2)}) copy-start(bf16[768,192]{0,1:T(8,128)(2,1)} %param.35) | copy-start | bytes 884740
  83.8 22.0 %copy-start.5 = (bf16[768,192]{0,1:T(8,128)(2,1)S(1)}, bf16[768,192]{0,1:T(8,128)(2,1)}, u32[]{:S(2)}) copy-start(bf16[768,192]{0,1:T(8,128)(2,1)} %param.36) | copy-start | bytes 884740
  83.8 22.0 %copy-start.7 = (bf16[768,192]{0,1:T(8,128)(2,1)S(1)}, bf16[768,192]{0,1:T(8,128)(2,1)}, u32[]{:S(2)}) copy-start(bf16[768,192]{0,1:T(8,128)(2,1)} %param.37) | copy-start | bytes 884740
  83.8 22.0 %copy-start.10 = (bf16[256,384]{1,0:T(8,128)(2,1)S(1)}, bf16[256,384]{1,0:T(8,128)(2,1)}, u32[]{:S(2)}) copy-start(bf16[256,384]{1,0:T(8,128)(2,1)} %copy-done.8) | copy-start | bytes 589828
  83.9 21.9 %collective-permute-start.13 = (bf16[192,1536]{1,0:T(8,128)(2,1)}, bf16[192,1536]{1,0:T(8,128)(2,1)S(1)}, u32[]{:S(2)}, u32[]{:S(2)}) collective-permute-start(bf16[192,1536]{1,0:T(8,128)(2,1)} %collective-permute-done.8.refs_2_), channel_id=1, source_target_pairs={{0,1},{1,0},{2,3},{3,2},{4,5},{5,4},{6,7},{7,6},{8,9},{9,8},{10,11... | collective-permute-start | bytes 1769480 | tf_op jit(solution)/shard_map/ppermute | solution.py:402
  84.4 7.4 %collective-permute-start.10 = (bf16[256,384]{1,0:T(8,128)(2,1)S(1)}, bf16[256,384]{1,0:T(8,128)(2,1)S(1)}, u32[]{:S(2)}, u32[]{:S(2)}) collective-permute-start(bf16[256,384]{1,0:T(8,128)(2,1)S(1)} %copy-done.9), channel_id=1, source_target_pairs={{0,4},{4,0},{8,12},{12,8},{16,20},{20,16},{24,28},{28,24},{1,5},{5... | collective-permute-start | bytes 589832 | tf_op jit(solution)/shard_map/ppermute | solution.py:402
  85.7 31.8 %collective-permute-start.17 = (bf16[192,768]{1,0:T(8,128)(2,1)}, bf16[192,768]{1,0:T(8,128)(2,1)}, u32[]{:S(2)}, u32[]{:S(2)}) collective-permute-start(bf16[192,768]{1,0:T(8,128)(2,1)} %refs_4_), channel_id=1, source_target_pairs={{0,1},{1,0},{2,3},{3,2},{4,5},{5,4},{6,7},{7,6},{8,9},{9,8},{10,11... | collective-permute-start | bytes 884744 | tf_op jit(solution)/shard_map/ppermute | solution.py:402
  91.7 25.8 %collective-permute-start.18 = (bf16[192,768]{1,0:T(8,128)(2,1)}, bf16[192,768]{1,0:T(8,128)(2,1)}, u32[]{:S(2)}, u32[]{:S(2)}) collective-permute-start(bf16[192,768]{1,0:T(8,128)(2,1)} %collective-permute-done.9.refs_6_), channel_id=1, source_target_pairs={{0,1},{1,0},{2,3},{3,2},{4,5},{5,4},{6,7},{7,6},{8,9},{9,8},{10,11... | collective-permute-start | bytes 884744 | tf_op jit(solution)/shard_map/ppermute | solution.py:402
  91.7 14.0 %all-to-all-start.3 = ((bf16[32,16,128]{2,1,0:T(8,128)(2,1)}), bf16[32,16,128]{2,1,0:T(8,128)(2,1)}, u32[]{:S(2)}, u32[]{:S(2)}) async-start(bf16[32,16,128]{2,1,0:T(8,128)(2,1)} %copy-done.11), calls=%async_computation.3 | async-start | bytes 262144 | tf_op jit(solution)/shard_map/all_to_all | solution.py:537
  96.6 1.0 copy-start.16
  97.6 0.9 copy-start.22
  105.8 1.0 copy-start.13
  106.8 0.9 copy-start.18
  115.6 2.0 %collective-permute-start.14 = (bf16[64,256]{1,0:T(8,128)(2,1)S(1)}, bf16[64,256]{1,0:T(8,128)(2,1)S(1)}, u32[]{:S(2)}, u32[]{:S(2)}) collective-permute-start(bf16[64,256]{1,0:T(8,128)(2,1)S(1)} %get-tuple-element.65), channel_id=1, source_target_pairs={{0,1},{1,0},{2,3},{3,2},{4,5},{5,4},{6,7},{7,6},{8,9},{9,8},{10,11... | collective-permute-start | bytes 98312 | tf_op jit(solution)/shard_map/ppermute | solution.py:402
  115.7 4.0 %collective-permute-start.15 = (bf16[64,256]{1,0:T(8,128)(2,1)S(1)}, bf16[64,256]{1,0:T(8,128)(2,1)S(1)}, u32[]{:S(2)}, u32[]{:S(2)}) collective-permute-start(bf16[64,256]{1,0:T(8,128)(2,1)S(1)} %get-tuple-element.66), channel_id=1, source_target_pairs={{0,2},{1,3},{2,0},{3,1},{4,6},{5,7},{6,4},{7,5},{8,10},{9,11},{10,... | collective-permute-start | bytes 98312 | tf_op jit(solution)/shard_map/ppermute | solution.py:402
  117.3 3.4 %collective-permute-start.16 = (bf16[64,256]{1,0:T(8,128)(2,1)S(1)}, bf16[64,256]{1,0:T(8,128)(2,1)S(1)}, u32[]{:S(2)}, u32[]{:S(2)}) collective-permute-start(bf16[64,256]{1,0:T(8,128)(2,1)S(1)} %get-tuple-element.67), channel_id=1, source_target_pairs={{0,3},{1,2},{2,1},{3,0},{4,7},{5,6},{6,5},{7,4},{8,11},{9,10},{10,... | collective-permute-start | bytes 98312 | tf_op jit(solution)/shard_map/ppermute | solution.py:402
  (9 other events, 6.3 us)

commit v5 on v4

--- a/solution.py
+++ b/solution.py
@@ -74,8 +74,11 @@
 
 
 def base_kernel(
-    cached_ref, kept_ref, mask_ref, gain_ref, wq_ref, wk_ref, wv_ref, rows_ref, q_ref, kv_ref
+    cached_ref, kept_ref, mask_ref, gain_ref, wq_ref, wk_ref, wv_ref, embed_ref, project_ref,
+    rows_ref, q_ref, kv_ref, joined_ref,
 ):
+    joined_ref[:, 0:DV] = embed_ref[...]
+    joined_ref[:, DV:] = project_ref[...]
     span = kept_ref.shape[0]
     kept = column(jnp.where(kept_ref[...].reshape(1, span) != 0, 1.0, 0.0), span)
     mask_row = mask_ref[...].reshape(1, DS).astype(BF16).astype(F32)
@@ -285,42 +288,40 @@
 
 
 def base_attention_kernel(
-    span, total, padded, groups, state, pos_ref, offset_ref, pack_ref, q_ref, *refs
+    span, total, padded, groups, pos_ref, offset_ref, pack_ref, q_ref, *refs
 ):
     kv_refs, refs = refs[: len(groups)], refs[len(groups) :]
-    ml_ref, acc_ref = refs[-2:]
+    kv_ref = kv_refs[0] if len(groups) == 1 else refs[0]
+    krows_ref, ml_ref, acc_ref = refs[-3:]
     step = pl.program_id(0)
     rows = q_ref.shape[0]
 
     @pl.when(step == 0)
     def _():
-        if state:
-            ml_ref[...] = refs[0][...]
-            acc_ref[...] = refs[1][...]
-        else:
-            clear_state(ml_ref, acc_ref)
-
+        clear_state(ml_ref, acc_ref)
+
+    masks = None
+    if len(groups) > 1:
+        masks = sum(groups, ())
+        start = 0
+        for ref in kv_refs:
+            kv_ref[start : start + ref.shape[0], :] = ref[...]
+            start += ref.shape[0]
     _, pos_col, _, flag_col = fresh_places(padded, pack_ref, pos_ref)
     place = lax.broadcasted_iota(I32, (rows, 1), 0) + lax.axis_index("tile") * span
-    q_rows = as_bf16(branch_rows(place, 1, offset_ref, span, total))
-    q = q_ref[...]
-    lane = lax.broadcasted_iota(I32, (1, 256), 1)
-    branch = lax.broadcasted_iota(I32, (1, 24), 1)
-    for masks, kv_ref in zip(groups, kv_refs):
-        keys = key_places(masks, kv_ref.shape[0], span, step)
-        k_rows = key_rows(keys, pos_col, flag_col, offset_ref, span, total)
-        for head in range(3):
-            q_head = jnp.where(lane // HEAD == head, q, jnp.zeros_like(q))
-            r_head = jnp.where(branch // 8 == head, q_rows, jnp.zeros_like(q_rows))
-            add_state(attend(q_head, r_head, kv_ref, k_rows), head, ml_ref, acc_ref)
+    q_rows = stack_heads(as_bf16(branch_rows(place, 1, offset_ref, span, total)), 8)
+    keys = key_places(masks, kv_ref.shape[0], span, step)
+    k_rows = key_rows(keys, pos_col, flag_col, offset_ref, span, total)
+    krows_ref[...] = k_rows
+    add_stacked(attend(stack_heads(q_ref[...], HEAD), q_rows, kv_ref, k_rows), ml_ref, acc_ref)
 
 
 def fresh_kernel(
-    span, total, groups, pos_ref, offset_ref, pack_ref, q_ref, shares_ref, final_ref, gain_ref,
+    span, total, pos_ref, offset_ref, pack_ref, q_ref, shares_ref, final_ref, gain_ref,
     wq_ref, wk_ref, wv_ref, ml_ref, acc_ref, rows_ref, *refs,
 ):
     embed_refs, refs = refs[:4], refs[4:]
-    kv_refs, refs = refs[: len(groups)], refs[len(groups) :]
+    kv_ref, krows_ref, *refs = refs
     outs, refs = refs[:4], refs[4:]
     mine_ref, fresh_s, qf_s, kvf_s, mlf_s, accf_s, mlb_s, att_s = refs
     step = pl.program_id(0)
@@ -339,7 +340,7 @@
         pooled = jnp.concatenate([summed[:, row, :] for row in range(DV // 128)], axis=1)
         summary = layer_norm(pooled, final_ref[...].reshape(1, DV)).astype(BF16)
         fresh_s[...] = jnp.zeros_like(fresh_s)
-        pieces = [dot_nt(summary, ref[...]) for ref in embed_refs]
+        pieces = [dot_nt(summary, ref[:, 0:DV]) for ref in embed_refs]
         for part in range(4):
             piece = pieces[0]
             for mask in range(1, 4):
@@ -354,10 +355,7 @@
         clear_state(mlf_s, accf_s)
 
     qf = stack_heads(qf_s[...], HEAD)
-    for masks, kv_ref in zip(groups, kv_refs):
-        keys = key_places(masks, kv_ref.shape[0], span, step)
-        k_rows = key_rows(keys, pos_col, flag_col, offset_ref, span, total)
-        add_stacked(attend(qf, f_rows, kv_ref, k_rows), mlf_s, accf_s)
+    add_stacked(attend(qf, f_rows, kv_ref, krows_ref[...]), mlf_s, accf_s)
 
     @pl.when(step == pl.num_programs(0) - 1)
     def _():
@@ -391,7 +389,7 @@
     out_ref = refs[8]
     total = mine_ref[...]
     for mask in range(4):
-        att, weight = refs[mask][...], refs[4 + mask]
+        att, weight = refs[mask][...], refs[4 + mask][...]
         total = total + dot(att[:, 128:256], weight[0:128])
         total = total + dot(att[:, 64:128], weight[128:192])
     out_ref[...] = total.astype(BF16)
@@ -437,19 +435,21 @@
         compiler_params=params(60),
         name="class_row",
     )(patches, vit_norm_gain, slide_pos, kept)
-    pack, cached = together(pack, cached)
+    pack, value, cached = together(pack, vit_value, cached)
     pack = lax.all_to_all(pack, "tile", 0, 0, tiled=True)
-    base_rows, q_base, kv_base = call(
+    base_rows, q_base, kv_base, joined = call(
         base_kernel,
-        out_shape=(sds((span, DS), BF16), sds((span, 256), BF16), sds((span, 384), BF16)),
-        in_specs=[VMEM] * 7,
-        out_specs=(VMEM,) * 3,
-        compiler_params=params(16),
+        out_shape=(
+            sds((span, DS), BF16), sds((span, 256), BF16), sds((span, 384), BF16),
+            sds((192, DV + DS), BF16),
+        ),
+        in_specs=[VMEM] * 9,
+        out_specs=(VMEM,) * 4,
+        compiler_params=params(60),
         name="base_rows",
-    )(cached, kept, mask_token, slide_gain, *weights)
-    value = vit_value
+    )(cached, kept, mask_token, slide_gain, *weights, embed, slide_out)
+    joined_x = trade(joined, "seg", 2)
     if small:
-        kv_base, value = together(kv_base, value)
         value_z = jnp.concatenate([trade(value, "tile", mask) for mask in GROUPS[1]], axis=0)
         value_y = trade(value, "tile", 1)
         kv_y = trade(kv_base, "tile", 1)
@@ -463,8 +463,8 @@
         compiler_params=params(8 if small else 16),
         name="query_share",
     )(pack, vit_query)
-    part, patches = together(part, patches)
     if small:
+        part, value_z, kv_own = together(part, value_z, kv_base)
         part = lax.all_to_all(part, "tile", 0, 0, tiled=True)
     else:
         part = lax.psum(part, "tile")
@@ -476,8 +476,9 @@
         compiler_params=params(12),
         name="token_norm",
     )(patches, vit_norm_gain)
+    joined, joined_x = together(joined, joined_x)
+    joined_all = [joined, trade(joined, "seg", 1), joined_x, trade(joined_x, "seg", 1)]
     if small:
-        normed, value_z, kv_own = together(normed, value_z, kv_base)
         wv_all = [value, value_z, value_y, trade(value_z, "tile", 1)]
         kv_z = jnp.concatenate([trade(kv_own, "tile", mask) for mask in GROUPS[1]], axis=0)
     else:
@@ -492,35 +493,13 @@
         name="fold_key",
     )(part, vit_key)
     if small:
-        folded, kv_z = together(folded, kv_z)
+        folded, kv_z, kv_y = together(folded, kv_z, kv_y)
         kv_all = [kv_own, kv_z, kv_y, trade(kv_z, "tile", 1)]
         groups = GROUPS
     else:
         kv_all = [lax.all_gather(kv_base, "tile", axis=0, tiled=True)]
         groups = (None,)
     folded = lax.all_to_all(folded, "tile", 0, 0, tiled=True)
-    block = min(total, 2048)
-    steps = 1 if small else total // block
-    kv_spec = VMEM if small else pl.BlockSpec((block, 384), lambda i: (i, 0))
-
-    def attention(blocks, picked, state):
-        return call(
-            functools.partial(
-                base_attention_kernel, span, total, padded, picked, len(state) > 0
-            ),
-            out_shape=(sds((span, 128), F32), sds((span, 256), F32)),
-            grid=(steps,),
-            in_specs=[SMEM, SMEM, VMEM, VMEM] + [kv_spec] * len(blocks) + [VMEM] * len(state),
-            out_specs=(VMEM, VMEM),
-            compiler_params=params(16 if small else 32),
-            name="base_attention",
-        )(slide_pos, offsets, pack, q_base, *blocks, *state)
-
-    state = attention(kv_all[:2], groups[:2], ())
-    state, embed, slide_out = together(state, embed, slide_out)
-    embed_x = trade(embed, "seg", 2)
-    out_x = trade(slide_out, "seg", 2)
-
     sent = call(
         functools.partial(tile_kernel, cut),
         out_shape=sds((devices, 16, 128), BF16),
@@ -533,19 +512,32 @@
         compiler_params=params(16 if small else 32),
         name="tile_attention",
     )(patches, normed, folded, layer_scale, embed_bias, vit_out, *wv_all)
-    sent, state, embed_x, out_x = together(sent, state, embed_x, out_x)
     shares = lax.all_to_all(sent, ("tile", "seg"), 0, 0, tiled=True)
-    if small:
-        state = attention(kv_all[2:], groups[2:], state)
-    embed_all = [embed, trade(embed, "seg", 1), embed_x, trade(embed_x, "seg", 1)]
-    slide_out_all = [slide_out, trade(slide_out, "seg", 1), out_x, trade(out_x, "seg", 1)]
+    block = min(total, 2048)
+    steps = total // block
+    kv_spec = pl.BlockSpec((block, 384), lambda i: (i, 0))
+    krows_spec = pl.BlockSpec((24, block), lambda i: (0, i))
+    kv_shape = [sds((total, 384), BF16)] if small else []
+    *kv_sorted, krows, ml, acc = call(
+        functools.partial(base_attention_kernel, span, total, padded, groups),
+        out_shape=(
+            *kv_shape, sds((24, total), BF16), sds((span, 128), F32), sds((span, 256), F32),
+        ),
+        grid=(steps,),
+        in_specs=[SMEM, SMEM, VMEM, VMEM] + ([VMEM] * 4 if small else [kv_spec]),
+        out_specs=(*([kv_spec] if small else []), krows_spec, VMEM, VMEM),
+        compiler_params=params(60),
+        name="base_attention",
+    )(slide_pos, offsets, pack, q_base, *kv_all)
+    kv_sorted = kv_sorted[0] if small else kv_all[0]
 
     count = span // segs
     outs = call(
-        functools.partial(fresh_kernel, span, total, groups),
+        functools.partial(fresh_kernel, span, total),
         out_shape=(sds((count, 256), BF16),) * 4 + (sds((count, DS), F32),),
         grid=(steps,),
-        in_specs=[SMEM] * 2 + [VMEM] * 15 + [kv_spec] * len(kv_all),
+        in_specs=[SMEM] * 2 + [VMEM] * 9 + [VMEM] * 2
+        + [pl.BlockSpec((192, DV), lambda i: (0, 0))] * 4 + [kv_spec, krows_spec],
         out_specs=(VMEM,) * 5,
         scratch_shapes=[
             pltpu.VMEM((padded, DS), F32),
@@ -556,21 +548,22 @@
             pltpu.VMEM((span, 128), F32),
             pltpu.VMEM((span, 256), F32),
         ],
-        compiler_params=params(16 if small else 48),
+        compiler_params=params(60),
         name="fresh_attention",
     )(
-        slide_pos, offsets, pack, q_base, shares, final_gain, slide_gain, *weights, *state,
-        base_rows, *embed_all, *kv_all,
+        slide_pos, offsets, pack, q_base, shares, final_gain, slide_gain, *weights, ml, acc,
+        base_rows, *joined_all, kv_sorted, krows,
     )
     swapped = [outs[0]] + [trade(outs[mask], "seg", mask) for mask in range(1, 4)]
     return call(
         out_kernel,
         out_shape=sds((count, DS), BF16),
-        in_specs=[VMEM] * 9,
+        grid=(1,),
+        in_specs=[VMEM] * 5 + [pl.BlockSpec((192, DS), lambda i: (0, DV // DS))] * 4,
         out_specs=VMEM,
-        compiler_params=params(8),
+        compiler_params=params(60),
         name="slide_next",
-    )(outs[4], *swapped, *slide_out_all)
+    )(outs[4], *swapped, *joined_all)
 
 
 def solution(mesh):

time: 124 us -> 107 us (0.86)
  blocking collectives: 32.3 us -> 13.5 us
  waiting for transfers between devices: 17 us -> 32.2 us
  local copies, waits for them, and re-layouts: 15.3 us -> 1.28 us
  other arithmetic: 0.11 us -> 1.85 us
    all_to_all x1 -> x0, blocking collectives: 16.9 us -> none  [shards(): part = lax.all_to_all(part, 'tile', 0, 0, tiled=True)]
    unnamed x72 -> x28, local copies, waits for them, and re-layouts: 15.3 us -> 1.28 us
    all_to_all x0 -> x1, waiting for transfers between devices: none -> 9.68 us  [shards(): part = lax.all_to_all(part, 'tile', 0, 0, tiled=True)]
    ppermute x19 -> x16, waiting for transfers between devices: 17 us -> 22 us  [trade(): return lax.ppermute(block, axis, [(i, i ^ mask) for i in range(count)])]
    all_to_all x0 -> x1, starting transfers between devices: none -> 4.01 us  [shards(): part = lax.all_to_all(part, 'tile', 0, 0, tiled=True)]
    pallas_call x4 -> x3, Pallas kernels: 21.1 us -> 17.8 us  [the longest x1 7.91 us: shards(): call(functools.partial(fresh_kernel, span, total), out_shape=(sds((count,...]
    pallas_call x1, Pallas kernels: 0.85 us -> 3.45 us  [shards(): call(base_kernel, out_shape=(sds((span, DS), BF16), sds((span, 256), BF16...]
    all_to_all x1, starting transfers between devices: 4.86 us -> 2.9 us  [shards(): shares = lax.all_to_all(sent, ('tile', 'seg'), 0, 0, tiled=True)]
  transfers between devices with their start and end apart: 21 -> 19, of which waited for: 5 -> 6; matrix products, arithmetic and copies ran while one was open for 0% -> 2% of each run, Pallas kernels for 14% -> 13%
where the time goes in v5:
time: 107 us
  waiting for transfers between devices  32.2 us (30%)
  starting transfers between devices  29.1 us (27%)
  Pallas kernels  28.9 us (27%)
  blocking collectives  13.5 us (13%)
  other arithmetic  1.85 us (2%)
  local copies, waits for them, and re-layouts  1.28 us (1%)
    ppermute x16, waiting for transfers between devices, trade(): return lax.ppermute(block, axis, [(i, i ^ mask) for i in range(count)])  22 us
    ppermute x16, starting transfers between devices, trade(): return lax.ppermute(block, axis, [(i, i ^ mask) for i in range(count)])  18.7 us
    all_to_all x1, blocking collectives, shards(): pack = lax.all_to_all(pack, 'tile', 0, 0, tiled=True)  13.5 us
    all_to_all x1, waiting for transfers between devices, shards(): part = lax.all_to_all(part, 'tile', 0, 0, tiled=True)  9.68 us
    pallas_call x1, Pallas kernels, shards(): call(functools.partial(fresh_kernel, span, total), out_shape=(sds((count,...  7.91 us
    pallas_call x1, Pallas kernels, shards(): call(functools.partial(base_attention_kernel, span, total, padded, groups...  7.49 us
    all_to_all x1, starting transfers between devices, shards(): part = lax.all_to_all(part, 'tile', 0, 0, tiled=True)  4.01 us
    pallas_call x1, Pallas kernels, shards(): call(functools.partial(tile_kernel, cut), out_shape=sds((devices, 16, 128...  3.76 us
  transfers between devices with their start and end apart: 19, of which 6 were waited for; matrix products, arithmetic and copies ran while one was open for 2% of the time, Pallas kernels for 13%

profile of v5, /device:TPU:0, one launch (start us, length us, event | category | flops | bytes accessed | tf_op | source)
XLA Modules:
  0.0 106.9 jit_solution(17975066764169832994)
XLA Ops:
  0.0 1.7 %class_row.1 = f32[8,8,256]{2,1,0:T(8,128)} custom-call(bf16[1,257,1536]{2,1,0:T(8,128)(2,1)} %patch_ref.5, f32[1536]{0:T(1024)} %gain_ref.6, s32[8]{0:T(128)} %pos_ref.5, s32[256]{0:T(256)} %kept_ref.3), custom_call_target="tpu_custom_call" | custom-call | tf_op jit(solution)/shard_map/class_row/pallas_call | solution.py:429
  1.7 3.5 %base_rows.1 = (bf16[256,768]{1,0:T(8,128)(2,1)}, bf16[256,256]{1,0:T(8,128)(2,1)}, bf16[256,384]{1,0:T(8,128)(2,1)}, bf16[192,2304]{1,0:T(8,128)(2,1)}) custom-call(bf16[256,768]{1,0:T(8,128)(2,1)} %cached_ref, s32[256]{0:T(256)} %kept_ref.3, f32[768]{0:T(1024)} %mask_ref.1, f32[768]{0:T(1024)} %gain_ref.7, bf16[192,768]{1,0:T(8,128)(2,1)} %bitcast.4, ...), custom_call_target="tpu_custom_call" | custom-call | tf_op jit(solution)/shard_map/base_rows/pallas_call | solution.py:440
  5.2 2.9 %collective-permute-start.10 = (bf16[192,2304]{1,0:T(8,128)(2,1)}, bf16[192,2304]{1,0:T(8,128)(2,1)}, u32[]{:S(2)}, u32[]{:S(2)}) collective-permute-start(bf16[192,2304]{1,0:T(8,128)(2,1)} %get-tuple-element.44.refs_0_.refs_4_), channel_id=1, source_target_pairs={{0,2},{1,3},{2,0},{3,1},{4,6},{5,7},{6,4},{7,5},{8,10},{9,11},{10,... | collective-permute-start | bytes 2654216 | tf_op jit(solution)/shard_map/ppermute | solution.py:400
  8.1 3.6 %collective-permute-start.2 = (bf16[192,384]{1,0:T(8,128)(2,1)S(1)}, bf16[192,384]{1,0:T(8,128)(2,1)S(1)}, u32[]{:S(2)}, u32[]{:S(2)}) collective-permute-start(bf16[192,384]{1,0:T(8,128)(2,1)S(1)} %copy-done.3), channel_id=1, source_target_pairs={{0,24},{4,28},{8,16},{12,20},{16,8},{20,12},{24,0},{28,4},{1,25},{... | collective-permute-start | bytes 442376 | tf_op jit(solution)/shard_map/ppermute | solution.py:400
  11.7 0.0 collective-permute-start.1
  11.7 0.8 collective-permute-start
  12.5 13.5 %all_to_all.20.pack_ref = f32[8,8,256]{2,1,0:T(8,128)S(1)} all-to-all(f32[8,8,256]{2,1,0:T(8,128)S(1)} %copy-done.10), channel_id=1, replica_groups=mesh['tile'=8,'seg'=4] {'tile'}, dimensions={0} | all-to-all | bytes 131072 | tf_op jit(solution)/shard_map/all_to_all | solution.py:439
  26.0 0.8 query_share.1
  26.8 0.0 collective-permute-done.2
  26.8 0.0 collective-permute-done.1
  26.9 2.5 %collective-permute-start.5 = (bf16[256,384]{1,0:T(8,128)(2,1)}, bf16[256,384]{1,0:T(8,128)(2,1)S(1)}, u32[]{:S(2)}, u32[]{:S(2)}) collective-permute-start(bf16[256,384]{1,0:T(8,128)(2,1)} %get-tuple-element.35.refs_0_), channel_id=1, source_target_pairs={{0,24},{4,28},{8,16},{12,20},{16,8},{20,12},{24,0},{28,4},{1,25},{... | collective-permute-start | bytes 589832 | tf_op jit(solution)/shard_map/ppermute | solution.py:400
  29.4 0.0 collective-permute-start.4
  29.4 1.9 %collective-permute-start.3 = (bf16[256,384]{1,0:T(8,128)(2,1)}, bf16[256,384]{1,0:T(8,128)(2,1)}, u32[]{:S(2)}, u32[]{:S(2)}) collective-permute-start(bf16[256,384]{1,0:T(8,128)(2,1)} %get-tuple-element.35.refs_0_), channel_id=1, source_target_pairs={{0,8},{4,12},{8,0},{12,4},{16,24},{20,28},{24,16},{28,20},{1,9},{5... | collective-permute-start | bytes 589832 | tf_op jit(solution)/shard_map/ppermute | solution.py:400
  31.4 4.0 %all-to-all-start.1 = ((f32[8,8,384]{2,1,0:T(8,128)}), f32[8,8,384]{2,1,0:T(8,128)S(1)}, u32[]{:S(2)}, u32[]{:S(2)}) async-start(f32[8,8,384]{2,1,0:T(8,128)} %query_share.1), calls=%async_computation.1 | async-start | bytes 196608 | tf_op jit(solution)/shard_map/all_to_all | solution.py:468
  35.4 0.0 collective-permute-done.10.refs_2_.refs_6_
  35.4 0.1 collective-permute-start.11
  35.4 0.5 collective-permute-start.12
  35.9 0.9 collective-permute-done.5
  36.9 1.0 collective-permute-start.6
  37.9 9.7 %all-to-all-done.1.part_ref = f32[8,8,384]{2,1,0:T(8,128)S(1)} async-done(((f32[8,8,384]{2,1,0:T(8,128)}), f32[8,8,384]{2,1,0:T(8,128)S(1)}, u32[]{:S(2)}, u32[]{:S(2)}) %all-to-all-start.1) | async-done | bytes 98336 | tf_op jit(solution)/shard_map/all_to_all | solution.py:468
  47.6 0.8 fold_key.1
  48.4 0.0 collective-permute-done.4
  48.4 1.4 %collective-permute-start.8 = (bf16[576,384]{1,0:T(8,128)(2,1)S(1)}, bf16[576,384]{1,0:T(8,128)(2,1)}, u32[]{:S(2)}, u32[]{:S(2)}) collective-permute-start(bf16[576,384]{1,0:T(8,128)(2,1)S(1)} %pad_maximum_fusion.1.refs_1_), channel_id=1, source_target_pairs={{0,4},{4,0},{8,12},{12,8},{16,20},{20,16},{24,28},{28,24},{1,5},{5... | collective-permute-start | bytes 1327112 | tf_op jit(solution)/shard_map/ppermute | solution.py:400
  49.8 0.0 collective-permute-done.3
  49.8 1.8 %pad_maximum_fusion.refs_1_ = bf16[768,384]{1,0:T(8,128)(2,1)} fusion(bf16[256,384]{1,0:T(8,128)(2,1)S(1)} %collective-permute-done.5, bf16[256,384]{1,0:T(8,128)(2,1)S(1)} %collective-permute-done.4, bf16[256,384]{1,0:T(8,128)(2,1)} %collective-permute-done.3), kind=kLoop, calls=%fused_computation | loop fusion | flops 1769472 | bytes 1179648 | tf_op jit(solution)/shard_map/concatenate | solution.py:483
  51.6 0.7 collective-permute-start.9
  52.3 1.3 %collective-permute-start.7 = (bf16[192,384]{1,0:T(8,128)(2,1)S(1)}, bf16[192,384]{1,0:T(8,128)(2,1)}, u32[]{:S(2)}, u32[]{:S(2)}) collective-permute-start(bf16[192,384]{1,0:T(8,128)(2,1)S(1)} %copy-done.3), channel_id=1, source_target_pairs={{0,4},{4,0},{8,12},{12,8},{16,20},{20,16},{24,28},{28,24},{1,5},{5... | collective-permute-start | bytes 442376 | tf_op jit(solution)/shard_map/ppermute | solution.py:400
  53.6 3.4 %all-to-all-start.2 = ((f32[8,8,256]{2,1,0:T(8,128)}), f32[8,8,256]{2,1,0:T(8,128)S(1)}, u32[]{:S(2)}, u32[]{:S(2)}) async-start(f32[8,8,256]{2,1,0:T(8,128)} %fold_key.1), calls=%async_computation.2 | async-start | bytes 131072 | tf_op jit(solution)/shard_map/all_to_all | solution.py:502
  57.1 0.5 token_norm.1.normed_ref
  57.6 18.0 %collective-permute-done.7.refs_2_ = bf16[192,384]{1,0:T(8,128)(2,1)} collective-permute-done((bf16[192,384]{1,0:T(8,128)(2,1)S(1)}, bf16[192,384]{1,0:T(8,128)(2,1)}, u32[]{:S(2)}, u32[]{:S(2)}) %collective-permute-start.7) | collective-permute-done | bytes 147488 | tf_op jit(solution)/shard_map/ppermute | solution.py:400
  75.7 0.0 collective-permute-done.8.refs_3_
  75.7 3.8 %tile_attention.1 = bf16[32,16,128]{2,1,0:T(8,128)(2,1)} custom-call(bf16[1,257,1536]{2,1,0:T(8,128)(2,1)S(1)} %copy-done, bf16[257,1536]{1,0:T(8,128)(2,1)S(1)} %token_norm.1.normed_ref, f32[8,8,256]{2,1,0:T(8,128)S(1)} %all-to-all-done.2.fold_ref, f32[1536]{0:T(1024)S(1)} %copy-done.7, f32[192]{0:T(256)S(1)} %copy-done.8, bf16[384,1536]{1,0:T(8,128)(2,1)S(1)} %copy-done.1, ...), custom_call_target="tpu_custom_call" | custom-call | tf_op jit(solution)/shard_map/tile_attention/pallas_call | solution.py:503
  79.5 2.9 %all-to-all-start.3 = ((bf16[32,16,128]{2,1,0:T(8,128)(2,1)}), bf16[32,16,128]{2,1,0:T(8,128)(2,1)S(1)}, u32[]{:S(2)}, u32[]{:S(2)}) async-start(bf16[32,16,128]{2,1,0:T(8,128)(2,1)} %tile_attention.1), calls=%async_computation.3 | async-start | bytes 262144 | tf_op jit(solution)/shard_map/all_to_all | solution.py:515
  82.4 0.0 collective-permute-done.9.refs_3_
  82.4 7.5 %base_attention.1 = (bf16[2048,384]{1,0:T(8,128)(2,1)}, bf16[24,2048]{1,0:T(8,128)(2,1)}, f32[256,128]{1,0:T(8,128)}, f32[256,256]{1,0:T(8,128)}) custom-call(s32[8]{0:T(128)} %pos_ref.5, s32[5,12]{1,0:T(8,128)} %offset_ref.3, f32[8,8,256]{2,1,0:T(8,128)} %copy-done.2, bf16[256,256]{1,0:T(8,128)(2,1)} %get-tuple-element.31.q_ref, ...), custom_call_target="tpu_custom_call" | custom-call | tf_op jit(solution)/shard_map/base_attention/pallas_call | solution.py:521
  89.9 0.5 all-to-all-done.3.shares_ref
  90.4 0.0 collective-permute-done.11.refs_1_.refs_5_
  90.4 0.6 copy-done.9
  91.1 7.9 %fresh_attention.1 = (bf16[64,256]{1,0:T(8,128)(2,1)}, bf16[64,256]{1,0:T(8,128)(2,1)}, bf16[64,256]{1,0:T(8,128)(2,1)}, bf16[64,256]{1,0:T(8,128)(2,1)}, f32[64,768]{1,0:T(8,128)}) custom-call(s32[8]{0:T(128)} %pos_ref.5, s32[5,12]{1,0:T(8,128)} %offset_ref.3, f32[8,8,256]{2,1,0:T(8,128)} %copy-done.2, bf16[256,256]{1,0:T(8,128)(2,1)} %get-tuple-element.31.q_ref, ...), custom_call_target="tpu_custom_call" | custom-call | tf_op jit(solution)/shard_map/fresh_attention/pallas_call | solution.py:535
  99.0 0.3 collective-permute-start.13
  99.2 1.0 collective-permute-start.14
  100.2 0.6 collective-permute-start.15
  100.9 0.0 collective-permute-done.13.refs_1_
  100.9 2.5 %collective-permute-done.14.refs_2_ = bf16[64,256]{1,0:T(8,128)(2,1)S(1)} collective-permute-done((bf16[64,256]{1,0:T(8,128)(2,1)}, bf16[64,256]{1,0:T(8,128)(2,1)S(1)}, u32[]{:S(2)}, u32[]{:S(2)}) %collective-permute-start.14) | collective-permute-done | bytes 32800 | tf_op jit(solution)/shard_map/ppermute | solution.py:400
  103.4 0.5 collective-permute-done.15.refs_3_
  103.9 0.1 copy-done.12
  104.0 0.5 copy-done.13
  104.5 2.4 %slide_next.1 = bf16[64,768]{1,0:T(8,128)(2,1)} custom-call(f32[64,768]{1,0:T(8,128)} %get-tuple-element.48.mine_ref, bf16[64,256]{1,0:T(8,128)(2,1)} %get-tuple-element.49.refs_0_, bf16[64,256]{1,0:T(8,128)(2,1)} %copy-done.11, bf16[64,256]{1,0:T(8,128)(2,1)} %copy-done.12, bf16[64,256]{1,0:T(8,128)(2,1)} %copy-done.13, ...), custom_call_target="tpu_custom_call" | custom-call | tf_op jit(solution)/shard_map/slide_next/pallas_call | solution.py:558
  (30 shorter events, 0.1 us)
Async XLA Ops:
  1.7 6.4 %copy-start.3 = (bf16[192,384]{1,0:T(8,128)(2,1)S(1)}, bf16[192,384]{1,0:T(8,128)(2,1)}, u32[]{:S(2)}) copy-start(bf16[192,384]{1,0:T(8,128)(2,1)} %refs_0_) | copy-start | bytes 442372
  1.7 10.8 %copy-start.10 = (f32[8,8,256]{2,1,0:T(8,128)S(1)}, f32[8,8,256]{2,1,0:T(8,128)}, u32[]{:S(2)}) copy-start(f32[8,8,256]{2,1,0:T(8,128)} %class_row.1) | copy-start | bytes 196612
  1.7 24.3 %copy-start.4 = (bf16[192,384]{1,0:T(8,128)(2,1)S(1)}, bf16[192,384]{1,0:T(8,128)(2,1)}, u32[]{:S(2)}) copy-start(bf16[192,384]{1,0:T(8,128)(2,1)} %wq_ref.1) | copy-start | bytes 442372
  5.2 42.4 %copy-start.5 = (bf16[192,384]{1,0:T(8,128)(2,1)S(1)}, bf16[192,384]{1,0:T(8,128)(2,1)}, u32[]{:S(2)}) copy-start(bf16[192,384]{1,0:T(8,128)(2,1)} %wk_ref.1) | copy-start | bytes 442372
  5.2 30.2 %collective-permute-start.10 = (bf16[192,2304]{1,0:T(8,128)(2,1)}, bf16[192,2304]{1,0:T(8,128)(2,1)}, u32[]{:S(2)}, u32[]{:S(2)}) collective-permute-start(bf16[192,2304]{1,0:T(8,128)(2,1)} %get-tuple-element.44.refs_0_.refs_4_), channel_id=1, source_target_pairs={{0,2},{1,3},{2,0},{3,1},{4,6},{5,7},{6,4},{7,5},{8,10},{9,11},{10,... | collective-permute-start | bytes 2654216 | tf_op jit(solution)/shard_map/ppermute | solution.py:400
  8.1 18.7 %collective-permute-start.2 = (bf16[192,384]{1,0:T(8,128)(2,1)S(1)}, bf16[192,384]{1,0:T(8,128)(2,1)S(1)}, u32[]{:S(2)}, u32[]{:S(2)}) collective-permute-start(bf16[192,384]{1,0:T(8,128)(2,1)S(1)} %copy-done.3), channel_id=1, source_target_pairs={{0,24},{4,28},{8,16},{12,20},{16,8},{20,12},{24,0},{28,4},{1,25},{... | collective-permute-start | bytes 442376 | tf_op jit(solution)/shard_map/ppermute | solution.py:400
  11.7 15.1 %collective-permute-start.1 = (bf16[192,384]{1,0:T(8,128)(2,1)S(1)}, bf16[192,384]{1,0:T(8,128)(2,1)S(1)}, u32[]{:S(2)}, u32[]{:S(2)}) collective-permute-start(bf16[192,384]{1,0:T(8,128)(2,1)S(1)} %copy-done.3), channel_id=1, source_target_pairs={{0,16},{4,20},{8,24},{12,28},{16,0},{20,4},{24,8},{28,12},{1,17},{... | collective-permute-start | bytes 442376 | tf_op jit(solution)/shard_map/ppermute | solution.py:400
  11.7 15.1 %collective-permute-start = (bf16[192,384]{1,0:T(8,128)(2,1)S(1)}, bf16[192,384]{1,0:T(8,128)(2,1)S(1)}, u32[]{:S(2)}, u32[]{:S(2)}) collective-permute-start(bf16[192,384]{1,0:T(8,128)(2,1)S(1)} %copy-done.3), channel_id=1, source_target_pairs={{0,8},{4,12},{8,0},{12,4},{16,24},{20,28},{24,16},{28,20},{1,9},{5... | collective-permute-start | bytes 442376 | tf_op jit(solution)/shard_map/ppermute | solution.py:400
  26.0 25.6 %copy-start.2 = (f32[8,8,256]{2,1,0:T(8,128)}, f32[8,8,256]{2,1,0:T(8,128)S(1)}, u32[]{:S(2)}) copy-start(f32[8,8,256]{2,1,0:T(8,128)S(1)} %all_to_all.20.pack_ref) | copy-start | bytes 196612
  26.8 30.3 %copy-start = (bf16[1,257,1536]{2,1,0:T(8,128)(2,1)S(1)}, bf16[1,257,1536]{2,1,0:T(8,128)(2,1)}, u32[]{:S(2)}) copy-start(bf16[1,257,1536]{2,1,0:T(8,128)(2,1)} %patch_ref.5) | copy-start | bytes 2368516
  26.8 30.3 %copy-start.6 = (f32[1536]{0:T(1024)S(1)}, f32[1536]{0:T(1024)}, u32[]{:S(2)}) copy-start(f32[1536]{0:T(1024)} %gain_ref.6) | copy-start | bytes 18436
  26.9 10.0 %collective-permute-start.5 = (bf16[256,384]{1,0:T(8,128)(2,1)}, bf16[256,384]{1,0:T(8,128)(2,1)S(1)}, u32[]{:S(2)}, u32[]{:S(2)}) collective-permute-start(bf16[256,384]{1,0:T(8,128)(2,1)} %get-tuple-element.35.refs_0_), channel_id=1, source_target_pairs={{0,24},{4,28},{8,16},{12,20},{16,8},{20,12},{24,0},{28,4},{1,25},{... | collective-permute-start | bytes 589832 | tf_op jit(solution)/shard_map/ppermute | solution.py:400
  29.4 19.0 %collective-permute-start.4 = (bf16[256,384]{1,0:T(8,128)(2,1)}, bf16[256,384]{1,0:T(8,128)(2,1)S(1)}, u32[]{:S(2)}, u32[]{:S(2)}) collective-permute-start(bf16[256,384]{1,0:T(8,128)(2,1)} %get-tuple-element.35.refs_0_), channel_id=1, source_target_pairs={{0,16},{4,20},{8,24},{12,28},{16,0},{20,4},{24,8},{28,12},{1,17},{... | collective-permute-start | bytes 589832 | tf_op jit(solution)/shard_map/ppermute | solution.py:400
  29.4 20.4 %collective-permute-start.3 = (bf16[256,384]{1,0:T(8,128)(2,1)}, bf16[256,384]{1,0:T(8,128)(2,1)}, u32[]{:S(2)}, u32[]{:S(2)}) collective-permute-start(bf16[256,384]{1,0:T(8,128)(2,1)} %get-tuple-element.35.refs_0_), channel_id=1, source_target_pairs={{0,8},{4,12},{8,0},{12,4},{16,24},{20,28},{24,16},{28,20},{1,9},{5... | collective-permute-start | bytes 589832 | tf_op jit(solution)/shard_map/ppermute | solution.py:400
  31.4 16.2 %all-to-all-start.1 = ((f32[8,8,384]{2,1,0:T(8,128)}), f32[8,8,384]{2,1,0:T(8,128)S(1)}, u32[]{:S(2)}, u32[]{:S(2)}) async-start(f32[8,8,384]{2,1,0:T(8,128)} %query_share.1), calls=%async_computation.1 | async-start | bytes 196608 | tf_op jit(solution)/shard_map/all_to_all | solution.py:468
  35.4 55.0 %collective-permute-start.11 = (bf16[192,2304]{1,0:T(8,128)(2,1)}, bf16[192,2304]{1,0:T(8,128)(2,1)}, u32[]{:S(2)}, u32[]{:S(2)}) collective-permute-start(bf16[192,2304]{1,0:T(8,128)(2,1)} %get-tuple-element.44.refs_0_.refs_4_), channel_id=1, source_target_pairs={{0,1},{1,0},{2,3},{3,2},{4,5},{5,4},{6,7},{7,6},{8,9},{9,8},{10,11... | collective-permute-start | bytes 2654216 | tf_op jit(solution)/shard_map/ppermute | solution.py:400
  35.4 55.0 %collective-permute-start.12 = (bf16[192,2304]{1,0:T(8,128)(2,1)}, bf16[192,2304]{1,0:T(8,128)(2,1)}, u32[]{:S(2)}, u32[]{:S(2)}) collective-permute-start(bf16[192,2304]{1,0:T(8,128)(2,1)} %collective-permute-done.10.refs_2_.refs_6_), channel_id=1, source_target_pairs={{0,1},{1,0},{2,3},{3,2},{4,5},{5,4},{6,7},{7,6},{8,9},{9,8},{10,11... | collective-permute-start | bytes 2654216 | tf_op jit(solution)/shard_map/ppermute | solution.py:400
  36.9 14.8 %collective-permute-start.6 = (bf16[256,384]{1,0:T(8,128)(2,1)}, bf16[256,384]{1,0:T(8,128)(2,1)}, u32[]{:S(2)}, u32[]{:S(2)}) collective-permute-start(bf16[256,384]{1,0:T(8,128)(2,1)} %get-tuple-element.35.refs_0_), channel_id=1, source_target_pairs={{0,4},{4,0},{8,12},{12,8},{16,20},{20,16},{24,28},{28,24},{1,5},{5... | collective-permute-start | bytes 589832 | tf_op jit(solution)/shard_map/ppermute | solution.py:400
  48.4 27.3 %copy-start.1 = (bf16[384,1536]{1,0:T(8,128)(2,1)S(1)}, bf16[384,1536]{1,0:T(8,128)(2,1)}, u32[]{:S(2)}) copy-start(bf16[384,1536]{1,0:T(8,128)(2,1)} %wo_ref.1) | copy-start | bytes 3538948
  48.4 27.3 %copy-start.7 = (f32[1536]{0:T(1024)S(1)}, f32[1536]{0:T(1024)}, u32[]{:S(2)}) copy-start(f32[1536]{0:T(1024)} %scale_ref.1) | copy-start | bytes 18436
  48.4 27.3 %copy-start.8 = (f32[192]{0:T(256)S(1)}, f32[192]{0:T(256)}, u32[]{:S(2)}) copy-start(f32[192]{0:T(256)} %bias_ref.1) | copy-start | bytes 2308
  48.4 27.3 %collective-permute-start.8 = (bf16[576,384]{1,0:T(8,128)(2,1)S(1)}, bf16[576,384]{1,0:T(8,128)(2,1)}, u32[]{:S(2)}, u32[]{:S(2)}) collective-permute-start(bf16[576,384]{1,0:T(8,128)(2,1)S(1)} %pad_maximum_fusion.1.refs_1_), channel_id=1, source_target_pairs={{0,4},{4,0},{8,12},{12,8},{16,20},{20,16},{24,28},{28,24},{1,5},{5... | collective-permute-start | bytes 1327112 | tf_op jit(solution)/shard_map/ppermute | solution.py:400
  51.6 30.7 %collective-permute-start.9 = (bf16[768,384]{1,0:T(8,128)(2,1)}, bf16[768,384]{1,0:T(8,128)(2,1)}, u32[]{:S(2)}, u32[]{:S(2)}) collective-permute-start(bf16[768,384]{1,0:T(8,128)(2,1)} %pad_maximum_fusion.refs_1_), channel_id=1, source_target_pairs={{0,4},{4,0},{8,12},{12,8},{16,20},{20,16},{24,28},{28,24},{1,5},{5... | collective-permute-start | bytes 1769480 | tf_op jit(solution)/shard_map/ppermute | solution.py:400
  52.3 23.3 %collective-permute-start.7 = (bf16[192,384]{1,0:T(8,128)(2,1)S(1)}, bf16[192,384]{1,0:T(8,128)(2,1)}, u32[]{:S(2)}, u32[]{:S(2)}) collective-permute-start(bf16[192,384]{1,0:T(8,128)(2,1)S(1)} %copy-done.3), channel_id=1, source_target_pairs={{0,4},{4,0},{8,12},{12,8},{16,20},{20,16},{24,28},{28,24},{1,5},{5... | collective-permute-start | bytes 442376 | tf_op jit(solution)/shard_map/ppermute | solution.py:400
  53.6 22.0 %all-to-all-start.2 = ((f32[8,8,256]{2,1,0:T(8,128)}), f32[8,8,256]{2,1,0:T(8,128)S(1)}, u32[]{:S(2)}, u32[]{:S(2)}) async-start(f32[8,8,256]{2,1,0:T(8,128)} %fold_key.1), calls=%async_computation.2 | async-start | bytes 131072 | tf_op jit(solution)/shard_map/all_to_all | solution.py:502
  79.5 11.0 %all-to-all-start.3 = ((bf16[32,16,128]{2,1,0:T(8,128)(2,1)}), bf16[32,16,128]{2,1,0:T(8,128)(2,1)S(1)}, u32[]{:S(2)}, u32[]{:S(2)}) async-start(bf16[32,16,128]{2,1,0:T(8,128)(2,1)} %tile_attention.1), calls=%async_computation.3 | async-start | bytes 262144 | tf_op jit(solution)/shard_map/all_to_all | solution.py:515
  90.4 0.7 copy-start.9
  99.0 1.9 %collective-permute-start.13 = (bf16[64,256]{1,0:T(8,128)(2,1)}, bf16[64,256]{1,0:T(8,128)(2,1)S(1)}, u32[]{:S(2)}, u32[]{:S(2)}) collective-permute-start(bf16[64,256]{1,0:T(8,128)(2,1)} %get-tuple-element.50), channel_id=1, source_target_pairs={{0,1},{1,0},{2,3},{3,2},{4,5},{5,4},{6,7},{7,6},{8,9},{9,8},{10,11... | collective-permute-start | bytes 98312 | tf_op jit(solution)/shard_map/ppermute | solution.py:400
  99.2 4.1 %collective-permute-start.14 = (bf16[64,256]{1,0:T(8,128)(2,1)}, bf16[64,256]{1,0:T(8,128)(2,1)S(1)}, u32[]{:S(2)}, u32[]{:S(2)}) collective-permute-start(bf16[64,256]{1,0:T(8,128)(2,1)} %get-tuple-element.51), channel_id=1, source_target_pairs={{0,2},{1,3},{2,0},{3,1},{4,6},{5,7},{6,4},{7,5},{8,10},{9,11},{10,... | collective-permute-start | bytes 98312 | tf_op jit(solution)/shard_map/ppermute | solution.py:400
  100.2 3.7 %collective-permute-start.15 = (bf16[64,256]{1,0:T(8,128)(2,1)}, bf16[64,256]{1,0:T(8,128)(2,1)S(1)}, u32[]{:S(2)}, u32[]{:S(2)}) collective-permute-start(bf16[64,256]{1,0:T(8,128)(2,1)} %get-tuple-element.52), channel_id=1, source_target_pairs={{0,3},{1,2},{2,1},{3,0},{4,7},{5,6},{6,5},{7,4},{8,11},{9,10},{10,... | collective-permute-start | bytes 98312 | tf_op jit(solution)/shard_map/ppermute | solution.py:400
  100.9 3.0 %copy-start.11 = (bf16[64,256]{1,0:T(8,128)(2,1)}, bf16[64,256]{1,0:T(8,128)(2,1)S(1)}, u32[]{:S(2)}) copy-start(bf16[64,256]{1,0:T(8,128)(2,1)S(1)} %collective-permute-done.13.refs_1_) | copy-start | bytes 98308
  103.4 0.6 copy-start.12
  103.9 0.6 copy-start.13

commit v6 on v5

--- a/solution.py
+++ b/solution.py
@@ -21,6 +21,7 @@
 I32 = jnp.int32
 VMEM = pl.BlockSpec(memory_space=pltpu.VMEM)
 SMEM = pl.BlockSpec(memory_space=pltpu.SMEM)
+ANY = pl.BlockSpec(memory_space=pl.ANY)
 NT = (((1,), (1,)), ((), ()))
 MIB = 1024 * 1024
 
@@ -99,7 +100,8 @@
     kv_ref[:, 256:384] = v[:, 0:128]
 
 
-def query_kernel(cut, pack_ref, wq_ref, part_ref):
+def query_kernel(cut, pack_ref, wq_ref, *refs):
+    part_ref = refs[-1]
     rows = pack_ref[:, 0, 0:cut].astype(BF16)
     part = dot(rows, wq_ref[...])
     if len(part_ref.shape) == 3:
@@ -108,7 +110,8 @@
         part_ref[...] = part
 
 
-def fold_kernel(part_ref, wk_ref, fold_ref):
+def fold_kernel(part_ref, wk_ref, *refs):
+    fold_ref = refs[-1]
     if len(part_ref.shape) == 3:
         queries = part_ref[0]
         for index in range(1, part_ref.shape[0]):
@@ -126,6 +129,10 @@
     fold_ref[:, :, 0:cut] = result
     if cut < fold_ref.shape[2]:
         fold_ref[:, :, cut:] = jnp.zeros((tiles, 8, fold_ref.shape[2] - cut), F32)
+
+
+def gate_kernel(*refs):
+    del refs
 
 
 def token_kernel(patch_ref, gain_ref, normed_ref):
@@ -454,15 +461,16 @@
         value_y = trade(value, "tile", 1)
         kv_y = trade(kv_base, "tile", 1)
 
+    due = [value_y] if small else []
     part_shape = (tiles, fresh, local_cols) if small else (fresh, local_cols)
     part = call(
         functools.partial(query_kernel, cut),
         out_shape=sds(part_shape, F32),
-        in_specs=[VMEM] * 2,
+        in_specs=[VMEM] * 2 + [ANY] * len(due),
         out_specs=VMEM,
         compiler_params=params(8 if small else 16),
         name="query_share",
-    )(pack, vit_query)
+    )(pack, vit_query, *due)
     if small:
         part, value_z, kv_own = together(part, value_z, kv_base)
         part = lax.all_to_all(part, "tile", 0, 0, tiled=True)
@@ -484,32 +492,43 @@
     else:
         wv_all = [lax.all_gather(value, "tile", axis=0, tiled=True)]
 
+    due = [kv_y, wv_all[3]] if small else []
     folded = call(
         fold_kernel,
         out_shape=sds((fresh, 8, round_up(cut, 128)), F32),
-        in_specs=[VMEM] * 2,
+        in_specs=[VMEM] * 2 + [ANY] * len(due),
         out_specs=VMEM,
         compiler_params=params(8 if small else 16),
         name="fold_key",
-    )(part, vit_key)
+    )(part, vit_key, *due)
     if small:
-        folded, kv_z, kv_y = together(folded, kv_z, kv_y)
-        kv_all = [kv_own, kv_z, kv_y, trade(kv_z, "tile", 1)]
         groups = GROUPS
     else:
         kv_all = [lax.all_gather(kv_base, "tile", axis=0, tiled=True)]
         groups = (None,)
     folded = lax.all_to_all(folded, "tile", 0, 0, tiled=True)
+    if small:
+        kv_z = call(
+            gate_kernel,
+            out_shape=sds(kv_z.shape, kv_z.dtype),
+            in_specs=[ANY] * 2,
+            out_specs=ANY,
+            input_output_aliases={0: 0},
+            compiler_params=params(8),
+            name="third_over",
+        )(kv_z, folded)
+        kv_all = [kv_own, kv_z, kv_y, trade(kv_z, "tile", 1)]
     sent = call(
         functools.partial(tile_kernel, cut),
         out_shape=sds((devices, 16, 128), BF16),
-        in_specs=[VMEM] * (6 + len(wv_all)),
+        grid=(1,),
+        in_specs=[pl.BlockSpec((1, 16, DV), lambda i: (0, 0, 0))] + [VMEM] * (5 + len(wv_all)),
         out_specs=VMEM,
         scratch_shapes=[
             pltpu.VMEM((8, DV), F32), pltpu.VMEM((tiles, 8, round_up(cut, 128)), F32),
             pltpu.VMEM((16, 128), F32),
         ],
-        compiler_params=params(16 if small else 32),
+        compiler_params=params(60),
         name="tile_attention",
     )(patches, normed, folded, layer_scale, embed_bias, vit_out, *wv_all)
     shares = lax.all_to_all(sent, ("tile", "seg"), 0, 0, tiled=True)

time: 107 us -> 97.4 us (0.910)
  waiting for transfers between devices: 32.2 us -> 22.2 us
    ppermute x16, waiting for transfers between devices: 22 us -> 10.5 us  [trade(): return lax.ppermute(block, axis, [(i, i ^ mask) for i in range(count)])]
    all_to_all x1, waiting for transfers between devices: 0.01 us -> 5.81 us  [shards(): folded = lax.all_to_all(folded, 'tile', 0, 0, tiled=True)]
    all_to_all x1, waiting for transfers between devices: 9.68 us -> 5.94 us  [shards(): part = lax.all_to_all(part, 'tile', 0, 0, tiled=True)]
    unnamed x28 -> x38, local copies, waits for them, and re-layouts: 1.28 us -> 2.18 us
  transfers between devices with their start and end apart: 19 -> 19, of which waited for: 6 -> 5; matrix products, arithmetic and copies ran while one was open for 2% -> 1% of each run, Pallas kernels for 13% -> 15%
where the time goes in v6:
time: 97.4 us; the launch traced here: 96.8 us
  Pallas kernels  29.6 us (30%)
  starting transfers between devices  28.9 us (30%)
  waiting for transfers between devices  22.2 us (23%)
  blocking collectives  12.5 us (13%)
  local copies, waits for them, and re-layouts  2.18 us (2%)
  other arithmetic  1.2 us (1%)
    ppermute x16, starting transfers between devices, trade(): return lax.ppermute(block, axis, [(i, i ^ mask) for i in range(count)])  18.2 us
    all_to_all x1, blocking collectives, shards(): pack = lax.all_to_all(pack, 'tile', 0, 0, tiled=True)  12.5 us
    ppermute x16, waiting for transfers between devices, trade(): return lax.ppermute(block, axis, [(i, i ^ mask) for i in range(count)])  10.5 us
    pallas_call x1, Pallas kernels, shards(): call(functools.partial(fresh_kernel, span, total), out_shape=(sds((count,...  7.91 us
    pallas_call x1, Pallas kernels, shards(): call(functools.partial(base_attention_kernel, span, total, padded, groups...  7.46 us
    all_to_all x1, waiting for transfers between devices, shards(): part = lax.all_to_all(part, 'tile', 0, 0, tiled=True)  5.94 us
    all_to_all x1, waiting for transfers between devices, shards(): folded = lax.all_to_all(folded, 'tile', 0, 0, tiled=True)  5.81 us
    all_to_all x1, starting transfers between devices, shards(): part = lax.all_to_all(part, 'tile', 0, 0, tiled=True)  4.56 us
  transfers between devices with their start and end apart: 19, of which 5 were waited for; matrix products, arithmetic and copies ran while one was open for 1% of the time, Pallas kernels for 15%

profile of v6, /device:TPU:0, one launch (start us, length us, event | category | flops | bytes accessed | tf_op | source)
XLA Modules:
  0.0 96.8 jit_solution(18328990684348332329)
XLA Ops:
  0.0 1.7 %class_row.1 = f32[8,8,256]{2,1,0:T(8,128)} custom-call(bf16[1,257,1536]{2,1,0:T(8,128)(2,1)} %patch_ref.5, f32[1536]{0:T(1024)} %gain_ref.6, s32[8]{0:T(128)} %pos_ref.5, s32[256]{0:T(256)} %kept_ref.3), custom_call_target="tpu_custom_call" | custom-call | tf_op jit(solution)/shard_map/class_row/pallas_call | solution.py:436
  1.7 3.4 %base_rows.1 = (bf16[256,768]{1,0:T(8,128)(2,1)}, bf16[256,256]{1,0:T(8,128)(2,1)}, bf16[256,384]{1,0:T(8,128)(2,1)}, bf16[192,2304]{1,0:T(8,128)(2,1)}) custom-call(bf16[256,768]{1,0:T(8,128)(2,1)} %cached_ref, s32[256]{0:T(256)} %kept_ref.3, f32[768]{0:T(1024)} %mask_ref.1, f32[768]{0:T(1024)} %gain_ref.7, bf16[192,768]{1,0:T(8,128)(2,1)} %bitcast.4, ...), custom_call_target="tpu_custom_call" | custom-call | tf_op jit(solution)/shard_map/base_rows/pallas_call | solution.py:447
  5.2 3.0 %collective-permute-start.10 = (bf16[192,2304]{1,0:T(8,128)(2,1)}, bf16[192,2304]{1,0:T(8,128)(2,1)}, u32[]{:S(2)}, u32[]{:S(2)}) collective-permute-start(bf16[192,2304]{1,0:T(8,128)(2,1)} %get-tuple-element.38.refs_0_.refs_4_), channel_id=1, source_target_pairs={{0,2},{1,3},{2,0},{3,1},{4,6},{5,7},{6,4},{7,5},{8,10},{9,11},{10,... | collective-permute-start | bytes 2654216 | tf_op jit(solution)/shard_map/ppermute | solution.py:407
  8.2 1.5 %collective-permute-start = (bf16[192,384]{1,0:T(8,128)(2,1)S(1)}, bf16[192,384]{1,0:T(8,128)(2,1)S(1)}, u32[]{:S(2)}, u32[]{:S(2)}) collective-permute-start(bf16[192,384]{1,0:T(8,128)(2,1)S(1)} %copy-done.15), channel_id=1, source_target_pairs={{0,4},{4,0},{8,12},{12,8},{16,20},{20,16},{24,28},{28,24},{1,5},{5... | collective-permute-start | bytes 442376 | tf_op jit(solution)/shard_map/ppermute | solution.py:407
  9.7 3.6 %collective-permute-start.3 = (bf16[192,384]{1,0:T(8,128)(2,1)S(1)}, bf16[192,384]{1,0:T(8,128)(2,1)S(1)}, u32[]{:S(2)}, u32[]{:S(2)}) collective-permute-start(bf16[192,384]{1,0:T(8,128)(2,1)S(1)} %copy-done.15), channel_id=1, source_target_pairs={{0,24},{4,28},{8,16},{12,20},{16,8},{20,12},{24,0},{28,4},{1,25},{... | collective-permute-start | bytes 442376 | tf_op jit(solution)/shard_map/ppermute | solution.py:407
  13.3 0.0 collective-permute-start.2
  13.3 0.8 collective-permute-start.1
  14.1 12.5 %all_to_all.20.pack_ref = f32[8,8,256]{2,1,0:T(8,128)S(1)} all-to-all(f32[8,8,256]{2,1,0:T(8,128)S(1)} %copy-done.14), channel_id=1, replica_groups=mesh['tile'=8,'seg'=4] {'tile'}, dimensions={0} | all-to-all | bytes 131072 | tf_op jit(solution)/shard_map/all_to_all | solution.py:446
  26.6 0.0 collective-permute-done.refs_0_.refs_2_
  26.6 0.8 query_share.1
  27.4 0.0 collective-permute-done.3
  27.4 0.0 collective-permute-done.2
  27.4 0.0 collective-permute-done.1
  27.5 1.4 %collective-permute-start.5 = (bf16[576,384]{1,0:T(8,128)(2,1)S(1)}, bf16[576,384]{1,0:T(8,128)(2,1)S(1)}, u32[]{:S(2)}, u32[]{:S(2)}) collective-permute-start(bf16[576,384]{1,0:T(8,128)(2,1)S(1)} %pad_maximum_fusion.1.refs_1_), channel_id=1, source_target_pairs={{0,4},{4,0},{8,12},{12,8},{16,20},{20,16},{24,28},{28,24},{1,5},{5... | collective-permute-start | bytes 1327112 | tf_op jit(solution)/shard_map/ppermute | solution.py:407
  28.9 0.7 collective-permute-start.4
  29.6 2.5 %collective-permute-start.8 = (bf16[256,384]{1,0:T(8,128)(2,1)}, bf16[256,384]{1,0:T(8,128)(2,1)S(1)}, u32[]{:S(2)}, u32[]{:S(2)}) collective-permute-start(bf16[256,384]{1,0:T(8,128)(2,1)} %get-tuple-element.33.refs_0_), channel_id=1, source_target_pairs={{0,24},{4,28},{8,16},{12,20},{16,8},{20,12},{24,0},{28,4},{1,25},{... | collective-permute-start | bytes 589832 | tf_op jit(solution)/shard_map/ppermute | solution.py:407
  32.1 0.0 collective-permute-start.7
  32.1 0.0 collective-permute-done.10.refs_2_.refs_6_
  32.1 1.9 %collective-permute-start.6 = (bf16[256,384]{1,0:T(8,128)(2,1)}, bf16[256,384]{1,0:T(8,128)(2,1)}, u32[]{:S(2)}, u32[]{:S(2)}) collective-permute-start(bf16[256,384]{1,0:T(8,128)(2,1)} %get-tuple-element.33.refs_0_), channel_id=1, source_target_pairs={{0,8},{4,12},{8,0},{12,4},{16,24},{20,28},{24,16},{28,20},{1,9},{5... | collective-permute-start | bytes 589832 | tf_op jit(solution)/shard_map/ppermute | solution.py:407
  34.0 4.6 %all-to-all-start.1 = ((f32[8,8,384]{2,1,0:T(8,128)}), f32[8,8,384]{2,1,0:T(8,128)S(1)}, u32[]{:S(2)}, u32[]{:S(2)}) async-start(f32[8,8,384]{2,1,0:T(8,128)} %query_share.1), calls=%async_computation.1 | async-start | bytes 196608 | tf_op jit(solution)/shard_map/all_to_all | solution.py:476
  38.6 4.7 %collective-permute-done.4.refs_0_.refs_2_ = bf16[256,384]{1,0:T(8,128)(2,1)S(1)} collective-permute-done((bf16[256,384]{1,0:T(8,128)(2,1)}, bf16[256,384]{1,0:T(8,128)(2,1)S(1)}, u32[]{:S(2)}, u32[]{:S(2)}) %collective-permute-start.4) | collective-permute-done | bytes 196640 | tf_op jit(solution)/shard_map/ppermute | solution.py:407
  43.2 0.0 collective-permute-start.11
  43.3 0.5 collective-permute-start.12
  43.7 5.9 %all-to-all-done.1.part_ref = f32[8,8,384]{2,1,0:T(8,128)S(1)} async-done(((f32[8,8,384]{2,1,0:T(8,128)}), f32[8,8,384]{2,1,0:T(8,128)S(1)}, u32[]{:S(2)}, u32[]{:S(2)}) %all-to-all-start.1) | async-done | bytes 98336 | tf_op jit(solution)/shard_map/all_to_all | solution.py:476
  49.7 0.8 fold_key.1
  50.5 3.4 %all-to-all-start.2 = ((f32[8,8,256]{2,1,0:T(8,128)}), f32[8,8,256]{2,1,0:T(8,128)S(1)}, u32[]{:S(2)}, u32[]{:S(2)}) async-start(f32[8,8,256]{2,1,0:T(8,128)} %fold_key.1), calls=%async_computation.2 | async-start | bytes 131072 | tf_op jit(solution)/shard_map/all_to_all | solution.py:509
  54.0 0.0 copy-start.10
  54.0 0.0 collective-permute-done.7
  54.0 0.0 collective-permute-done.6
  54.0 1.1 %pad_maximum_fusion.refs_0_ = bf16[768,384]{1,0:T(8,128)(2,1)S(1)} fusion(bf16[256,384]{1,0:T(8,128)(2,1)S(1)} %collective-permute-done.8, bf16[256,384]{1,0:T(8,128)(2,1)} %collective-permute-done.7, bf16[256,384]{1,0:T(8,128)(2,1)} %collective-permute-done.6), kind=kLoop, calls=%fused_computation | loop fusion | flops 1769472 | bytes 1179648 | tf_op jit(solution)/shard_map/concatenate | solution.py:491
  55.2 5.8 %all-to-all-done.2.fold_ref.refs_1_ = f32[8,8,256]{2,1,0:T(8,128)S(1)} async-done(((f32[8,8,256]{2,1,0:T(8,128)}), f32[8,8,256]{2,1,0:T(8,128)S(1)}, u32[]{:S(2)}, u32[]{:S(2)}) %all-to-all-start.2) | async-done | bytes 65568 | tf_op jit(solution)/shard_map/all_to_all | solution.py:509
  61.0 0.4 collective-permute-start.9
  61.4 0.5 token_norm.1.normed_ref
  61.9 0.9 copy-done.2
  62.8 4.5 %tile_attention.1 = bf16[32,16,128]{2,1,0:T(8,128)(2,1)} custom-call(bf16[1,257,1536]{2,1,0:T(8,128)(2,1)} %patch_ref.5, bf16[257,1536]{1,0:T(8,128)(2,1)} %copy-done.2, f32[8,8,256]{2,1,0:T(8,128)} %copy-done.6, f32[1536]{0:T(1024)} %scale_ref.1, f32[192]{0:T(256)} %bias_ref.1, bf16[384,1536]{1,0:T(8,128)(2,1)} %wo_ref.1, bf16[192,384]{1,0:T(8,128)(2,1)} %refs_0_, ...), custom_call_target="tpu_custom_call" | custom-call | tf_op jit(solution)/shard_map/tile_attention/pallas_call | solution.py:521
  67.3 2.7 %all-to-all-start.3 = ((bf16[32,16,128]{2,1,0:T(8,128)(2,1)}), bf16[32,16,128]{2,1,0:T(8,128)(2,1)S(1)}, u32[]{:S(2)}, u32[]{:S(2)}) async-start(bf16[32,16,128]{2,1,0:T(8,128)(2,1)} %tile_attention.1), calls=%async_computation.3 | async-start | bytes 262144 | tf_op jit(solution)/shard_map/all_to_all | solution.py:534
  70.1 3.2 %collective-permute-done.9.refs_3_ = bf16[768,384]{1,0:T(8,128)(2,1)} collective-permute-done((bf16[768,384]{1,0:T(8,128)(2,1)S(1)}, bf16[768,384]{1,0:T(8,128)(2,1)}, u32[]{:S(2)}, u32[]{:S(2)}) %collective-permute-start.9) | collective-permute-done | bytes 589856 | tf_op jit(solution)/shard_map/ppermute | solution.py:407
  73.3 7.5 %base_attention.1 = (bf16[2048,384]{1,0:T(8,128)(2,1)}, bf16[24,2048]{1,0:T(8,128)(2,1)}, f32[256,128]{1,0:T(8,128)}, f32[256,256]{1,0:T(8,128)}) custom-call(s32[8]{0:T(128)} %pos_ref.5, s32[5,12]{1,0:T(8,128)} %offset_ref.3, f32[8,8,256]{2,1,0:T(8,128)} %copy-done.4, bf16[256,256]{1,0:T(8,128)(2,1)} %get-tuple-element.28.q_ref, ...), custom_call_target="tpu_custom_call" | custom-call | tf_op jit(solution)/shard_map/base_attention/pallas_call | solution.py:540
  80.8 0.0 all-to-all-done.3.shares_ref
  80.8 0.6 copy-done.13
  81.4 7.9 %fresh_attention.1 = (bf16[64,256]{1,0:T(8,128)(2,1)}, bf16[64,256]{1,0:T(8,128)(2,1)}, bf16[64,256]{1,0:T(8,128)(2,1)}, bf16[64,256]{1,0:T(8,128)(2,1)}, f32[64,768]{1,0:T(8,128)}) custom-call(s32[8]{0:T(128)} %pos_ref.5, s32[5,12]{1,0:T(8,128)} %offset_ref.3, f32[8,8,256]{2,1,0:T(8,128)} %copy-done.4, bf16[256,256]{1,0:T(8,128)(2,1)} %get-tuple-element.28.q_ref, ...), custom_call_target="tpu_custom_call" | custom-call | tf_op jit(solution)/shard_map/fresh_attention/pallas_call | solution.py:554
  89.3 0.1 collective-permute-start.13
  89.4 0.5 collective-permute-start.14
  89.9 1.4 %collective-permute-start.15 = (bf16[64,256]{1,0:T(8,128)(2,1)}, bf16[64,256]{1,0:T(8,128)(2,1)S(1)}, u32[]{:S(2)}, u32[]{:S(2)}) collective-permute-start(bf16[64,256]{1,0:T(8,128)(2,1)} %get-tuple-element.46), channel_id=1, source_target_pairs={{0,3},{1,2},{2,1},{3,0},{4,7},{5,6},{6,5},{7,4},{8,11},{9,10},{10,... | collective-permute-start | bytes 98312 | tf_op jit(solution)/shard_map/ppermute | solution.py:407
  91.3 2.5 %collective-permute-done.14.refs_2_ = bf16[64,256]{1,0:T(8,128)(2,1)S(1)} collective-permute-done((bf16[64,256]{1,0:T(8,128)(2,1)}, bf16[64,256]{1,0:T(8,128)(2,1)S(1)}, u32[]{:S(2)}, u32[]{:S(2)}) %collective-permute-start.14) | collective-permute-done | bytes 32800 | tf_op jit(solution)/shard_map/ppermute | solution.py:407
  93.8 0.6 copy-done.17
  94.4 0.0 copy-done.18
  94.4 2.4 %slide_next.1 = bf16[64,768]{1,0:T(8,128)(2,1)} custom-call(f32[64,768]{1,0:T(8,128)} %get-tuple-element.42.mine_ref, bf16[64,256]{1,0:T(8,128)(2,1)} %get-tuple-element.43.refs_0_, bf16[64,256]{1,0:T(8,128)(2,1)} %copy-done.16, bf16[64,256]{1,0:T(8,128)(2,1)} %copy-done.17, bf16[64,256]{1,0:T(8,128)(2,1)} %copy-done.18, ...), custom_call_target="tpu_custom_call" | custom-call | tf_op jit(solution)/shard_map/slide_next/pallas_call | solution.py:577
  (41 shorter events, 0.1 us)
Async XLA Ops:
  1.7 6.4 %copy-start.15 = (bf16[192,384]{1,0:T(8,128)(2,1)S(1)}, bf16[192,384]{1,0:T(8,128)(2,1)}, u32[]{:S(2)}) copy-start(bf16[192,384]{1,0:T(8,128)(2,1)} %refs_0_) | copy-start | bytes 442372
  1.7 12.4 %copy-start.14 = (f32[8,8,256]{2,1,0:T(8,128)S(1)}, f32[8,8,256]{2,1,0:T(8,128)}, u32[]{:S(2)}) copy-start(f32[8,8,256]{2,1,0:T(8,128)} %class_row.1) | copy-start | bytes 196612
  1.7 24.9 %copy-start.8 = (bf16[192,384]{1,0:T(8,128)(2,1)S(1)}, bf16[192,384]{1,0:T(8,128)(2,1)}, u32[]{:S(2)}) copy-start(bf16[192,384]{1,0:T(8,128)(2,1)} %wq_ref.1) | copy-start | bytes 442372
  5.2 38.1 %copy-start.11 = (bf16[192,2304]{1,0:T(8,128)(2,1)S(1)}, bf16[192,2304]{1,0:T(8,128)(2,1)}, u32[]{:S(2)}) copy-start(bf16[192,2304]{1,0:T(8,128)(2,1)} %get-tuple-element.38.refs_0_.refs_4_) | copy-start | bytes 2654212
  5.2 44.5 %copy-start.9 = (bf16[192,384]{1,0:T(8,128)(2,1)S(1)}, bf16[192,384]{1,0:T(8,128)(2,1)}, u32[]{:S(2)}) copy-start(bf16[192,384]{1,0:T(8,128)(2,1)} %wk_ref.1) | copy-start | bytes 442372
  5.2 26.9 %collective-permute-start.10 = (bf16[192,2304]{1,0:T(8,128)(2,1)}, bf16[192,2304]{1,0:T(8,128)(2,1)}, u32[]{:S(2)}, u32[]{:S(2)}) collective-permute-start(bf16[192,2304]{1,0:T(8,128)(2,1)} %get-tuple-element.38.refs_0_.refs_4_), channel_id=1, source_target_pairs={{0,2},{1,3},{2,0},{3,1},{4,6},{5,7},{6,4},{7,5},{8,10},{9,11},{10,... | collective-permute-start | bytes 2654216 | tf_op jit(solution)/shard_map/ppermute | solution.py:407
  8.2 18.4 %collective-permute-start = (bf16[192,384]{1,0:T(8,128)(2,1)S(1)}, bf16[192,384]{1,0:T(8,128)(2,1)S(1)}, u32[]{:S(2)}, u32[]{:S(2)}) collective-permute-start(bf16[192,384]{1,0:T(8,128)(2,1)S(1)} %copy-done.15), channel_id=1, source_target_pairs={{0,4},{4,0},{8,12},{12,8},{16,20},{20,16},{24,28},{28,24},{1,5},{5... | collective-permute-start | bytes 442376 | tf_op jit(solution)/shard_map/ppermute | solution.py:407
  9.7 17.7 %collective-permute-start.3 = (bf16[192,384]{1,0:T(8,128)(2,1)S(1)}, bf16[192,384]{1,0:T(8,128)(2,1)S(1)}, u32[]{:S(2)}, u32[]{:S(2)}) collective-permute-start(bf16[192,384]{1,0:T(8,128)(2,1)S(1)} %copy-done.15), channel_id=1, source_target_pairs={{0,24},{4,28},{8,16},{12,20},{16,8},{20,12},{24,0},{28,4},{1,25},{... | collective-permute-start | bytes 442376 | tf_op jit(solution)/shard_map/ppermute | solution.py:407
  13.3 14.1 %collective-permute-start.2 = (bf16[192,384]{1,0:T(8,128)(2,1)S(1)}, bf16[192,384]{1,0:T(8,128)(2,1)S(1)}, u32[]{:S(2)}, u32[]{:S(2)}) collective-permute-start(bf16[192,384]{1,0:T(8,128)(2,1)S(1)} %copy-done.15), channel_id=1, source_target_pairs={{0,16},{4,20},{8,24},{12,28},{16,0},{20,4},{24,8},{28,12},{1,17},{... | collective-permute-start | bytes 442376 | tf_op jit(solution)/shard_map/ppermute | solution.py:407
  13.3 14.1 %collective-permute-start.1 = (bf16[192,384]{1,0:T(8,128)(2,1)S(1)}, bf16[192,384]{1,0:T(8,128)(2,1)S(1)}, u32[]{:S(2)}, u32[]{:S(2)}) collective-permute-start(bf16[192,384]{1,0:T(8,128)(2,1)S(1)} %copy-done.15), channel_id=1, source_target_pairs={{0,8},{4,12},{8,0},{12,4},{16,24},{20,28},{24,16},{28,20},{1,9},{5... | collective-permute-start | bytes 442376 | tf_op jit(solution)/shard_map/ppermute | solution.py:407
  26.6 23.9 %copy-start.4 = (f32[8,8,256]{2,1,0:T(8,128)}, f32[8,8,256]{2,1,0:T(8,128)S(1)}, u32[]{:S(2)}) copy-start(f32[8,8,256]{2,1,0:T(8,128)S(1)} %all_to_all.20.pack_ref) | copy-start | bytes 196612
  26.6 23.9 %copy-start.7 = (bf16[192,384]{1,0:T(8,128)(2,1)}, bf16[192,384]{1,0:T(8,128)(2,1)S(1)}, u32[]{:S(2)}) copy-start(bf16[192,384]{1,0:T(8,128)(2,1)S(1)} %collective-permute-done.refs_0_.refs_2_) | copy-start | bytes 442372
  27.5 23.0 %copy-start.12 = (bf16[576,384]{1,0:T(8,128)(2,1)}, bf16[576,384]{1,0:T(8,128)(2,1)S(1)}, u32[]{:S(2)}) copy-start(bf16[576,384]{1,0:T(8,128)(2,1)S(1)} %pad_maximum_fusion.1.refs_1_) | copy-start | bytes 1327108
  27.5 15.7 %collective-permute-start.5 = (bf16[576,384]{1,0:T(8,128)(2,1)S(1)}, bf16[576,384]{1,0:T(8,128)(2,1)S(1)}, u32[]{:S(2)}, u32[]{:S(2)}) collective-permute-start(bf16[576,384]{1,0:T(8,128)(2,1)S(1)} %pad_maximum_fusion.1.refs_1_), channel_id=1, source_target_pairs={{0,4},{4,0},{8,12},{12,8},{16,20},{20,16},{24,28},{28,24},{1,5},{5... | collective-permute-start | bytes 1327112 | tf_op jit(solution)/shard_map/ppermute | solution.py:407
  28.9 14.3 %collective-permute-start.4 = (bf16[256,384]{1,0:T(8,128)(2,1)}, bf16[256,384]{1,0:T(8,128)(2,1)S(1)}, u32[]{:S(2)}, u32[]{:S(2)}) collective-permute-start(bf16[256,384]{1,0:T(8,128)(2,1)} %get-tuple-element.33.refs_0_), channel_id=1, source_target_pairs={{0,4},{4,0},{8,12},{12,8},{16,20},{20,16},{24,28},{28,24},{1,5},{5... | collective-permute-start | bytes 589832 | tf_op jit(solution)/shard_map/ppermute | solution.py:407
  29.6 24.4 %collective-permute-start.8 = (bf16[256,384]{1,0:T(8,128)(2,1)}, bf16[256,384]{1,0:T(8,128)(2,1)S(1)}, u32[]{:S(2)}, u32[]{:S(2)}) collective-permute-start(bf16[256,384]{1,0:T(8,128)(2,1)} %get-tuple-element.33.refs_0_), channel_id=1, source_target_pairs={{0,24},{4,28},{8,16},{12,20},{16,8},{20,12},{24,0},{28,4},{1,25},{... | collective-permute-start | bytes 589832 | tf_op jit(solution)/shard_map/ppermute | solution.py:407
  32.1 21.9 %collective-permute-start.7 = (bf16[256,384]{1,0:T(8,128)(2,1)}, bf16[256,384]{1,0:T(8,128)(2,1)}, u32[]{:S(2)}, u32[]{:S(2)}) collective-permute-start(bf16[256,384]{1,0:T(8,128)(2,1)} %get-tuple-element.33.refs_0_), channel_id=1, source_target_pairs={{0,16},{4,20},{8,24},{12,28},{16,0},{20,4},{24,8},{28,12},{1,17},{... | collective-permute-start | bytes 589832 | tf_op jit(solution)/shard_map/ppermute | solution.py:407
  32.1 21.9 %collective-permute-start.6 = (bf16[256,384]{1,0:T(8,128)(2,1)}, bf16[256,384]{1,0:T(8,128)(2,1)}, u32[]{:S(2)}, u32[]{:S(2)}) collective-permute-start(bf16[256,384]{1,0:T(8,128)(2,1)} %get-tuple-element.33.refs_0_), channel_id=1, source_target_pairs={{0,8},{4,12},{8,0},{12,4},{16,24},{20,28},{24,16},{28,20},{1,9},{5... | collective-permute-start | bytes 589832 | tf_op jit(solution)/shard_map/ppermute | solution.py:407
  34.0 15.7 %all-to-all-start.1 = ((f32[8,8,384]{2,1,0:T(8,128)}), f32[8,8,384]{2,1,0:T(8,128)S(1)}, u32[]{:S(2)}, u32[]{:S(2)}) async-start(f32[8,8,384]{2,1,0:T(8,128)} %query_share.1), calls=%async_computation.1 | async-start | bytes 196608 | tf_op jit(solution)/shard_map/all_to_all | solution.py:476
  43.2 17.7 %copy-start.5 = (bf16[256,384]{1,0:T(8,128)(2,1)}, bf16[256,384]{1,0:T(8,128)(2,1)S(1)}, u32[]{:S(2)}) copy-start(bf16[256,384]{1,0:T(8,128)(2,1)S(1)} %collective-permute-done.4.refs_0_.refs_2_) | copy-start | bytes 589828
  43.2 37.6 %collective-permute-start.11 = (bf16[192,2304]{1,0:T(8,128)(2,1)S(1)}, bf16[192,2304]{1,0:T(8,128)(2,1)}, u32[]{:S(2)}, u32[]{:S(2)}) collective-permute-start(bf16[192,2304]{1,0:T(8,128)(2,1)S(1)} %copy-done.11), channel_id=1, source_target_pairs={{0,1},{1,0},{2,3},{3,2},{4,5},{5,4},{6,7},{7,6},{8,9},{9,8},{10,11... | collective-permute-start | bytes 2654216 | tf_op jit(solution)/shard_map/ppermute | solution.py:407
  43.2 17.7 %copy-start.3 = (bf16[576,384]{1,0:T(8,128)(2,1)}, bf16[576,384]{1,0:T(8,128)(2,1)S(1)}, u32[]{:S(2)}) copy-start(bf16[576,384]{1,0:T(8,128)(2,1)S(1)} %collective-permute-done.5.refs_1_.refs_3_) | copy-start | bytes 1327108
  43.3 37.5 %collective-permute-start.12 = (bf16[192,2304]{1,0:T(8,128)(2,1)}, bf16[192,2304]{1,0:T(8,128)(2,1)}, u32[]{:S(2)}, u32[]{:S(2)}) collective-permute-start(bf16[192,2304]{1,0:T(8,128)(2,1)} %collective-permute-done.10.refs_2_.refs_6_), channel_id=1, source_target_pairs={{0,1},{1,0},{2,3},{3,2},{4,5},{5,4},{6,7},{7,6},{8,9},{9,8},{10,11... | collective-permute-start | bytes 2654216 | tf_op jit(solution)/shard_map/ppermute | solution.py:407
  50.5 10.4 %all-to-all-start.2 = ((f32[8,8,256]{2,1,0:T(8,128)}), f32[8,8,256]{2,1,0:T(8,128)S(1)}, u32[]{:S(2)}, u32[]{:S(2)}) async-start(f32[8,8,256]{2,1,0:T(8,128)} %fold_key.1), calls=%async_computation.2 | async-start | bytes 131072 | tf_op jit(solution)/shard_map/all_to_all | solution.py:509
  54.0 7.4 %copy-start = (bf16[1,257,1536]{2,1,0:T(8,128)(2,1)S(1)}, bf16[1,257,1536]{2,1,0:T(8,128)(2,1)}, u32[]{:S(2)}) copy-start(bf16[1,257,1536]{2,1,0:T(8,128)(2,1)} %patch_ref.5) | copy-start | bytes 2368516
  54.0 7.4 %copy-start.10 = (f32[1536]{0:T(1024)S(1)}, f32[1536]{0:T(1024)}, u32[]{:S(2)}) copy-start(f32[1536]{0:T(1024)} %gain_ref.6) | copy-start | bytes 18436
  61.0 0.9 copy-start.6
  61.0 6.4 %copy-start.1 = (bf16[768,384]{1,0:T(8,128)(2,1)}, bf16[768,384]{1,0:T(8,128)(2,1)S(1)}, u32[]{:S(2)}) copy-start(bf16[768,384]{1,0:T(8,128)(2,1)S(1)} %third_over.1.refs_1_) | copy-start | bytes 1769476
  61.0 12.3 %collective-permute-start.9 = (bf16[768,384]{1,0:T(8,128)(2,1)S(1)}, bf16[768,384]{1,0:T(8,128)(2,1)}, u32[]{:S(2)}, u32[]{:S(2)}) collective-permute-start(bf16[768,384]{1,0:T(8,128)(2,1)S(1)} %third_over.1.refs_1_), channel_id=1, source_target_pairs={{0,4},{4,0},{8,12},{12,8},{16,20},{20,16},{24,28},{28,24},{1,5},{5... | collective-permute-start | bytes 1769480 | tf_op jit(solution)/shard_map/ppermute | solution.py:407
  61.9 0.9 copy-start.2
  67.3 13.4 %all-to-all-start.3 = ((bf16[32,16,128]{2,1,0:T(8,128)(2,1)}), bf16[32,16,128]{2,1,0:T(8,128)(2,1)S(1)}, u32[]{:S(2)}, u32[]{:S(2)}) async-start(bf16[32,16,128]{2,1,0:T(8,128)(2,1)} %tile_attention.1), calls=%async_computation.3 | async-start | bytes 262144 | tf_op jit(solution)/shard_map/all_to_all | solution.py:534
  80.8 0.7 copy-start.13
  89.3 1.9 %collective-permute-start.13 = (bf16[64,256]{1,0:T(8,128)(2,1)}, bf16[64,256]{1,0:T(8,128)(2,1)S(1)}, u32[]{:S(2)}, u32[]{:S(2)}) collective-permute-start(bf16[64,256]{1,0:T(8,128)(2,1)} %get-tuple-element.44), channel_id=1, source_target_pairs={{0,1},{1,0},{2,3},{3,2},{4,5},{5,4},{6,7},{7,6},{8,9},{9,8},{10,11... | collective-permute-start | bytes 98312 | tf_op jit(solution)/shard_map/ppermute | solution.py:407
  89.4 4.4 %collective-permute-start.14 = (bf16[64,256]{1,0:T(8,128)(2,1)}, bf16[64,256]{1,0:T(8,128)(2,1)S(1)}, u32[]{:S(2)}, u32[]{:S(2)}) collective-permute-start(bf16[64,256]{1,0:T(8,128)(2,1)} %get-tuple-element.45), channel_id=1, source_target_pairs={{0,2},{1,3},{2,0},{3,1},{4,6},{5,7},{6,4},{7,5},{8,10},{9,11},{10,... | collective-permute-start | bytes 98312 | tf_op jit(solution)/shard_map/ppermute | solution.py:407
  89.9 3.9 %collective-permute-start.15 = (bf16[64,256]{1,0:T(8,128)(2,1)}, bf16[64,256]{1,0:T(8,128)(2,1)S(1)}, u32[]{:S(2)}, u32[]{:S(2)}) collective-permute-start(bf16[64,256]{1,0:T(8,128)(2,1)} %get-tuple-element.46), channel_id=1, source_target_pairs={{0,3},{1,2},{2,1},{3,0},{4,7},{5,6},{6,5},{7,4},{8,11},{9,10},{10,... | collective-permute-start | bytes 98312 | tf_op jit(solution)/shard_map/ppermute | solution.py:407
  91.3 2.6 %copy-start.16 = (bf16[64,256]{1,0:T(8,128)(2,1)}, bf16[64,256]{1,0:T(8,128)(2,1)S(1)}, u32[]{:S(2)}) copy-start(bf16[64,256]{1,0:T(8,128)(2,1)S(1)} %collective-permute-done.13.refs_1_) | copy-start | bytes 98308
  93.8 0.6 copy-start.17
  93.8 0.6 copy-start.18

commit v7 on v6

--- a/solution.py
+++ b/solution.py
@@ -243,6 +243,19 @@
     acc_ref[...] = jnp.where(value_lanes(head), num, acc_ref[...])
 
 
+def set_stacked(new, ml_ref, acc_ref):
+    rows = acc_ref.shape[0]
+    lane = lax.broadcasted_iota(I32, ml_ref.shape, 1)
+    ml = jnp.zeros(ml_ref.shape, F32)
+    acc = jnp.zeros(acc_ref.shape, F32)
+    for head in range(3):
+        top, den, num = (x[head * rows : (head + 1) * rows] for x in new)
+        ml = jnp.where(lane == head, top, jnp.where(lane == head + 8, den, ml))
+        acc = jnp.where(value_lanes(head), num, acc)
+    ml_ref[...] = ml
+    acc_ref[...] = acc
+
+
 def add_stacked(new, ml_ref, acc_ref):
     rows = acc_ref.shape[0]
     for head in range(3):
@@ -303,10 +316,6 @@
     step = pl.program_id(0)
     rows = q_ref.shape[0]
 
-    @pl.when(step == 0)
-    def _():
-        clear_state(ml_ref, acc_ref)
-
     masks = None
     if len(groups) > 1:
         masks = sum(groups, ())
@@ -317,10 +326,21 @@
     _, pos_col, _, flag_col = fresh_places(padded, pack_ref, pos_ref)
     place = lax.broadcasted_iota(I32, (rows, 1), 0) + lax.axis_index("tile") * span
     q_rows = stack_heads(as_bf16(branch_rows(place, 1, offset_ref, span, total)), 8)
+    block = kv_ref.shape[0]
+    if block < total:
+
+        @pl.when(step == 0)
+        def _():
+            clear_state(ml_ref, acc_ref)
+
     keys = key_places(masks, kv_ref.shape[0], span, step)
     k_rows = key_rows(keys, pos_col, flag_col, offset_ref, span, total)
     krows_ref[...] = k_rows
-    add_stacked(attend(stack_heads(q_ref[...], HEAD), q_rows, kv_ref, k_rows), ml_ref, acc_ref)
+    new = attend(stack_heads(q_ref[...], HEAD), q_rows, kv_ref, k_rows)
+    if block == total:
+        set_stacked(new, ml_ref, acc_ref)
+    else:
+        add_stacked(new, ml_ref, acc_ref)
 
 
 def fresh_kernel(
@@ -362,7 +382,11 @@
         clear_state(mlf_s, accf_s)
 
     qf = stack_heads(qf_s[...], HEAD)
-    add_stacked(attend(qf, f_rows, kv_ref, krows_ref[...]), mlf_s, accf_s)
+    new = attend(qf, f_rows, kv_ref, krows_ref[...])
+    if kv_ref.shape[0] == total:
+        set_stacked(new, mlf_s, accf_s)
+    else:
+        add_stacked(new, mlf_s, accf_s)
 
     @pl.when(step == pl.num_programs(0) - 1)
     def _():

time: 97.4 us -> 97.3 us (level)
  no operation moved by 1% of the time
where the time goes in v7:
time: 97.3 us; the launch traced here: 96.8 us
  Pallas kernels  29.6 us (30%)
  starting transfers between devices  28.9 us (30%)
  waiting for transfers between devices  22.2 us (23%)
  blocking collectives  12.5 us (13%)
  local copies, waits for them, and re-layouts  2.18 us (2%)
  other arithmetic  1.2 us (1%)
    ppermute x16, starting transfers between devices, trade(): return lax.ppermute(block, axis, [(i, i ^ mask) for i in range(count)])  18.2 us
    all_to_all x1, blocking collectives, shards(): pack = lax.all_to_all(pack, 'tile', 0, 0, tiled=True)  12.5 us
    ppermute x16, waiting for transfers between devices, trade(): return lax.ppermute(block, axis, [(i, i ^ mask) for i in range(count)])  10.5 us
    pallas_call x1, Pallas kernels, shards(): call(functools.partial(base_attention_kernel, span, total, padded, groups...  7.67 us
    pallas_call x1, Pallas kernels, shards(): call(functools.partial(fresh_kernel, span, total), out_shape=(sds((count,...  7.64 us
    all_to_all x1, waiting for transfers between devices, shards(): part = lax.all_to_all(part, 'tile', 0, 0, tiled=True)  5.94 us
    all_to_all x1, waiting for transfers between devices, shards(): folded = lax.all_to_all(folded, 'tile', 0, 0, tiled=True)  5.81 us
    all_to_all x1, starting transfers between devices, shards(): part = lax.all_to_all(part, 'tile', 0, 0, tiled=True)  4.56 us
  transfers between devices with their start and end apart: 19, of which 5 were waited for; matrix products, arithmetic and copies ran while one was open for 1% of the time, Pallas kernels for 15%

profile of v7, /device:TPU:0, one launch (start us, length us, event | category | flops | bytes accessed | tf_op | source)
XLA Modules:
  0.0 96.8 jit_solution(11204815670721273938)
XLA Ops:
  0.0 1.7 %class_row.1 = f32[8,8,256]{2,1,0:T(8,128)} custom-call(bf16[1,257,1536]{2,1,0:T(8,128)(2,1)} %patch_ref.5, f32[1536]{0:T(1024)} %gain_ref.6, s32[8]{0:T(128)} %pos_ref.5, s32[256]{0:T(256)} %kept_ref.3), custom_call_target="tpu_custom_call" | custom-call | tf_op jit(solution)/shard_map/class_row/pallas_call | solution.py:460
  1.7 3.4 %base_rows.1 = (bf16[256,768]{1,0:T(8,128)(2,1)}, bf16[256,256]{1,0:T(8,128)(2,1)}, bf16[256,384]{1,0:T(8,128)(2,1)}, bf16[192,2304]{1,0:T(8,128)(2,1)}) custom-call(bf16[256,768]{1,0:T(8,128)(2,1)} %cached_ref, s32[256]{0:T(256)} %kept_ref.3, f32[768]{0:T(1024)} %mask_ref.1, f32[768]{0:T(1024)} %gain_ref.7, bf16[192,768]{1,0:T(8,128)(2,1)} %bitcast.4, ...), custom_call_target="tpu_custom_call" | custom-call | tf_op jit(solution)/shard_map/base_rows/pallas_call | solution.py:471
  5.2 3.0 %collective-permute-start.10 = (bf16[192,2304]{1,0:T(8,128)(2,1)}, bf16[192,2304]{1,0:T(8,128)(2,1)}, u32[]{:S(2)}, u32[]{:S(2)}) collective-permute-start(bf16[192,2304]{1,0:T(8,128)(2,1)} %get-tuple-element.38.refs_0_.refs_4_), channel_id=1, source_target_pairs={{0,2},{1,3},{2,0},{3,1},{4,6},{5,7},{6,4},{7,5},{8,10},{9,11},{10,... | collective-permute-start | bytes 2654216 | tf_op jit(solution)/shard_map/ppermute | solution.py:431
  8.2 1.5 %collective-permute-start = (bf16[192,384]{1,0:T(8,128)(2,1)S(1)}, bf16[192,384]{1,0:T(8,128)(2,1)S(1)}, u32[]{:S(2)}, u32[]{:S(2)}) collective-permute-start(bf16[192,384]{1,0:T(8,128)(2,1)S(1)} %copy-done.15), channel_id=1, source_target_pairs={{0,4},{4,0},{8,12},{12,8},{16,20},{20,16},{24,28},{28,24},{1,5},{5... | collective-permute-start | bytes 442376 | tf_op jit(solution)/shard_map/ppermute | solution.py:431
  9.7 3.6 %collective-permute-start.3 = (bf16[192,384]{1,0:T(8,128)(2,1)S(1)}, bf16[192,384]{1,0:T(8,128)(2,1)S(1)}, u32[]{:S(2)}, u32[]{:S(2)}) collective-permute-start(bf16[192,384]{1,0:T(8,128)(2,1)S(1)} %copy-done.15), channel_id=1, source_target_pairs={{0,24},{4,28},{8,16},{12,20},{16,8},{20,12},{24,0},{28,4},{1,25},{... | collective-permute-start | bytes 442376 | tf_op jit(solution)/shard_map/ppermute | solution.py:431
  13.3 0.0 collective-permute-start.2
  13.3 0.8 collective-permute-start.1
  14.1 12.5 %all_to_all.20.pack_ref = f32[8,8,256]{2,1,0:T(8,128)S(1)} all-to-all(f32[8,8,256]{2,1,0:T(8,128)S(1)} %copy-done.14), channel_id=1, replica_groups=mesh['tile'=8,'seg'=4] {'tile'}, dimensions={0} | all-to-all | bytes 131072 | tf_op jit(solution)/shard_map/all_to_all | solution.py:470
  26.6 0.0 collective-permute-done.refs_0_.refs_2_
  26.6 0.8 query_share.1
  27.4 0.0 collective-permute-done.3
  27.4 0.0 collective-permute-done.2
  27.4 0.0 collective-permute-done.1
  27.5 1.4 %collective-permute-start.5 = (bf16[576,384]{1,0:T(8,128)(2,1)S(1)}, bf16[576,384]{1,0:T(8,128)(2,1)S(1)}, u32[]{:S(2)}, u32[]{:S(2)}) collective-permute-start(bf16[576,384]{1,0:T(8,128)(2,1)S(1)} %pad_maximum_fusion.1.refs_1_), channel_id=1, source_target_pairs={{0,4},{4,0},{8,12},{12,8},{16,20},{20,16},{24,28},{28,24},{1,5},{5... | collective-permute-start | bytes 1327112 | tf_op jit(solution)/shard_map/ppermute | solution.py:431
  28.9 0.7 collective-permute-start.4
  29.6 2.5 %collective-permute-start.8 = (bf16[256,384]{1,0:T(8,128)(2,1)}, bf16[256,384]{1,0:T(8,128)(2,1)S(1)}, u32[]{:S(2)}, u32[]{:S(2)}) collective-permute-start(bf16[256,384]{1,0:T(8,128)(2,1)} %get-tuple-element.33.refs_0_), channel_id=1, source_target_pairs={{0,24},{4,28},{8,16},{12,20},{16,8},{20,12},{24,0},{28,4},{1,25},{... | collective-permute-start | bytes 589832 | tf_op jit(solution)/shard_map/ppermute | solution.py:431
  32.1 1.9 %collective-permute-start.6 = (bf16[256,384]{1,0:T(8,128)(2,1)}, bf16[256,384]{1,0:T(8,128)(2,1)}, u32[]{:S(2)}, u32[]{:S(2)}) collective-permute-start(bf16[256,384]{1,0:T(8,128)(2,1)} %get-tuple-element.33.refs_0_), channel_id=1, source_target_pairs={{0,8},{4,12},{8,0},{12,4},{16,24},{20,28},{24,16},{28,20},{1,9},{5... | collective-permute-start | bytes 589832 | tf_op jit(solution)/shard_map/ppermute | solution.py:431
  34.0 4.6 %all-to-all-start.1 = ((f32[8,8,384]{2,1,0:T(8,128)}), f32[8,8,384]{2,1,0:T(8,128)S(1)}, u32[]{:S(2)}, u32[]{:S(2)}) async-start(f32[8,8,384]{2,1,0:T(8,128)} %query_share.1), calls=%async_computation.1 | async-start | bytes 196608 | tf_op jit(solution)/shard_map/all_to_all | solution.py:500
  38.6 4.7 %collective-permute-done.4.refs_0_.refs_2_ = bf16[256,384]{1,0:T(8,128)(2,1)S(1)} collective-permute-done((bf16[256,384]{1,0:T(8,128)(2,1)}, bf16[256,384]{1,0:T(8,128)(2,1)S(1)}, u32[]{:S(2)}, u32[]{:S(2)}) %collective-permute-start.4) | collective-permute-done | bytes 196640 | tf_op jit(solution)/shard_map/ppermute | solution.py:431
  43.2 0.0 collective-permute-start.11
  43.3 0.5 collective-permute-start.12
  43.7 5.9 %all-to-all-done.1.part_ref = f32[8,8,384]{2,1,0:T(8,128)S(1)} async-done(((f32[8,8,384]{2,1,0:T(8,128)}), f32[8,8,384]{2,1,0:T(8,128)S(1)}, u32[]{:S(2)}, u32[]{:S(2)}) %all-to-all-start.1) | async-done | bytes 98336 | tf_op jit(solution)/shard_map/all_to_all | solution.py:500
  49.7 0.8 fold_key.1
  50.5 3.4 %all-to-all-start.2 = ((f32[8,8,256]{2,1,0:T(8,128)}), f32[8,8,256]{2,1,0:T(8,128)S(1)}, u32[]{:S(2)}, u32[]{:S(2)}) async-start(f32[8,8,256]{2,1,0:T(8,128)} %fold_key.1), calls=%async_computation.2 | async-start | bytes 131072 | tf_op jit(solution)/shard_map/all_to_all | solution.py:533
  54.0 0.0 copy-start.10
  54.0 0.0 collective-permute-done.7
  54.0 1.1 %pad_maximum_fusion.refs_0_ = bf16[768,384]{1,0:T(8,128)(2,1)S(1)} fusion(bf16[256,384]{1,0:T(8,128)(2,1)S(1)} %collective-permute-done.8, bf16[256,384]{1,0:T(8,128)(2,1)} %collective-permute-done.7, bf16[256,384]{1,0:T(8,128)(2,1)} %collective-permute-done.6), kind=kLoop, calls=%fused_computation | loop fusion | flops 1769472 | bytes 1179648 | tf_op jit(solution)/shard_map/concatenate | solution.py:515
  55.2 5.8 %all-to-all-done.2.fold_ref.refs_1_ = f32[8,8,256]{2,1,0:T(8,128)S(1)} async-done(((f32[8,8,256]{2,1,0:T(8,128)}), f32[8,8,256]{2,1,0:T(8,128)S(1)}, u32[]{:S(2)}, u32[]{:S(2)}) %all-to-all-start.2) | async-done | bytes 65568 | tf_op jit(solution)/shard_map/all_to_all | solution.py:533
  61.0 0.4 collective-permute-start.9
  61.4 0.5 token_norm.1.normed_ref
  61.9 0.9 copy-done.2
  62.8 4.5 %tile_attention.1 = bf16[32,16,128]{2,1,0:T(8,128)(2,1)} custom-call(bf16[1,257,1536]{2,1,0:T(8,128)(2,1)} %patch_ref.5, bf16[257,1536]{1,0:T(8,128)(2,1)} %copy-done.2, f32[8,8,256]{2,1,0:T(8,128)} %copy-done.6, f32[1536]{0:T(1024)} %scale_ref.1, f32[192]{0:T(256)} %bias_ref.1, bf16[384,1536]{1,0:T(8,128)(2,1)} %wo_ref.1, bf16[192,384]{1,0:T(8,128)(2,1)} %refs_0_, ...), custom_call_target="tpu_custom_call" | custom-call | tf_op jit(solution)/shard_map/tile_attention/pallas_call | solution.py:545
  67.3 2.7 %all-to-all-start.3 = ((bf16[32,16,128]{2,1,0:T(8,128)(2,1)}), bf16[32,16,128]{2,1,0:T(8,128)(2,1)S(1)}, u32[]{:S(2)}, u32[]{:S(2)}) async-start(bf16[32,16,128]{2,1,0:T(8,128)(2,1)} %tile_attention.1), calls=%async_computation.3 | async-start | bytes 262144 | tf_op jit(solution)/shard_map/all_to_all | solution.py:558
  70.1 3.2 %collective-permute-done.9.refs_3_ = bf16[768,384]{1,0:T(8,128)(2,1)} collective-permute-done((bf16[768,384]{1,0:T(8,128)(2,1)S(1)}, bf16[768,384]{1,0:T(8,128)(2,1)}, u32[]{:S(2)}, u32[]{:S(2)}) %collective-permute-start.9) | collective-permute-done | bytes 589856 | tf_op jit(solution)/shard_map/ppermute | solution.py:431
  73.3 7.7 %base_attention.1 = (bf16[2048,384]{1,0:T(8,128)(2,1)}, bf16[24,2048]{1,0:T(8,128)(2,1)}, f32[256,128]{1,0:T(8,128)}, f32[256,256]{1,0:T(8,128)}) custom-call(s32[8]{0:T(128)} %pos_ref.5, s32[5,12]{1,0:T(8,128)} %offset_ref.3, f32[8,8,256]{2,1,0:T(8,128)} %copy-done.4, bf16[256,256]{1,0:T(8,128)(2,1)} %get-tuple-element.28.q_ref, ...), custom_call_target="tpu_custom_call" | custom-call | tf_op jit(solution)/shard_map/base_attention/pallas_call | solution.py:564
  81.0 0.0 collective-permute-done.11.refs_1_.refs_5_
  81.0 0.0 collective-permute-done.12.refs_3_.refs_7_
  81.0 0.6 copy-done.13
  81.7 7.6 %fresh_attention.1 = (bf16[64,256]{1,0:T(8,128)(2,1)}, bf16[64,256]{1,0:T(8,128)(2,1)}, bf16[64,256]{1,0:T(8,128)(2,1)}, bf16[64,256]{1,0:T(8,128)(2,1)}, f32[64,768]{1,0:T(8,128)}) custom-call(s32[8]{0:T(128)} %pos_ref.5, s32[5,12]{1,0:T(8,128)} %offset_ref.3, f32[8,8,256]{2,1,0:T(8,128)} %copy-done.4, bf16[256,256]{1,0:T(8,128)(2,1)} %get-tuple-element.28.q_ref, ...), custom_call_target="tpu_custom_call" | custom-call | tf_op jit(solution)/shard_map/fresh_attention/pallas_call | solution.py:578
  89.3 0.1 collective-permute-start.13
  89.4 0.5 collective-permute-start.14
  89.9 1.4 %collective-permute-start.15 = (bf16[64,256]{1,0:T(8,128)(2,1)}, bf16[64,256]{1,0:T(8,128)(2,1)S(1)}, u32[]{:S(2)}, u32[]{:S(2)}) collective-permute-start(bf16[64,256]{1,0:T(8,128)(2,1)} %get-tuple-element.46), channel_id=1, source_target_pairs={{0,3},{1,2},{2,1},{3,0},{4,7},{5,6},{6,5},{7,4},{8,11},{9,10},{10,... | collective-permute-start | bytes 98312 | tf_op jit(solution)/shard_map/ppermute | solution.py:431
  91.2 0.0 collective-permute-done.13.refs_1_
  91.2 2.5 %collective-permute-done.14.refs_2_ = bf16[64,256]{1,0:T(8,128)(2,1)S(1)} collective-permute-done((bf16[64,256]{1,0:T(8,128)(2,1)}, bf16[64,256]{1,0:T(8,128)(2,1)S(1)}, u32[]{:S(2)}, u32[]{:S(2)}) %collective-permute-start.14) | collective-permute-done | bytes 32800 | tf_op jit(solution)/shard_map/ppermute | solution.py:431
  93.8 0.0 collective-permute-done.15.refs_3_
  93.8 0.6 copy-done.17
  94.4 0.0 copy-done.18
  94.4 2.4 %slide_next.1 = bf16[64,768]{1,0:T(8,128)(2,1)} custom-call(f32[64,768]{1,0:T(8,128)} %get-tuple-element.42.mine_ref, bf16[64,256]{1,0:T(8,128)(2,1)} %get-tuple-element.43.refs_0_, bf16[64,256]{1,0:T(8,128)(2,1)} %copy-done.16, bf16[64,256]{1,0:T(8,128)(2,1)} %copy-done.17, bf16[64,256]{1,0:T(8,128)(2,1)} %copy-done.18, ...), custom_call_target="tpu_custom_call" | custom-call | tf_op jit(solution)/shard_map/slide_next/pallas_call | solution.py:601
  (41 shorter events, 0.1 us)
Async XLA Ops:
  1.7 6.4 %copy-start.15 = (bf16[192,384]{1,0:T(8,128)(2,1)S(1)}, bf16[192,384]{1,0:T(8,128)(2,1)}, u32[]{:S(2)}) copy-start(bf16[192,384]{1,0:T(8,128)(2,1)} %refs_0_) | copy-start | bytes 442372
  1.7 12.4 %copy-start.14 = (f32[8,8,256]{2,1,0:T(8,128)S(1)}, f32[8,8,256]{2,1,0:T(8,128)}, u32[]{:S(2)}) copy-start(f32[8,8,256]{2,1,0:T(8,128)} %class_row.1) | copy-start | bytes 196612
  1.7 24.9 %copy-start.8 = (bf16[192,384]{1,0:T(8,128)(2,1)S(1)}, bf16[192,384]{1,0:T(8,128)(2,1)}, u32[]{:S(2)}) copy-start(bf16[192,384]{1,0:T(8,128)(2,1)} %wq_ref.1) | copy-start | bytes 442372
  5.2 38.1 %copy-start.11 = (bf16[192,2304]{1,0:T(8,128)(2,1)S(1)}, bf16[192,2304]{1,0:T(8,128)(2,1)}, u32[]{:S(2)}) copy-start(bf16[192,2304]{1,0:T(8,128)(2,1)} %get-tuple-element.38.refs_0_.refs_4_) | copy-start | bytes 2654212
  5.2 44.5 %copy-start.9 = (bf16[192,384]{1,0:T(8,128)(2,1)S(1)}, bf16[192,384]{1,0:T(8,128)(2,1)}, u32[]{:S(2)}) copy-start(bf16[192,384]{1,0:T(8,128)(2,1)} %wk_ref.1) | copy-start | bytes 442372
  5.2 26.9 %collective-permute-start.10 = (bf16[192,2304]{1,0:T(8,128)(2,1)}, bf16[192,2304]{1,0:T(8,128)(2,1)}, u32[]{:S(2)}, u32[]{:S(2)}) collective-permute-start(bf16[192,2304]{1,0:T(8,128)(2,1)} %get-tuple-element.38.refs_0_.refs_4_), channel_id=1, source_target_pairs={{0,2},{1,3},{2,0},{3,1},{4,6},{5,7},{6,4},{7,5},{8,10},{9,11},{10,... | collective-permute-start | bytes 2654216 | tf_op jit(solution)/shard_map/ppermute | solution.py:431
  8.2 18.4 %collective-permute-start = (bf16[192,384]{1,0:T(8,128)(2,1)S(1)}, bf16[192,384]{1,0:T(8,128)(2,1)S(1)}, u32[]{:S(2)}, u32[]{:S(2)}) collective-permute-start(bf16[192,384]{1,0:T(8,128)(2,1)S(1)} %copy-done.15), channel_id=1, source_target_pairs={{0,4},{4,0},{8,12},{12,8},{16,20},{20,16},{24,28},{28,24},{1,5},{5... | collective-permute-start | bytes 442376 | tf_op jit(solution)/shard_map/ppermute | solution.py:431
  9.7 17.7 %collective-permute-start.3 = (bf16[192,384]{1,0:T(8,128)(2,1)S(1)}, bf16[192,384]{1,0:T(8,128)(2,1)S(1)}, u32[]{:S(2)}, u32[]{:S(2)}) collective-permute-start(bf16[192,384]{1,0:T(8,128)(2,1)S(1)} %copy-done.15), channel_id=1, source_target_pairs={{0,24},{4,28},{8,16},{12,20},{16,8},{20,12},{24,0},{28,4},{1,25},{... | collective-permute-start | bytes 442376 | tf_op jit(solution)/shard_map/ppermute | solution.py:431
  13.3 14.1 %collective-permute-start.2 = (bf16[192,384]{1,0:T(8,128)(2,1)S(1)}, bf16[192,384]{1,0:T(8,128)(2,1)S(1)}, u32[]{:S(2)}, u32[]{:S(2)}) collective-permute-start(bf16[192,384]{1,0:T(8,128)(2,1)S(1)} %copy-done.15), channel_id=1, source_target_pairs={{0,16},{4,20},{8,24},{12,28},{16,0},{20,4},{24,8},{28,12},{1,17},{... | collective-permute-start | bytes 442376 | tf_op jit(solution)/shard_map/ppermute | solution.py:431
  13.3 14.1 %collective-permute-start.1 = (bf16[192,384]{1,0:T(8,128)(2,1)S(1)}, bf16[192,384]{1,0:T(8,128)(2,1)S(1)}, u32[]{:S(2)}, u32[]{:S(2)}) collective-permute-start(bf16[192,384]{1,0:T(8,128)(2,1)S(1)} %copy-done.15), channel_id=1, source_target_pairs={{0,8},{4,12},{8,0},{12,4},{16,24},{20,28},{24,16},{28,20},{1,9},{5... | collective-permute-start | bytes 442376 | tf_op jit(solution)/shard_map/ppermute | solution.py:431
  26.6 23.9 %copy-start.4 = (f32[8,8,256]{2,1,0:T(8,128)}, f32[8,8,256]{2,1,0:T(8,128)S(1)}, u32[]{:S(2)}) copy-start(f32[8,8,256]{2,1,0:T(8,128)S(1)} %all_to_all.20.pack_ref) | copy-start | bytes 196612
  26.6 23.9 %copy-start.7 = (bf16[192,384]{1,0:T(8,128)(2,1)}, bf16[192,384]{1,0:T(8,128)(2,1)S(1)}, u32[]{:S(2)}) copy-start(bf16[192,384]{1,0:T(8,128)(2,1)S(1)} %collective-permute-done.refs_0_.refs_2_) | copy-start | bytes 442372
  27.5 23.0 %copy-start.12 = (bf16[576,384]{1,0:T(8,128)(2,1)}, bf16[576,384]{1,0:T(8,128)(2,1)S(1)}, u32[]{:S(2)}) copy-start(bf16[576,384]{1,0:T(8,128)(2,1)S(1)} %pad_maximum_fusion.1.refs_1_) | copy-start | bytes 1327108
  27.5 15.7 %collective-permute-start.5 = (bf16[576,384]{1,0:T(8,128)(2,1)S(1)}, bf16[576,384]{1,0:T(8,128)(2,1)S(1)}, u32[]{:S(2)}, u32[]{:S(2)}) collective-permute-start(bf16[576,384]{1,0:T(8,128)(2,1)S(1)} %pad_maximum_fusion.1.refs_1_), channel_id=1, source_target_pairs={{0,4},{4,0},{8,12},{12,8},{16,20},{20,16},{24,28},{28,24},{1,5},{5... | collective-permute-start | bytes 1327112 | tf_op jit(solution)/shard_map/ppermute | solution.py:431
  28.9 14.3 %collective-permute-start.4 = (bf16[256,384]{1,0:T(8,128)(2,1)}, bf16[256,384]{1,0:T(8,128)(2,1)S(1)}, u32[]{:S(2)}, u32[]{:S(2)}) collective-permute-start(bf16[256,384]{1,0:T(8,128)(2,1)} %get-tuple-element.33.refs_0_), channel_id=1, source_target_pairs={{0,4},{4,0},{8,12},{12,8},{16,20},{20,16},{24,28},{28,24},{1,5},{5... | collective-permute-start | bytes 589832 | tf_op jit(solution)/shard_map/ppermute | solution.py:431
  29.6 24.4 %collective-permute-start.8 = (bf16[256,384]{1,0:T(8,128)(2,1)}, bf16[256,384]{1,0:T(8,128)(2,1)S(1)}, u32[]{:S(2)}, u32[]{:S(2)}) collective-permute-start(bf16[256,384]{1,0:T(8,128)(2,1)} %get-tuple-element.33.refs_0_), channel_id=1, source_target_pairs={{0,24},{4,28},{8,16},{12,20},{16,8},{20,12},{24,0},{28,4},{1,25},{... | collective-permute-start | bytes 589832 | tf_op jit(solution)/shard_map/ppermute | solution.py:431
  32.1 21.9 %collective-permute-start.7 = (bf16[256,384]{1,0:T(8,128)(2,1)}, bf16[256,384]{1,0:T(8,128)(2,1)}, u32[]{:S(2)}, u32[]{:S(2)}) collective-permute-start(bf16[256,384]{1,0:T(8,128)(2,1)} %get-tuple-element.33.refs_0_), channel_id=1, source_target_pairs={{0,16},{4,20},{8,24},{12,28},{16,0},{20,4},{24,8},{28,12},{1,17},{... | collective-permute-start | bytes 589832 | tf_op jit(solution)/shard_map/ppermute | solution.py:431
  32.1 21.9 %collective-permute-start.6 = (bf16[256,384]{1,0:T(8,128)(2,1)}, bf16[256,384]{1,0:T(8,128)(2,1)}, u32[]{:S(2)}, u32[]{:S(2)}) collective-permute-start(bf16[256,384]{1,0:T(8,128)(2,1)} %get-tuple-element.33.refs_0_), channel_id=1, source_target_pairs={{0,8},{4,12},{8,0},{12,4},{16,24},{20,28},{24,16},{28,20},{1,9},{5... | collective-permute-start | bytes 589832 | tf_op jit(solution)/shard_map/ppermute | solution.py:431
  34.0 15.7 %all-to-all-start.1 = ((f32[8,8,384]{2,1,0:T(8,128)}), f32[8,8,384]{2,1,0:T(8,128)S(1)}, u32[]{:S(2)}, u32[]{:S(2)}) async-start(f32[8,8,384]{2,1,0:T(8,128)} %query_share.1), calls=%async_computation.1 | async-start | bytes 196608 | tf_op jit(solution)/shard_map/all_to_all | solution.py:500
  43.2 17.7 %copy-start.5 = (bf16[256,384]{1,0:T(8,128)(2,1)}, bf16[256,384]{1,0:T(8,128)(2,1)S(1)}, u32[]{:S(2)}) copy-start(bf16[256,384]{1,0:T(8,128)(2,1)S(1)} %collective-permute-done.4.refs_0_.refs_2_) | copy-start | bytes 589828
  43.2 37.8 %collective-permute-start.11 = (bf16[192,2304]{1,0:T(8,128)(2,1)S(1)}, bf16[192,2304]{1,0:T(8,128)(2,1)}, u32[]{:S(2)}, u32[]{:S(2)}) collective-permute-start(bf16[192,2304]{1,0:T(8,128)(2,1)S(1)} %copy-done.11), channel_id=1, source_target_pairs={{0,1},{1,0},{2,3},{3,2},{4,5},{5,4},{6,7},{7,6},{8,9},{9,8},{10,11... | collective-permute-start | bytes 2654216 | tf_op jit(solution)/shard_map/ppermute | solution.py:431
  43.2 17.7 %copy-start.3 = (bf16[576,384]{1,0:T(8,128)(2,1)}, bf16[576,384]{1,0:T(8,128)(2,1)S(1)}, u32[]{:S(2)}) copy-start(bf16[576,384]{1,0:T(8,128)(2,1)S(1)} %collective-permute-done.5.refs_1_.refs_3_) | copy-start | bytes 1327108
  43.3 37.8 %collective-permute-start.12 = (bf16[192,2304]{1,0:T(8,128)(2,1)}, bf16[192,2304]{1,0:T(8,128)(2,1)}, u32[]{:S(2)}, u32[]{:S(2)}) collective-permute-start(bf16[192,2304]{1,0:T(8,128)(2,1)} %collective-permute-done.10.refs_2_.refs_6_), channel_id=1, source_target_pairs={{0,1},{1,0},{2,3},{3,2},{4,5},{5,4},{6,7},{7,6},{8,9},{9,8},{10,11... | collective-permute-start | bytes 2654216 | tf_op jit(solution)/shard_map/ppermute | solution.py:431
  50.5 10.4 %all-to-all-start.2 = ((f32[8,8,256]{2,1,0:T(8,128)}), f32[8,8,256]{2,1,0:T(8,128)S(1)}, u32[]{:S(2)}, u32[]{:S(2)}) async-start(f32[8,8,256]{2,1,0:T(8,128)} %fold_key.1), calls=%async_computation.2 | async-start | bytes 131072 | tf_op jit(solution)/shard_map/all_to_all | solution.py:533
  54.0 7.4 %copy-start = (bf16[1,257,1536]{2,1,0:T(8,128)(2,1)S(1)}, bf16[1,257,1536]{2,1,0:T(8,128)(2,1)}, u32[]{:S(2)}) copy-start(bf16[1,257,1536]{2,1,0:T(8,128)(2,1)} %patch_ref.5) | copy-start | bytes 2368516
  54.0 7.4 %copy-start.10 = (f32[1536]{0:T(1024)S(1)}, f32[1536]{0:T(1024)}, u32[]{:S(2)}) copy-start(f32[1536]{0:T(1024)} %gain_ref.6) | copy-start | bytes 18436
  61.0 0.9 copy-start.6
  61.0 6.4 %copy-start.1 = (bf16[768,384]{1,0:T(8,128)(2,1)}, bf16[768,384]{1,0:T(8,128)(2,1)S(1)}, u32[]{:S(2)}) copy-start(bf16[768,384]{1,0:T(8,128)(2,1)S(1)} %third_over.1.refs_1_) | copy-start | bytes 1769476
  61.0 12.3 %collective-permute-start.9 = (bf16[768,384]{1,0:T(8,128)(2,1)S(1)}, bf16[768,384]{1,0:T(8,128)(2,1)}, u32[]{:S(2)}, u32[]{:S(2)}) collective-permute-start(bf16[768,384]{1,0:T(8,128)(2,1)S(1)} %third_over.1.refs_1_), channel_id=1, source_target_pairs={{0,4},{4,0},{8,12},{12,8},{16,20},{20,16},{24,28},{28,24},{1,5},{5... | collective-permute-start | bytes 1769480 | tf_op jit(solution)/shard_map/ppermute | solution.py:431
  61.9 0.9 copy-start.2
  67.3 13.6 %all-to-all-start.3 = ((bf16[32,16,128]{2,1,0:T(8,128)(2,1)}), bf16[32,16,128]{2,1,0:T(8,128)(2,1)S(1)}, u32[]{:S(2)}, u32[]{:S(2)}) async-start(bf16[32,16,128]{2,1,0:T(8,128)(2,1)} %tile_attention.1), calls=%async_computation.3 | async-start | bytes 262144 | tf_op jit(solution)/shard_map/all_to_all | solution.py:558
  81.0 0.7 copy-start.13
  89.3 1.9 %collective-permute-start.13 = (bf16[64,256]{1,0:T(8,128)(2,1)}, bf16[64,256]{1,0:T(8,128)(2,1)S(1)}, u32[]{:S(2)}, u32[]{:S(2)}) collective-permute-start(bf16[64,256]{1,0:T(8,128)(2,1)} %get-tuple-element.44), channel_id=1, source_target_pairs={{0,1},{1,0},{2,3},{3,2},{4,5},{5,4},{6,7},{7,6},{8,9},{9,8},{10,11... | collective-permute-start | bytes 98312 | tf_op jit(solution)/shard_map/ppermute | solution.py:431
  89.4 4.4 %collective-permute-start.14 = (bf16[64,256]{1,0:T(8,128)(2,1)}, bf16[64,256]{1,0:T(8,128)(2,1)S(1)}, u32[]{:S(2)}, u32[]{:S(2)}) collective-permute-start(bf16[64,256]{1,0:T(8,128)(2,1)} %get-tuple-element.45), channel_id=1, source_target_pairs={{0,2},{1,3},{2,0},{3,1},{4,6},{5,7},{6,4},{7,5},{8,10},{9,11},{10,... | collective-permute-start | bytes 98312 | tf_op jit(solution)/shard_map/ppermute | solution.py:431
  89.9 3.9 %collective-permute-start.15 = (bf16[64,256]{1,0:T(8,128)(2,1)}, bf16[64,256]{1,0:T(8,128)(2,1)S(1)}, u32[]{:S(2)}, u32[]{:S(2)}) collective-permute-start(bf16[64,256]{1,0:T(8,128)(2,1)} %get-tuple-element.46), channel_id=1, source_target_pairs={{0,3},{1,2},{2,1},{3,0},{4,7},{5,6},{6,5},{7,4},{8,11},{9,10},{10,... | collective-permute-start | bytes 98312 | tf_op jit(solution)/shard_map/ppermute | solution.py:431
  91.2 2.6 %copy-start.16 = (bf16[64,256]{1,0:T(8,128)(2,1)}, bf16[64,256]{1,0:T(8,128)(2,1)S(1)}, u32[]{:S(2)}) copy-start(bf16[64,256]{1,0:T(8,128)(2,1)S(1)} %collective-permute-done.13.refs_1_) | copy-start | bytes 98308
  93.8 0.6 copy-start.17
  93.8 0.6 copy-start.18
